TPU v7x, 32 devices: a whole 2x2x4 slice. The times are simulated.
32 devices in a mesh: fft: 16 (over z, x, core), grp: 2 (over y).
Axes of the slice: x: 2, y: 2, z: 4, core: 2. Of those that a mesh axis runs over, the one named last changes fastest.
Arguments:
- psi_valence: bfloat16 [16, 64, 4096], P(None, 'fft'), may hold values from -6 to 6
- psi_conduction: bfloat16 [384, 64, 4096], P(None, 'fft'), may hold values from -6 to 6
- energy_valence: float32 [16], replicated, may hold values from -6 to -0.5
- energy_conduction: float32 [384], replicated, may hold values from 0.5 to 8
- pair_valence: int32 [80], P('grp'), may hold values from 0 to 15
- pair_conduction: int32 [80], P('grp'), may hold values from 0 to 383
- g_index: int32 [6144], replicated, may hold values from 0 to 262143, as said below
Outputs:
- chi_real: float32 [6144, 6144], P('fft', 'grp')
- chi_imag: float32 [6144, 6144], P('fft', 'grp')
Inputs may be any that keep to these rules, and one draw needn't show every extreme that they name: `g_index`: the 6144 entries are distinct grid points in flat order a * 64 * 64 + b * 64 + c.
All inputs are finite; a program needn't handle non-finite values.
Results may differ from a plain program's by a relative error of at most 0.0041.
Values may be sent and summed in bfloat16 or wider, within the bound.
No kernel may reach another device: no remote copies, remote signals or barrier semaphores. Data moves between devices by JAX's collectives and lax.ppermute only.
A program may use at most 128 MiB of HBM per device.

v0:
```python
import math

import jax
import jax.numpy as jnp
from jax import lax
from jax.sharding import PartitionSpec as P

HIGHEST = lax.Precision.HIGHEST


def phase_table(length):
    steps_idx = jnp.arange(length, dtype=jnp.int32)
    turn_count = (steps_idx[:, None] * steps_idx[None, :] % length).astype(jnp.float32)
    angles = turn_count * (2.0 * math.pi / length)
    return (jnp.cos(angles), jnp.sin(angles))


def rotate(real_part, imag_part, cos_table, sin_table, pattern):
    real_cos = jnp.einsum(
        pattern, real_part, cos_table, precision=HIGHEST, preferred_element_type=jnp.float32
    )
    real_sin = jnp.einsum(
        pattern, real_part, sin_table, precision=HIGHEST, preferred_element_type=jnp.float32
    )
    imag_cos = jnp.einsum(
        pattern, imag_part, cos_table, precision=HIGHEST, preferred_element_type=jnp.float32
    )
    imag_sin = jnp.einsum(
        pattern, imag_part, sin_table, precision=HIGHEST, preferred_element_type=jnp.float32
    )
    return (real_cos + imag_sin, imag_cos - real_sin)


def per_device(
    psi_valence,
    psi_conduction,
    energy_valence,
    energy_conduction,
    pair_valence,
    pair_conduction,
    g_index,
):
    planes = psi_valence.shape[1]
    plane_size = psi_valence.shape[2]
    length = math.isqrt(plane_size)
    pair_count = pair_valence.shape[0]
    cos_table, sin_table = phase_table(length)
    density = psi_valence[pair_valence].astype(jnp.float32) * psi_conduction[
        pair_conduction
    ].astype(jnp.float32)
    density = density.reshape(pair_count, planes, length, length)
    z_real = jnp.einsum(
        "pxyz,kz->pxyk", density, cos_table, precision=HIGHEST, preferred_element_type=jnp.float32
    )
    z_imag = -jnp.einsum(
        "pxyz,kz->pxyk", density, sin_table, precision=HIGHEST, preferred_element_type=jnp.float32
    )
    y_real, y_imag = rotate(z_real, z_imag, cos_table, sin_table, "pxyz,ky->pxkz")
    x_index = g_index // plane_size
    in_plane = g_index % plane_size
    pen_real, pen_imag = (
        lax.all_to_all(y_real, "fft", split_axis=2, concat_axis=1, tiled=True),
        lax.all_to_all(y_imag, "fft", split_axis=2, concat_axis=1, tiled=True),
    )
    k_real, k_imag = rotate(pen_real, pen_imag, cos_table, sin_table, "pxyz,kx->pkyz")
    width_y = pen_real.shape[2]
    y_start = lax.axis_index("fft") * width_y
    y_value = in_plane // length
    inside = (y_value >= y_start) & (y_value < y_start + width_y)
    local_index = x_index * (width_y * length) + (y_value - y_start) * length + in_plane % length
    local_index = jnp.where(inside, local_index, 0)
    keep_mask = inside.astype(jnp.float32)
    part_real = k_real.reshape(pair_count, -1)[:, local_index] * keep_mask
    part_imag = k_imag.reshape(pair_count, -1)[:, local_index] * keep_mask
    weight = 2.0 / (energy_conduction[pair_conduction] - energy_valence[pair_valence])
    factor = jnp.sqrt(weight) * (pair_count * lax.axis_size("grp")) ** (-0.25) * length ** (-1.5)
    sum_real, sum_imag = lax.psum((part_real, part_imag), "fft")
    scaled_real = (sum_real * factor[:, None]).astype(jnp.bfloat16)
    scaled_imag = (sum_imag * factor[:, None]).astype(jnp.bfloat16)
    sphere_total = g_index.shape[0]
    row_width = sphere_total // lax.axis_size("fft")
    row_start = lax.axis_index("fft") * row_width
    col_width = sphere_total // lax.axis_size("grp")
    col_real, col_imag = (
        lax.all_to_all(scaled_real, "grp", split_axis=1, concat_axis=0, tiled=True),
        lax.all_to_all(scaled_imag, "grp", split_axis=1, concat_axis=0, tiled=True),
    )
    own_real = lax.dynamic_slice_in_dim(scaled_real, row_start, row_width, 1)
    own_imag = lax.dynamic_slice_in_dim(scaled_imag, row_start, row_width, 1)
    zero_block = jnp.zeros((row_width, col_width), jnp.float32)
    pieces = (
        lax.all_gather(own_real, "grp", axis=0, tiled=True),
        lax.all_gather(own_imag, "grp", axis=0, tiled=True),
    )
    left_sum = jnp.concatenate([pieces[0], pieces[1]], 0)
    left_cross = jnp.concatenate([pieces[0], -pieces[1]], 0)
    right_sum = jnp.concatenate([col_real, col_imag], 0)
    right_cross = jnp.concatenate([col_imag, col_real], 0)
    real_add = jnp.einsum("pg,ph->gh", left_sum, right_sum, preferred_element_type=jnp.float32)
    imag_add = jnp.einsum("pg,ph->gh", left_cross, right_cross, preferred_element_type=jnp.float32)
    chi_real = (zero_block, zero_block)[0] - real_add
    return (chi_real, imag_add)


def solution(mesh):
    placed = (P(None, "fft", None), P(None, "fft", None), P(), P(), P("grp"), P("grp"), P())
    return jax.shard_map(
        per_device,
        mesh=mesh,
        in_specs=placed,
        out_specs=(P("fft", "grp"), P("fft", "grp")),
        check_vma=False,
    )
```

profile of v0, /device:TPU:0, one launch (start us, length us, event | category | flops | bytes accessed | tf_op | source)
XLA Modules:
  0.0 493.7 jit_solution(11956558118216582575)
XLA Ops:
  8.2 2.9 gather_fusion
  11.2 7.5 %gather_fusion.1 = bf16[40,4,4096]{2,1,0:T(4,128)(2,1)} fusion(bf16[384,4,4096]{2,1,0:T(4,128)(2,1)} %param.8, s32[1024]{0:T(1024)S(1)} %pad_clamp_fusion), kind=kCustom, calls=%fused_computation.1 | custom fusion | bytes 2621600 | tf_op jit(solution)/shard_map/gather | solution.py:48
  18.7 2.0 convert_multiply_fusion
  20.7 4.1 mul.160
  24.8 8.9 %fusion.25 = f32[40,4,64,64]{3,2,1,0:T(8,128)S(1)} fusion(f32[40,4,64,64]{3,2,1,0:T(8,128)} %mul.160), kind=kOutput, calls=%fused_computation.53 | convolution fusion | flops 503373824 | bytes 5242880 | tf_op jit(solution)/shard_map/pxyz,kz->pxyk/dot_general | solution.py:55
  33.6 4.6 fusion.34
  38.2 2.4 copy-done.4
  40.6 4.9 fusion.22
  45.5 4.9 subtract_bitcast_fusion.1
  50.5 5.7 %copy.39 = f32[40,4,64,64]{3,1,0,2:T(4,128)} copy(f32[40,4,64,64]{3,2,1,0:T(8,128)S(1)} %subtract_bitcast_fusion.1) | data formatting | bytes 5242880 | tf_op jit(solution)/shard_map/sub | solution.py:31
  56.2 7.7 %reshape.89 = f32[16,1,40960]{2,1,0:T(1,128)} reshape(f32[64,40,4,64]{3,2,1,0:T(4,128)} %bitcast.85) | data formatting | bytes 5242880
  63.9 7.8 %all-to-all-start.1 = ((f32[16,1,40960]{2,1,0:T(1,128)}), f32[16,1,40960]{2,1,0:T(1,128)}, u32[]{:S(2)}, u32[]{:S(2)}) async-start(f32[16,1,40960]{2,1,0:T(1,128)} %reshape.89), calls=%async_computation.1 | async-start | bytes 5242880 | tf_op jit(solution)/shard_map/all_to_all | solution.py:63
  71.7 7.0 %fusion.32 = f32[64,40,4,64]{3,0,2,1:T(8,128)S(1)} fusion(f32[40,4,64,64]{3,2,1,0:T(8,128)} %copy-done.4), kind=kOutput, calls=%fused_computation.60 | convolution fusion | flops 503373824 | bytes 5242880 | tf_op jit(solution)/shard_map/pxyz,ky->pxkz/dot_general | solution.py:19
  78.7 4.8 add_bitcast_fusion.1
  83.6 5.7 %copy.40 = f32[40,4,64,64]{3,1,0,2:T(4,128)} copy(f32[40,4,64,64]{3,2,1,0:T(8,128)S(1)} %add_bitcast_fusion.1) | data formatting | bytes 5242880 | tf_op jit(solution)/shard_map/add | solution.py:31
  89.3 8.1 %reshape.91 = f32[16,1,40960]{2,1,0:T(1,128)} reshape(f32[64,40,4,64]{3,2,1,0:T(4,128)} %bitcast.86) | data formatting | bytes 5242880
  97.4 24.5 %all-to-all-done.1 = f32[16,1,40960]{2,1,0:T(1,128)} async-done(((f32[16,1,40960]{2,1,0:T(1,128)}), f32[16,1,40960]{2,1,0:T(1,128)}, u32[]{:S(2)}, u32[]{:S(2)}) %all-to-all-start.1) | async-done | bytes 2621472 | tf_op jit(solution)/shard_map/all_to_all | solution.py:63
  121.9 13.3 %all-to-all-start = ((f32[16,1,40960]{2,1,0:T(1,128)}), f32[16,1,40960]{2,1,0:T(1,128)S(1)}, u32[]{:S(2)}, u32[]{:S(2)}) async-start(f32[16,1,40960]{2,1,0:T(1,128)} %reshape.91), calls=%async_computation | async-start | bytes 5242880 | tf_op jit(solution)/shard_map/all_to_all | solution.py:62
  136.0 10.2 %reduce.1 = f32[16,40960]{1,0:T(8,128)} reduce(f32[16,1,40960]{2,1,0:T(1,128)} %all-to-all-done.1, f32[]{:T(128)} %broadcast.127), dimensions={1}, to_apply=%all_to_all.58.reduce_sub_computation | reduce | bytes 5242884 | tf_op jit(solution)/shard_map/all_to_all | solution.py:63
  146.3 6.6 %reshape.90 = f32[64,40,4,64]{3,2,1,0:T(4,128)} reshape(f32[16,40960]{1,0:T(8,128)} %reduce.1) | data formatting | bytes 5242880
  152.9 6.3 %copy.22 = f32[40,4,16,4,64]{4,1,2,3,0:T(4,128)} copy(f32[40,4,16,4,64]{4,1,0,3,2:T(4,128)} %bitcast.87) | data formatting | bytes 5242880 | tf_op jit(solution)/shard_map/all_to_all | solution.py:63
  159.2 26.3 %all-to-all-done = f32[16,1,40960]{2,1,0:T(1,128)S(1)} async-done(((f32[16,1,40960]{2,1,0:T(1,128)}), f32[16,1,40960]{2,1,0:T(1,128)S(1)}, u32[]{:S(2)}, u32[]{:S(2)}) %all-to-all-start) | async-done | bytes 2621472 | tf_op jit(solution)/shard_map/all_to_all | solution.py:62
  185.5 9.2 %reduce = f32[16,40960]{1,0:T(8,128)} reduce(f32[16,1,40960]{2,1,0:T(1,128)S(1)} %all-to-all-done, f32[]{:T(128)} %broadcast.127), dimensions={1}, to_apply=%all_to_all.54.reduce_sub_computation | reduce | bytes 5242884 | tf_op jit(solution)/shard_map/all_to_all | solution.py:62
  194.7 6.7 %reshape.92 = f32[64,40,4,64]{3,2,1,0:T(4,128)} reshape(f32[16,40960]{1,0:T(8,128)} %reduce) | data formatting | bytes 5242880
  201.4 4.1 copy.20
  205.5 4.9 fusion.30
  210.4 5.3 %fusion.27 = f32[64,40,4,64]{3,0,2,1:T(8,128)S(1)} fusion(f32[40,64,4,64]{3,1,2,0:T(8,128)S(1)} %bitcast.77), kind=kOutput, calls=%fused_computation.55 | convolution fusion | flops 503373824 | bytes 5242880 | tf_op jit(solution)/shard_map/pxyz,kx->pkyz/dot_general | solution.py:25
  215.7 6.8 %add_bitcast_fusion = f32[40,64,4,64]{3,1,2,0:T(8,128)} fusion(f32[64,40,4,64]{3,0,2,1:T(8,128)S(1)} %fusion.30, f32[40,64,4,64]{3,1,2,0:T(8,128)S(1)} %bitcast.78), kind=kOutput, calls=%fused_computation.7 | convolution fusion | flops 504029184 | bytes 7864320 | tf_op jit(solution)/shard_map/pxyz,kx->pkyz/dot_general | solution.py:28
  222.5 6.8 %subtract_bitcast_fusion = f32[40,64,4,64]{3,1,2,0:T(8,128)} fusion(f32[64,40,4,64]{3,0,2,1:T(8,128)S(1)} %fusion.27, f32[40,64,4,64]{3,1,2,0:T(8,128)S(1)} %bitcast.80), kind=kOutput, calls=%fused_computation.6 | convolution fusion | flops 504029184 | bytes 7864320 | tf_op jit(solution)/shard_map/pxyz,kx->pkyz/dot_general | solution.py:22
  229.3 8.2 %copy.34 = f32[40,64,4,64]{0,3,2,1:T(8,128)} copy(f32[40,64,4,64]{3,1,2,0:T(8,128)} %subtract_bitcast_fusion) | data formatting | bytes 5242880 | tf_op jit(solution)/shard_map/reshape | solution.py:74
  237.4 8.1 %copy.33 = f32[40,64,4,64]{0,3,2,1:T(8,128)} copy(f32[40,64,4,64]{3,1,2,0:T(8,128)} %add_bitcast_fusion) | data formatting | bytes 5242880 | tf_op jit(solution)/shard_map/reshape | solution.py:73
  245.5 24.5 %gather_fusion.5 = f32[6144,40]{1,0:T(8,128)} fusion(f32[40,16384]{0,1:T(8,128)} %bitcast.84, s32[6144]{0:T(1024)S(1)} %fusion.43), kind=kCustom, calls=%fused_computation.5 | custom fusion | bytes 1990656 | tf_op jit(solution)/shard_map/gather | solution.py:74
  270.0 24.5 %gather_fusion.2 = f32[6144,40]{1,0:T(8,128)} fusion(f32[40,16384]{0,1:T(8,128)} %bitcast.83, s32[6144]{0:T(1024)S(1)} %fusion.43), kind=kCustom, calls=%fused_computation.2 | custom fusion | bytes 1990656 | tf_op jit(solution)/shard_map/gather | solution.py:73
  294.5 5.1 %multiply_bitcast_fusion.1 = (f32[40,6144]{0,1:T(8,128)}, f32[40,6144]{0,1:T(8,128)}) fusion(f32[6144,40]{1,0:T(8,128)} %gather_fusion.2, f32[6144]{0:T(1024)S(1)} %fusion.46, f32[6144,40]{1,0:T(8,128)} %gather_fusion.5), kind=kLoop, calls=%fused_computation.16 | loop fusion | flops 491520 | bytes 3956736 | tf_op jit(solution)/shard_map/mul | solution.py:73
  300.2 0.8 gather_fusion.3
  301.0 0.8 gather_fusion.4
  301.8 145.9 %all-reduce.3.cloned.1.call-done = (f32[40,6144]{0,1:T(8,128)}, f32[40,6144]{0,1:T(8,128)}) async-done(((f32[40,6144]{0,1:T(8,128)}, f32[40,6144]{0,1:T(8,128)}), (f32[40,6144]{0,1:T(8,128)}, f32[40,6144]{0,1:T(8,128)})) %all-reduce.3.cloned.1.call-update) | async-done | bytes 1966096 | tf_op jit(solution)/shard_map/psum | solution.py:77
  447.7 4.5 multiply_convert_fusion.1
  452.2 1.3 copy.30
  453.5 3.5 all-to-all-start.3
  457.0 2.3 copy.29
  459.3 5.5 %all-to-all-done.3 = bf16[40,2,3072]{2,0,1:T(8,128)(2,1)S(1)} async-done(((bf16[40,2,3072]{2,0,1:T(8,128)(2,1)}), bf16[40,2,3072]{2,0,1:T(8,128)(2,1)S(1)}, u32[]{:S(2)}, u32[]{:S(2)}) %all-to-all-start.3) | async-done | bytes 491552 | tf_op jit(solution)/shard_map/all_to_all | solution.py:86
  464.8 3.5 all-to-all-start.2
  468.3 0.9 constant_dynamic-slice_fusion.1
  469.4 6.5 %all_gather.7 = bf16[80,384]{1,0:T(8,128)(2,1)S(1)} all-gather(bf16[40,384]{1,0:T(8,128)(2,1)S(1)} %copy.28), channel_id=1, replica_groups=mesh['fft'=16,'grp'=2] {'grp'}, dimensions={0}, use_global_device_ids=true | all-gather | bytes 92160 | tf_op jit(solution)/shard_map/all_gather | solution.py:93
  475.9 4.6 all_gather.6
  480.5 3.0 convolution_subtract_fusion
  483.5 3.0 fusion.11
  (39 shorter events, 2.7 us)
Async XLA Ops:
  7.2 1.1 copy-start
  24.8 8.9 %copy-start.5 = (f32[40,4,64,64]{3,2,1,0:T(8,128)S(1)}, f32[40,4,64,64]{3,2,1,0:T(8,128)}, u32[]{:S(2)}) copy-start(f32[40,4,64,64]{3,2,1,0:T(8,128)} %mul.160) | copy-start | bytes 7864324
  33.6 11.9 %copy-start.6 = (f32[40,4,64,64]{3,2,1,0:T(8,128)}, f32[40,4,64,64]{3,2,1,0:T(8,128)S(1)}, u32[]{:S(2)}) copy-start(f32[40,4,64,64]{3,2,1,0:T(8,128)S(1)} %fusion.25) | copy-start | bytes 7864324
  38.2 2.4 copy-start.4
  63.9 14.8 %slice-start.2 = ((s8[5242880]{0:T(1024)(128)(4,1)}), s8[1048576]{0:T(1024)(128)(4,1)S(1)}, s32[]{:S(2)}) async-start(s8[5242880]{0:T(1024)(128)(4,1)} %bitcast.81), calls=%async_computation.7 | async-start | bytes 2097152
  63.9 58.0 %all-to-all-start.1 = ((f32[16,1,40960]{2,1,0:T(1,128)}), f32[16,1,40960]{2,1,0:T(1,128)}, u32[]{:S(2)}, u32[]{:S(2)}) async-start(f32[16,1,40960]{2,1,0:T(1,128)} %reshape.89), calls=%async_computation.1 | async-start | bytes 5242880 | tf_op jit(solution)/shard_map/all_to_all | solution.py:63
  71.7 7.1 %slice-start.3 = ((s8[5242880]{0:T(1024)(128)(4,1)}), s8[4194304]{0:T(1024)(128)(4,1)S(1)}, s32[]{:S(2)}) async-start(s8[5242880]{0:T(1024)(128)(4,1)} %bitcast.81), calls=%async_computation.8 | async-start | bytes 8388608
  89.3 46.0 %copy-start.7 = (s32[6144]{0:T(1024)S(1)}, s32[6144]{0:T(1024)}, u32[]{:S(2)}) copy-start(s32[6144]{0:T(1024)} %param.13) | copy-start | bytes 73732
  121.9 63.6 %all-to-all-start = ((f32[16,1,40960]{2,1,0:T(1,128)}), f32[16,1,40960]{2,1,0:T(1,128)S(1)}, u32[]{:S(2)}, u32[]{:S(2)}) async-start(f32[16,1,40960]{2,1,0:T(1,128)} %reshape.91), calls=%async_computation | async-start | bytes 5242880 | tf_op jit(solution)/shard_map/all_to_all | solution.py:62
  135.3 312.4 %all-reduce.3.cloned.1.call-start = ((), (), s32[]{:S(2)}) async-start(), calls=%async_computation.4 | async-start | bytes 12582912 | tf_op jit(solution)/shard_map/psum | solution.py:77
  201.4 9.0 %slice-start = ((s8[5242880]{0:T(1024)(128)(4,1)}), s8[1048576]{0:T(1024)(128)(4,1)S(1)}, s32[]{:S(2)}) async-start(s8[5242880]{0:T(1024)(128)(4,1)} %bitcast.75), calls=%async_computation.5 | async-start | bytes 2097152
  205.5 4.9 slice-start.1
  299.5 0.7 copy-start.3
  299.5 1.5 copy-start.2
  453.5 11.3 %all-to-all-start.3 = ((bf16[40,2,3072]{2,0,1:T(8,128)(2,1)}), bf16[40,2,3072]{2,0,1:T(8,128)(2,1)S(1)}, u32[]{:S(2)}, u32[]{:S(2)}) async-start(bf16[40,2,3072]{2,0,1:T(8,128)(2,1)} %copy.30), calls=%async_computation.3 | async-start | bytes 983040 | tf_op jit(solution)/shard_map/all_to_all | solution.py:86
  464.8 15.7 %all-to-all-start.2 = ((bf16[40,2,3072]{2,0,1:T(8,128)(2,1)}), bf16[40,2,3072]{2,0,1:T(8,128)(2,1)S(1)}, u32[]{:S(2)}, u32[]{:S(2)}) async-start(bf16[40,2,3072]{2,0,1:T(8,128)(2,1)} %copy.29), calls=%async_computation.2 | async-start | bytes 983040 | tf_op jit(solution)/shard_map/all_to_all | solution.py:85
  480.5 6.0 %copy-start.1 = (bf16[16,4,4096]{2,1,0:T(4,128)(2,1)S(1)}, bf16[16,4,4096]{2,1,0:T(4,128)(2,1)}, u32[]{:S(2)}) copy-start(bf16[16,4,4096]{2,1,0:T(4,128)(2,1)} %param.7) | copy-start | bytes 1572868
Sparse Core Ops, SparseCore 0:
  299.7 147.9 all-reduce.2
where the time goes:
time: 501 us; the launch traced here: 494 us
  waiting for transfers between devices  202 us (40%)
  local copies, waits for them, and re-layouts  141 us (28%)
  matrix products  64.8 us (13%)
  other arithmetic  31.9 us (6%)
  starting transfers between devices  28.1 us (6%)
  between operations  14.8 us (3%)
  blocking collectives  11 us (2%)
    psum x1, waiting for transfers between devices, per_device(): sum_real, sum_imag = lax.psum((part_real, part_imag), 'fft')  146 us
    unnamed x28, local copies, waits for them, and re-layouts  32.5 us
    all_to_all x1, waiting for transfers between devices, per_device(): lax.all_to_all(y_real, 'fft', split_axis=2, concat_axis=1, tiled=True)  26.3 us
    all_to_all x1, waiting for transfers between devices, per_device(): lax.all_to_all(y_imag, 'fft', split_axis=2, concat_axis=1, tiled=True)  24.5 us
    gather x1, local copies, waits for them, and re-layouts, per_device(): part_imag = k_imag.reshape(pair_count, -1)[:, local_index] * keep_mask  24.5 us
    gather x1, local copies, waits for them, and re-layouts, per_device(): part_real = k_real.reshape(pair_count, -1)[:, local_index] * keep_mask  24.5 us
    all_to_all x1, starting transfers between devices, per_device(): lax.all_to_all(y_real, 'fft', split_axis=2, concat_axis=1, tiled=True)  13.3 us
    dot_general x2, matrix products, rotate(): jnp.einsum(pattern, real_part, cos_table, precision=HIGHEST, preferred_el...  11.9 us
  transfers between devices with their start and end apart: 5, of which 4 were waited for; matrix products, arithmetic and copies ran while one was open for 11% of the time, Pallas kernels for 0%

commit v1 on v0

v1 whole, which is shorter than its diff:
```python
import functools
import math

import jax
import jax.numpy as jnp
import numpy as np
from jax import lax
from jax.experimental import pallas as pl
from jax.experimental.pallas import tpu as pltpu
from jax.sharding import PartitionSpec as P

LANES = 128
SLOT = 64
UNROLL = 8
BF16 = jnp.bfloat16
F32 = jnp.float32


def split_table(table):
    high = table.astype(np.float32).astype(jnp.bfloat16)
    low = (table - high.astype(np.float64)).astype(np.float32).astype(jnp.bfloat16)
    return high, low


def dft_tables(length, pair_count):
    half = length // 2 + 1
    group = 2 * LANES // length
    index = np.arange(length)
    angle = 2.0 * np.pi * (np.outer(index, index) % length) / length
    cosine, sine = np.cos(angle), np.sin(angle)
    z_table = np.zeros((half + half % 2, 2, group, group, length))
    for y in range(group):
        z_table[:half, 0, y, y, :] = cosine[:half]
        z_table[:half, 1, y, y, :] = -sine[:half]
    z_table = z_table.reshape(-1, group * length)
    y_table = np.zeros((2, length, length // group, 2, group))
    folded = lambda t: t.reshape(length, length // group, group)
    y_table[0, :, :, 0, :] = folded(cosine)
    y_table[0, :, :, 1, :] = folded(sine)
    y_table[1, :, :, 0, :] = folded(-sine)
    y_table[1, :, :, 1, :] = folded(cosine)
    y_table = y_table.reshape(2 * length, 2 * length)
    deep = [np.concatenate([high, high, low], 1) for high, low in map(split_table, (y_table, z_table))]
    tables = np.zeros((deep[0].shape[0] + deep[1].shape[0], deep[1].shape[1]), jnp.bfloat16)
    tables[: deep[0].shape[0], : deep[0].shape[1]] = deep[0]
    tables[deep[0].shape[0] :] = deep[1]
    pick = (np.arange(2 * LANES)[None, :] % SLOT == np.arange(pair_count)[:, None]).astype(jnp.bfloat16)
    return tables, pick


def split(values):
    high = values.astype(BF16)
    low = (values - high.astype(F32)).astype(BF16)
    return high, low


def dot_nt(left, right):
    return lax.dot_general(left, right, (((1,), (1,)), ((), ())), preferred_element_type=F32)


def transform_kernel(length, pair_count, info, psi_v, psi_c, source, plane, coef, *scratch):
    val, con, tables, density, rows_z, sems = scratch
    half = length // 2 + 1
    planes = psi_v.shape[1]
    chunks = density.shape[0]
    copies = [
        pltpu.make_async_copy(a, b, sems.at[pair_count + i]) for i, (a, b) in enumerate([(psi_v, val), (source, tables)])
    ]
    copies[0].start()

    def pair_copy(p):
        return pltpu.make_async_copy(psi_c.at[info[pair_count + p]], con.at[p], sems.at[p])

    for p in range(pair_count):
        pair_copy(p).start()
    copies[1].start()
    shape = (length, 4 * LANES)
    a = lax.broadcasted_iota(jnp.int32, shape, 0)
    lane = lax.broadcasted_iota(jnp.int32, shape, 1)
    x = lax.axis_index("fft") * planes + lane % (2 * LANES) // SLOT
    turn = a * x - length // 4 * (lane // (2 * LANES)) + length
    high, low = split(jnp.cos((turn % length).astype(F32) * (2.0 * math.pi / length)))
    coef[:length] = high
    coef[length:] = low
    copies[0].wait()
    for p in range(pair_count):
        pair_copy(p).wait()
        pair_density = con[p].astype(F32) * val[info[p]].astype(F32)
        for k in range(chunks):
            density[k, p * planes : (p + 1) * planes, :] = pair_density[:, k * LANES : (k + 1) * LANES]
    copies[1].wait()

    y_rows = 2 * length
    z_rows = half * 8

    def z_step(step, _):
        parts = []
        for k in range(2):
            blocks = []
            for x in range(planes):
                blocks.append(density[2 * step + k, pl.ds(x, pair_count, stride=planes), :])
                blocks.append(jnp.zeros((SLOT - pair_count, LANES), F32))
            blocks += [jnp.zeros((SLOT, LANES), F32)] * (4 - planes)
            parts.append(jnp.concatenate(blocks, 0))
        high, low = split(jnp.concatenate(parts, 1))
        result = dot_nt(tables[y_rows:, :], jnp.concatenate([high, low, high], 1))[:z_rows]
        rows_z[:, pl.ds(pl.multiple_of(step * 8, 8), 8), :] = result.reshape(half, 8, 2 * LANES)
        return 0

    lax.fori_loop(0, chunks // 2, z_step, 0, unroll=2)

    def y_step(c, _):
        high, low = split(rows_z[c])
        result = jnp.dot(
            tables[:y_rows, : 3 * y_rows], jnp.concatenate([high, low, high], 0), preferred_element_type=F32
        )
        for part in range(2):
            for xh in range(2):
                block = result[part * length : (part + 1) * length, xh * LANES : (xh + 1) * LANES]
                plane[pl.ds(c * (4 * length) + part * 2 + xh, length, stride=4), :] = block
        return 0

    lax.fori_loop(0, half, y_step, 0, unroll=3)


def transform(psi_v, psi_c, info, pair_count, tables):
    planes, plane_size = psi_v.shape[1], psi_v.shape[2]
    length = math.isqrt(plane_size)
    half = length // 2 + 1
    chunks = plane_size // LANES
    hbm = pl.BlockSpec(memory_space=pl.ANY)
    return pl.pallas_call(
        functools.partial(transform_kernel, length, pair_count),
        out_shape=[
            jax.ShapeDtypeStruct((half * length * 4, LANES), F32),
            jax.ShapeDtypeStruct((2 * length, 4 * LANES), BF16),
        ],
        in_specs=[pl.BlockSpec(memory_space=pltpu.SMEM)] + [hbm] * 3,
        out_specs=[pl.BlockSpec(memory_space=pltpu.VMEM)] * 2,
        scratch_shapes=[
            pltpu.VMEM(psi_v.shape, BF16),
            pltpu.VMEM((pair_count, planes, plane_size), BF16),
            pltpu.VMEM(tables.shape, BF16),
            pltpu.VMEM((chunks, pair_count * planes, LANES), F32),
            pltpu.VMEM((half, 2 * length, 2 * LANES), F32),
            pltpu.SemaphoreType.DMA((pair_count + 2,)),
        ],
        compiler_params=pltpu.CompilerParams(vmem_limit_bytes=46 * 2**20),
        name="transform",
    )(info, psi_v, psi_c, tables)


def landing(chip, chips):
    return chip * 2 % chips + chip // (chips // 2)


def points_kernel(length, pair_count, planes, width, order, info, phase, plane, coef, pick, *refs):
    out, tiles_0, tiles_1, peak = refs[-4:]
    me = lax.axis_index("fft")
    blocks, rows = out.shape[0], out.shape[1]
    chunked = order is not None
    peak[...] = jnp.zeros_like(peak)
    which = lax.broadcasted_iota(jnp.int32, (2 * length, width), 0) % length

    def index_of(block):
        if not chunked:
            return block
        far, across = order
        half = lax.rem(lax.rem(me, 2) + far, 2)
        chips = phase.shape[0] // 2
        return half * chips + landing(jnp.bitwise_xor(me // 2, 2 * block + across), chips)

    def gather(block, tiles):
        first = 2 * pair_count + index_of(block) * width
        for start in range(0, width, UNROLL):
            loaded = [plane[info[first + start + u]] for u in range(UNROLL)]
            for u in range(UNROLL):
                tiles[(start + u) * 4 : (start + u + 1) * 4, :] = loaded[u]

    def combine(block, tiles):
        turns = phase[index_of(block)]
        one_hot = jnp.where(which == turns % length, 1.0, 0.0).astype(BF16)
        factors = lax.dot_general(
            one_hot, coef[...], (((0,), (0,)), ((), ())), preferred_element_type=F32
        )
        cos = [factors[:, k * LANES : (k + 1) * LANES] for k in range(2)]
        sin = [factors[:, (k + 2) * LANES : (k + 3) * LANES] for k in range(2)]
        real = [tiles[pl.ds(k, width, stride=4), :] for k in range(2)]
        imag = [tiles[pl.ds(k + 2, width, stride=4), :] for k in range(2)]
        sums = (
            cos[0] * real[0] + sin[0] * imag[0] + (cos[1] * real[1] + sin[1] * imag[1]),
            cos[0] * imag[0] - sin[0] * real[0] + (cos[1] * imag[1] - sin[1] * real[1]),
        )
        sign = jnp.where(turns >= length, -1.0, 1.0)
        for to_imag in range(2):
            high, low = split(sums[to_imag])
            result = dot_nt(pick[...], jnp.concatenate([high, low], 1))
            if to_imag:
                result = result * sign
            if not chunked:
                out[block, to_imag * pair_count : (to_imag + 1) * pair_count, :] = result
                continue
            for k in range(width // LANES):
                start = (2 * k + to_imag) * pair_count
                tile = result[:, k * LANES : (k + 1) * LANES]
                out[block, start : start + pair_count, :] = tile
                peak[...] = jnp.maximum(peak[...], jnp.abs(tile))

    gather(0, tiles_0)

    def two_blocks(step, _):
        block = 2 * step
        gather(block + 1, tiles_1)
        combine(block, tiles_0)
        gather(jnp.minimum(block + 2, blocks - 1), tiles_0)
        combine(block + 1, tiles_1)
        return 0

    lax.fori_loop(0, blocks // 2, two_blocks, 0)
    if chunked:
        used = width // LANES * 2 * pair_count
        top = jnp.full((rows - used, LANES), jnp.max(peak[...]))
        for block in range(blocks):
            out[block, used:, :] = top


def points(plane, coef, pick, info, phase, length, pair_count, planes, out_shape, order, after):
    after = () if after is None else (after,)
    width = phase.shape[2]
    vmem = pl.BlockSpec(memory_space=pltpu.VMEM)
    return pl.pallas_call(
        functools.partial(points_kernel, length, pair_count, planes, width, order),
        out_shape=jax.ShapeDtypeStruct(out_shape, F32),
        in_specs=[pl.BlockSpec(memory_space=pltpu.SMEM)]
        + [vmem] * 4
        + [pl.BlockSpec(memory_space=pl.ANY)] * len(after),
        out_specs=vmem,
        scratch_shapes=[
            pltpu.VMEM((width * 4, LANES), F32),
            pltpu.VMEM((width * 4, LANES), F32),
            pltpu.VMEM((pair_count, LANES), F32),
        ],
        compiler_params=pltpu.CompilerParams(vmem_limit_bytes=12 * 2**20),
        cost_estimate=pl.CostEstimate(flops=10**9 * out_shape[0], bytes_accessed=2**20, transcendentals=0),
        name="points",
    )(info, phase, plane, coef, pick, *after)


def sphere_parts(psi_v, psi_c, pair_v, pair_c, g_index, devices, paired):
    planes, plane_size = psi_v.shape[1], psi_v.shape[2]
    length = math.isqrt(plane_size)
    pair_count = pair_v.shape[0]
    width = g_index.shape[0] // devices
    a, b, c = g_index // plane_size, g_index // length % length, g_index % length
    flip = c > length // 2
    mirrored = lambda k: jnp.where(flip, (length - k) % length, k)
    spot = mirrored(c) * length + mirrored(b)
    phase = (mirrored(a) + jnp.where(flip, length, 0)).reshape(devices, 1, width)
    info = jnp.concatenate([pair_v, pair_c, spot])
    tables, pick = dft_tables(length, pair_count)
    plane, coef = transform(psi_v, psi_c, info, pair_count, tables)
    rest = (plane.reshape(-1, 4, LANES), coef, pick, info, phase, length, pair_count, planes)
    if not paired:
        return points(*rest, (devices, 2 * pair_count, width), None, None)
    size = (width // LANES * 2 * pair_count + 16, LANES)
    quarter = devices // 4
    return [
        functools.partial(points, *rest, (quarter, *size), order)
        for order in ((1, 1), (0, 1), (1, 0), (0, 0))
    ]


def chi_kernel(groups, pair_count, first, rows, cols, real, imag, left):
    width = rows.shape[1]

    @pl.when(pl.program_id(0) == 0)
    def _():
        own = rows[...].astype(F32)
        cross = []
        for group in range(groups):
            start = group * 2 * pair_count
            cross.append(-own[start + pair_count : start + 2 * pair_count])
            cross.append(own[start : start + pair_count])
        left[:width] = (-own).T.astype(BF16)
        left[width:] = jnp.concatenate(cross, 0).T.astype(BF16)

    for k in range(cols.shape[0]):
        both = jnp.dot(left[...], cols[k], preferred_element_type=F32)
        real[:, k * width : (k + 1) * width] = both[:width]
        imag[:, k * width : (k + 1) * width] = both[width:]


def chi_blocks(rows, cols, first, blocks, groups, pair_count):
    depth, width = rows.shape
    out = jax.ShapeDtypeStruct((width, blocks * width), F32)
    step = LANES // math.gcd(width, LANES)
    out_spec = pl.BlockSpec((width, step * width), lambda j, first: (0, j))
    return pl.pallas_call(
        functools.partial(chi_kernel, groups, pair_count),
        out_shape=(out, out),
        grid_spec=pltpu.PrefetchScalarGridSpec(
            num_scalar_prefetch=1,
            grid=(blocks // step,),
            in_specs=[
                pl.BlockSpec((depth, width), lambda j, first: (0, 0)),
                pl.BlockSpec((step, depth, width), lambda j, first: (first[0] // step + j, 0, 0)),
            ],
            out_specs=(out_spec, out_spec),
            scratch_shapes=[pltpu.VMEM((2 * width, depth), BF16)],
        ),
        compiler_params=pltpu.CompilerParams(vmem_limit_bytes=32 * 2**20),
        name="chi",
    )(first, rows, cols)


def chi_direct_kernel(pair_count, width, skip, has_left, *refs):
    depth = 2 * pair_count
    chunks = width // LANES
    wide = lambda piece: jnp.concatenate([piece[k * depth : (k + 1) * depth] for k in range(chunks)], 1)
    chip, chips = lax.axis_index("fft") // 2, lax.axis_size("fft") // 2
    if has_left:
        left, refs = refs[0], refs[3:]
    else:
        row_refs, refs = refs[:2], refs[2:]
    cols, refs = refs[:2], refs[2:]
    count = cols[0].shape[0]
    real, imag, *refs = refs
    if not has_left:
        left, *refs = refs
        own = [wide(piece[...].astype(F32)) for piece in row_refs]
        cross = [part for piece in own for part in (-piece[pair_count:], piece[:pair_count])]
        left[:width] = (-jnp.concatenate(own, 0)).T.astype(BF16)
        left[width:] = jnp.concatenate(cross, 0).T.astype(BF16)
    stage, sems = refs

    def copies(s):
        block = landing(jnp.bitwise_xor(chip, 2 * s + skip), chips)
        start = pl.multiple_of(block * width, LANES)
        return [
            pltpu.make_async_copy(
                stage.at[s, pl.ds(i * width, width)], out.at[:, pl.ds(start, width)], sems.at[s, i]
            )
            for i, out in enumerate((real, imag))
        ]

    for s in range(count):
        right = jnp.concatenate([wide(cols[i][s][...]) for i in range(2)], 0)
        stage[s] = jnp.dot(left[...], right, preferred_element_type=F32)
        for copy in copies(s):
            copy.start()
    for s in range(count):
        for copy in copies(s):
            copy.wait()


def chi_direct(rows, cols, skip, done, pair_count, width, blocks):
    count = cols[0].shape[0]
    out = jax.ShapeDtypeStruct((width, blocks * width), F32)
    left = jax.ShapeDtypeStruct((2 * width, 4 * pair_count), BF16)
    vmem = pl.BlockSpec(memory_space=pltpu.VMEM)
    hbm = pl.BlockSpec(memory_space=pl.ANY)
    if done is None:
        args, specs, aliases = rows, [vmem, vmem], {}
        out_shape, out_specs = (out, out, left), (hbm, hbm, vmem)
    else:
        real, imag, left = done
        args, specs, aliases = (left, real, imag), [vmem, hbm, hbm], {1: 0, 2: 1}
        out_shape, out_specs = (out, out), (hbm, hbm)
    return pl.pallas_call(
        functools.partial(chi_direct_kernel, pair_count, width, skip, done is not None),
        out_shape=out_shape,
        in_specs=specs + [vmem] * 2,
        out_specs=out_specs,
        scratch_shapes=[
            pltpu.VMEM((count, 2 * width, width), F32),
            pltpu.SemaphoreType.DMA((count, 2)),
        ],
        input_output_aliases=aliases,
        compiler_params=pltpu.CompilerParams(vmem_limit_bytes=32 * 2**20),
        cost_estimate=pl.CostEstimate(
            flops=8 * count * width * width * pair_count * 2,
            bytes_accessed=8 * count * width * width,
            transcendentals=0,
        ),
        name="chi",
    )(*args, *cols)


def pair_factor(energy_v, energy_c, pair_v, pair_c, length):
    chosen = lambda table, which: jnp.sum(
        jnp.where(which[:, None] == jnp.arange(table.shape[0])[None, :], table[None, :], 0.0), 1
    )
    weight = 2.0 / (chosen(energy_c, pair_c) - chosen(energy_v, pair_v))
    return jnp.sqrt(weight) * (pair_v.shape[0] * lax.axis_size("grp")) ** (-0.25) * length ** (-1.5)


def permute(values, moves):
    chips = lax.axis_size("fft") // 2
    perm = []
    for chip in range(chips):
        for core in range(2):
            for y in range(2):
                to_chip, to_core, to_y = moves(chip, core, y)
                perm.append((chip * 4 + core * 2 + y, to_chip * 4 + to_core * 2 + to_y))
    return lax.ppermute(values, ("fft", "grp"), perm)


def encode(values, used):
    top = values[..., used : used + 1, :]
    exponent = jnp.ceil(jnp.log2(jnp.maximum(top, 2.0**-100))) - 14.0
    row = lax.broadcasted_iota(jnp.int32, values.shape, values.ndim - 2)
    return jnp.where(row < used, values * jnp.exp2(-exponent), exponent).astype(jnp.float16)


def decode(coded, used):
    scale = jnp.exp2(coded[..., used : used + 1, :].astype(F32))
    row = lax.broadcasted_iota(jnp.int32, coded.shape, coded.ndim - 2)
    return jnp.where(row < used, coded.astype(F32), 2.0**14) * scale


def two_groups(psi_v, psi_c, energy_v, energy_c, pair_v, pair_c, g_index):
    devices = lax.axis_size("fft")
    chips = devices // 2
    quarter = chips // 2
    length = math.isqrt(psi_v.shape[2])
    pair_count = pair_v.shape[0]
    width = g_index.shape[0] // devices
    chunks = width // LANES
    used = chunks * 2 * pair_count
    fft, grp = lax.axis_index("fft"), lax.axis_index("grp")
    factor = pair_factor(energy_v, energy_c, pair_v, pair_c, length)
    factor = jnp.tile(factor, 2 * chunks)[:, None]
    swap = lambda values: permute(values, lambda chip, core, y: (chip, 1 - core, y))
    swap_x = lambda values: permute(values, lambda chip, core, y: (chip ^ 1, core, y))

    calls = sphere_parts(psi_v, psi_c, pair_v, pair_c, g_index, devices, True)
    far_x = calls[0](None)
    arrived = swap(far_x)
    across = calls[1](far_x) + arrived
    coded, across = lax.optimization_barrier((encode(across, used), across))
    arrived_x = swap_x(coded)
    far = calls[2](across)
    arrived = swap(far)
    kept = calls[3](far) + arrived + decode(arrived_x, used)
    total = kept[0]
    for s in range(1, quarter):
        move = lambda chip, core, y, s=s: (chip ^ (2 * s), core, y)
        total = total + decode(permute(encode(kept[s], used), move), used)
    own = (total[:used] * factor).astype(BF16)

    first = jnp.stack(
        [permute(own, lambda chip, core, y, s=s: (chip ^ (2 * s), y, core)) for s in range(quarter)]
    )
    first_x = swap_x(first)
    second = swap(first)

    def row_home(chip, core):
        return chip % quarter + core * quarter, chip // quarter

    same = permute(own, lambda chip, core, y: (*row_home(chip, core), y))
    cross = permute(own, lambda chip, core, y: (*row_home(chip, core), 1 - y))
    agree = fft % 2 == grp
    rows = (jnp.where(agree, same, cross), jnp.where(agree, cross, same))
    done = chi_direct(rows, (first, second), 0, None, pair_count, width, chips)
    first_x, left = lax.optimization_barrier((first_x, done[2]))
    second_x = swap(first_x)
    done = (*done[:2], left)
    return chi_direct(None, (first_x, second_x), 1, done, pair_count, width, chips)


def any_groups(psi_v, psi_c, energy_v, energy_c, pair_v, pair_c, g_index):
    devices, groups = lax.axis_size("fft"), lax.axis_size("grp")
    length = math.isqrt(psi_v.shape[2])
    pair_count = pair_v.shape[0]
    parts = sphere_parts(psi_v, psi_c, pair_v, pair_c, g_index, devices, False)
    factor = pair_factor(energy_v, energy_c, pair_v, pair_c, length)
    factor = jnp.concatenate([factor, factor])
    arrived = lax.all_to_all(parts, "fft", split_axis=0, concat_axis=0, tiled=True)
    own = (jnp.sum(arrived, 0) * factor[:, None]).astype(BF16)
    rows = lax.all_gather(own, "grp", axis=0, tiled=True)
    cols = lax.all_gather(rows, "fft", axis=0, tiled=False)
    blocks = devices // groups
    first = (lax.axis_index("grp") * blocks).astype(jnp.int32).reshape(1)
    return chi_blocks(rows, cols, first, blocks, groups, pair_count)


def per_device(
    psi_valence,
    psi_conduction,
    energy_valence,
    energy_conduction,
    pair_valence,
    pair_conduction,
    g_index,
):
    args = (
        psi_valence,
        psi_conduction,
        energy_valence,
        energy_conduction,
        pair_valence,
        pair_conduction,
        g_index,
    )
    devices = lax.axis_size("fft")
    chips = devices // 2
    power_of_two = devices % 2 == 0 and chips & (chips - 1) == 0
    if lax.axis_size("grp") == 2 and power_of_two and chips >= 4 and g_index.shape[0] % (devices * LANES) == 0:
        return two_groups(*args)
    return any_groups(*args)


def solution(mesh):
    placed = (P(None, "fft", None), P(None, "fft", None), P(), P(), P("grp"), P("grp"), P())
    return jax.shard_map(
        per_device,
        mesh=mesh,
        in_specs=placed,
        out_specs=(P("fft", "grp"), P("fft", "grp")),
        check_vma=False,
    )
```

time: 501 us -> 75.1 us (0.15); the launches traced: 494 us -> 74.5 us
  waiting for transfers between devices: 202 us -> 13.9 us
  local copies, waits for them, and re-layouts: 141 us -> 5.22 us
  matrix products: 64.8 us -> 0 us
  Pallas kernels: 0 us -> 31.5 us
  other arithmetic: 31.9 us -> 1.88 us
  between operations: 14.8 us -> 0.93 us
  blocking collectives: 11 us -> 0 us
  starting transfers between devices: 28.1 us -> 21.1 us
    psum x1 -> x0, waiting for transfers between devices: 146 us -> none  [per_device(): sum_real, sum_imag = lax.psum((part_real, part_imag), 'fft')]
    dot_general x12 -> x0, matrix products: 64.8 us -> none  [the longest x2 11.9 us: rotate(): jnp.einsum(pattern, real_part, cos_table, precision=HIGHEST, preferred_el...]
    gather x6 -> x0, local copies, waits for them, and re-layouts: 60.9 us -> none  [the longest x1 24.5 us: per_device(): part_imag = k_imag.reshape(pair_count, -1)[:, local_index] * keep_mask]
    all_to_all x4 -> x0, waiting for transfers between devices: 56.3 us -> none  [the longest x1 26.3 us: per_device(): lax.all_to_all(y_real, 'fft', split_axis=2, concat_axis=1, tiled=True)]
    pallas_call x0 -> x7, Pallas kernels: none -> 31.5 us  [the longest x4 16.9 us: points(): pl.pallas_call(functools.partial(points_kernel, length, pair_count, plane...]
    unnamed x28 -> x20, local copies, waits for them, and re-layouts: 32.5 us -> 4.37 us
    all_to_all x4 -> x0, starting transfers between devices: 28 us -> none  [the longest x1 13.3 us: per_device(): lax.all_to_all(y_real, 'fft', split_axis=2, concat_axis=1, tiled=True)]
    ppermute x0 -> x15, starting transfers between devices: none -> 21.1 us  [permute(): return lax.ppermute(values, ('fft', 'grp'), perm)]
  transfers between devices with their start and end apart: 5 -> 15, of which waited for: 4 -> 5; matrix products, arithmetic and copies ran while one was open for 11% -> 1% of each run, Pallas kernels for 0% -> 15%
where the time goes in v1:
time: 75.1 us; the launch traced here: 74.5 us
  Pallas kernels  31.5 us (42%)
  starting transfers between devices  21.1 us (28%)
  waiting for transfers between devices  13.9 us (19%)
  local copies, waits for them, and re-layouts  5.22 us (7%)
  other arithmetic  1.88 us (3%)
  between operations  0.93 us (1%)
    ppermute x15, starting transfers between devices, permute(): return lax.ppermute(values, ('fft', 'grp'), perm)  21.1 us
    pallas_call x4, Pallas kernels, points(): pl.pallas_call(functools.partial(points_kernel, length, pair_count, plane...  16.9 us
    ppermute x15, waiting for transfers between devices, permute(): return lax.ppermute(values, ('fft', 'grp'), perm)  13.9 us
    pallas_call x1, Pallas kernels, transform(): pl.pallas_call(functools.partial(transform_kernel, length, pair_count), o...  9.31 us
    pallas_call x2, Pallas kernels, chi_direct(): pl.pallas_call(functools.partial(chi_direct_kernel, pair_count, width, sk...  5.33 us
    unnamed x20, local copies, waits for them, and re-layouts  4.37 us
  transfers between devices with their start and end apart: 15, of which 5 were waited for; matrix products, arithmetic and copies ran while one was open for 1% of the time, Pallas kernels for 15%

profile of v1, /device:TPU:0, one launch (start us, length us, event | category | flops | bytes accessed | tf_op | source)
XLA Modules:
  0.0 74.5 jit_solution(11554482712819246709)
XLA Ops:
  0.6 0.8 %fusion.23 = (s32[6144]{0:T(1024)S(1)}, s32[6144]{0:T(1024)S(1)}) fusion(s32[6144]{0:T(1024)} %param.15), kind=kLoop, calls=%fused_computation.55 | loop fusion | flops 516096 | bytes 73728 | tf_op jit(solution)/shard_map/add | solution.py:258
  1.5 0.8 %concatenate.3.info = s32[6224]{0:T(1024)S(1)} concatenate(s32[40]{0:T(128)} %param.13, s32[40]{0:T(128)} %param.14, s32[6144]{0:T(1024)S(1)} %get-tuple-element.38), dimensions={0} | concatenate | bytes 49792 | tf_op jit(solution)/shard_map/concatenate | solution.py:259
  2.2 0.0 copy-start
  2.2 1.1 %copy-done = bf16[400,768]{1,0:T(8,128)(2,1)S(1)} copy-done((bf16[400,768]{1,0:T(8,128)(2,1)S(1)}, bf16[400,768]{1,0:T(8,128)(2,1)}, u32[]{:S(2)}) %copy-start) | copy-done | bytes 614424
  3.3 1.0 %copy-done.1 = bf16[16,4,4096]{2,1,0:T(4,128)(2,1)S(1)} copy-done((bf16[16,4,4096]{2,1,0:T(4,128)(2,1)S(1)}, bf16[16,4,4096]{2,1,0:T(4,128)(2,1)}, u32[]{:S(2)}) %copy-start.1) | copy-done | bytes 524312
  4.3 9.3 %transform.1 = (f32[8448,128]{1,0:T(8,128)S(1)}, bf16[128,512]{1,0:T(8,128)(2,1)S(1)}) custom-call(s32[6224]{0:T(1024)S(1)} %concatenate.3.info, bf16[16,4,4096]{2,1,0:T(4,128)(2,1)S(1)} %copy-done.1, bf16[384,4,4096]{2,1,0:T(4,128)(2,1)} %psi_c.1, bf16[400,768]{1,0:T(8,128)(2,1)S(1)} %copy-done), custom_call_target="tpu_custom_call" | custom-call | tf_op jit(solution)/shard_map/transform/pallas_call | solution.py:132
  13.7 0.0 copy-start.2
  13.7 0.0 copy-start.8
  13.7 0.0 copy-start.9
  13.7 0.0 copy-start.6
  13.7 0.0 copy-start.7
  13.7 4.2 %points.4.refs_0_ = f32[4,256,128]{2,1,0:T(8,128)S(1)} custom-call(s32[6224]{0:T(1024)S(1)} %concatenate.3.info, s32[16,1,384]{2,1,0:T(1,128)S(1)} %bitcast.51, f32[2112,4,128]{2,1,0:T(4,128)S(1)} %bitcast.55, bf16[128,512]{1,0:T(8,128)(2,1)S(1)} %get-tuple-element.12.coef, bf16[40,256]{1,0:T(8,128)(2,1)S(1)} %copy-done.5), custom_call_target="tpu_custom_call" | custom-call | flops 4000000000 | bytes 1048576 | tf_op jit(solution)/shard_map/points/pallas_call | solution.py:231
  18.0 0.5 collective-permute-start
  18.5 0.1 select_reduce_fusion.1
  18.6 0.2 select_reduce_fusion
  18.8 0.1 mul.123
  18.9 0.0 copy-start.3
  18.9 2.2 %copy-done.3 = f32[8448,128]{1,0:T(8,128)S(1)} copy-done((f32[8448,128]{1,0:T(8,128)S(1)}, f32[8448,128]{1,0:T(8,128)}, u32[]{:S(2)}) %copy-start.3) | copy-done | bytes 4325400
  21.1 4.2 %points.5 = f32[4,256,128]{2,1,0:T(8,128)S(1)} custom-call(s32[6224]{0:T(1024)S(1)} %concatenate.3.info, s32[16,1,384]{2,1,0:T(1,128)S(1)} %bitcast.52, f32[2112,4,128]{2,1,0:T(4,128)S(1)} %bitcast.56, bf16[128,512]{1,0:T(8,128)(2,1)S(1)} %get-tuple-element.12.coef, bf16[40,256]{1,0:T(8,128)(2,1)S(1)} %copy-done.5, f32[4,256,128]{2,1,0:T(8,128)S(1)} %points.4.refs_0_), custom_call_target="tpu_custom_call" | custom-call | flops 4000000000 | bytes 1048576 | tf_op jit(solution)/shard_map/points/pallas_call | solution.py:231
  25.4 0.1 add.87.refs_0_
  25.4 0.1 select_convert_fusion
  25.6 4.2 %points.6.refs_0_ = f32[4,256,128]{2,1,0:T(8,128)S(1)} custom-call(s32[6224]{0:T(1024)S(1)} %concatenate.3.info, s32[16,1,384]{2,1,0:T(1,128)S(1)} %bitcast.53, f32[2112,4,128]{2,1,0:T(4,128)S(1)} %bitcast.57, bf16[128,512]{1,0:T(8,128)(2,1)S(1)} %get-tuple-element.12.coef, bf16[40,256]{1,0:T(8,128)(2,1)S(1)} %copy-done.5, f32[4,256,128]{2,1,0:T(8,128)S(1)} %add.87.refs_0_), custom_call_target="tpu_custom_call" | custom-call | flops 4000000000 | bytes 1048576 | tf_op jit(solution)/shard_map/points/pallas_call | solution.py:231
  29.8 2.6 %collective-permute-start.2 = (f16[4,256,128]{2,1,0:T(8,128)(2,1)S(1)}, f16[4,256,128]{2,1,0:T(8,128)(2,1)S(1)}, u32[]{:S(2)}, u32[]{:S(2)}) collective-permute-start(f16[4,256,128]{2,1,0:T(8,128)(2,1)S(1)} %select_convert_fusion), channel_id=1, source_target_pairs={{0,4},{1,5},{2,6},{3,7},{4,0},{5,1},{6,2},{7,3},{8,12},{9,13},{10,... | collective-permute-start | bytes 786440 | tf_op jit(solution)/shard_map/ppermute | solution.py:405
  32.4 0.2 collective-permute-start.1
  32.6 4.2 %points.7 = f32[4,256,128]{2,1,0:T(8,128)S(1)} custom-call(s32[6224]{0:T(1024)S(1)} %concatenate.3.info, s32[16,1,384]{2,1,0:T(1,128)S(1)} %bitcast.54, f32[2112,4,128]{2,1,0:T(4,128)S(1)} %bitcast.58, bf16[128,512]{1,0:T(8,128)(2,1)S(1)} %get-tuple-element.12.coef, bf16[40,256]{1,0:T(8,128)(2,1)S(1)} %copy-done.5, f32[4,256,128]{2,1,0:T(8,128)S(1)} %points.6.refs_0_), custom_call_target="tpu_custom_call" | custom-call | flops 4000000000 | bytes 1048576 | tf_op jit(solution)/shard_map/points/pallas_call | solution.py:231
  36.8 2.5 %collective-permute-done.2 = f16[4,256,128]{2,1,0:T(8,128)(2,1)S(1)} collective-permute-done((f16[4,256,128]{2,1,0:T(8,128)(2,1)S(1)}, f16[4,256,128]{2,1,0:T(8,128)(2,1)S(1)}, u32[]{:S(2)}, u32[]{:S(2)}) %collective-permute-start.2) | collective-permute-done | bytes 262176 | tf_op jit(solution)/shard_map/ppermute | solution.py:405
  39.4 0.2 multiply_add_fusion
  39.6 0.1 fusion.8
  39.7 1.9 %collective-permute-start.3 = (f16[256,128]{1,0:T(8,128)(2,1)S(1)}, f16[256,128]{1,0:T(8,128)(2,1)S(1)}, u32[]{:S(2)}, u32[]{:S(2)}) collective-permute-start(f16[256,128]{1,0:T(8,128)(2,1)S(1)} %get-tuple-element.28), channel_id=1, source_target_pairs={{0,8},{1,9},{2,10},{3,11},{4,12},{5,13},{6,14},{7,15},{8,0},{9,1},... | collective-permute-start | bytes 196616 | tf_op jit(solution)/shard_map/ppermute | solution.py:405
  41.7 2.5 %collective-permute-start.5 = (f16[256,128]{1,0:T(8,128)(2,1)S(1)}, f16[256,128]{1,0:T(8,128)(2,1)S(1)}, u32[]{:S(2)}, u32[]{:S(2)}) collective-permute-start(f16[256,128]{1,0:T(8,128)(2,1)S(1)} %get-tuple-element.29), channel_id=1, source_target_pairs={{0,24},{1,25},{2,26},{3,27},{4,28},{5,29},{6,30},{7,31},{8,16},{9,... | collective-permute-start | bytes 196616 | tf_op jit(solution)/shard_map/ppermute | solution.py:405
  44.2 0.2 collective-permute-start.4
  44.4 4.1 %collective-permute-done.5 = f16[256,128]{1,0:T(8,128)(2,1)S(1)} collective-permute-done((f16[256,128]{1,0:T(8,128)(2,1)S(1)}, f16[256,128]{1,0:T(8,128)(2,1)S(1)}, u32[]{:S(2)}, u32[]{:S(2)}) %collective-permute-start.5) | collective-permute-done | bytes 65568 | tf_op jit(solution)/shard_map/ppermute | solution.py:405
  48.5 2.1 %collective-permute-done.4 = f16[256,128]{1,0:T(8,128)(2,1)S(1)} collective-permute-done((f16[256,128]{1,0:T(8,128)(2,1)S(1)}, f16[256,128]{1,0:T(8,128)(2,1)S(1)}, u32[]{:S(2)}, u32[]{:S(2)}) %collective-permute-start.4) | collective-permute-done | bytes 65568 | tf_op jit(solution)/shard_map/ppermute | solution.py:405
  50.6 0.1 fusion.12
  50.7 2.4 %collective-permute-start.9 = (bf16[240,128]{1,0:T(8,128)(2,1)S(1)}, bf16[240,128]{1,0:T(8,128)(2,1)S(1)}, u32[]{:S(2)}, u32[]{:S(2)}) collective-permute-start(bf16[240,128]{1,0:T(8,128)(2,1)S(1)} %fusion.12), channel_id=1, source_target_pairs={{0,24},{1,26},{2,25},{3,27},{4,28},{5,30},{6,29},{7,31},{8,16},{9,... | collective-permute-start | bytes 184328 | tf_op jit(solution)/shard_map/ppermute | solution.py:405
  53.1 2.0 %collective-permute-start.7 = (bf16[240,128]{1,0:T(8,128)(2,1)S(1)}, bf16[240,128]{1,0:T(8,128)(2,1)S(1)}, u32[]{:S(2)}, u32[]{:S(2)}) collective-permute-start(bf16[240,128]{1,0:T(8,128)(2,1)S(1)} %fusion.12), channel_id=1, source_target_pairs={{0,8},{1,10},{2,9},{3,11},{4,12},{5,14},{6,13},{7,15},{8,0},{9,2},... | collective-permute-start | bytes 184328 | tf_op jit(solution)/shard_map/ppermute | solution.py:405
  55.2 0.7 collective-permute-start.6
  55.8 4.6 %collective-permute-start.12 = (bf16[240,128]{1,0:T(8,128)(2,1)S(1)}, bf16[240,128]{1,0:T(8,128)(2,1)S(1)}, u32[]{:S(2)}, u32[]{:S(2)}) collective-permute-start(bf16[240,128]{1,0:T(8,128)(2,1)S(1)} %fusion.12), channel_id=1, source_target_pairs={{0,1},{1,0},{2,17},{3,16},{4,5},{5,4},{6,21},{7,20},{8,9},{9,8},{1... | collective-permute-start | bytes 184328 | tf_op jit(solution)/shard_map/ppermute | solution.py:405
  60.4 0.0 collective-permute-done.9
  60.4 0.7 collective-permute-start.11
  61.1 0.0 collective-permute-done.8
  61.1 0.0 collective-permute-done.6
  61.2 1.3 %collective-permute-start.13 = (bf16[4,240,128]{2,1,0:T(8,128)(2,1)S(1)}, bf16[4,240,128]{2,1,0:T(8,128)(2,1)S(1)}, u32[]{:S(2)}, u32[]{:S(2)}) collective-permute-start(bf16[4,240,128]{2,1,0:T(8,128)(2,1)S(1)} %pad_maximum_fusion.refs_2_), channel_id=1, source_target_pairs={{0,2},{1,3},{2,0},{3,1},{4,6},{5,7},{6,4},{7,5},{8,10},{9,11},{10,... | collective-permute-start | bytes 737288 | tf_op jit(solution)/shard_map/ppermute | solution.py:405
  62.5 1.5 %collective-permute-start.10 = (bf16[4,240,128]{2,1,0:T(8,128)(2,1)S(1)}, bf16[4,240,128]{2,1,0:T(8,128)(2,1)S(1)}, u32[]{:S(2)}, u32[]{:S(2)}) collective-permute-start(bf16[4,240,128]{2,1,0:T(8,128)(2,1)S(1)} %pad_maximum_fusion.refs_2_), channel_id=1, source_target_pairs={{0,4},{1,5},{2,6},{3,7},{4,0},{5,1},{6,2},{7,3},{8,12},{9,13},{10,... | collective-permute-start | bytes 737288 | tf_op jit(solution)/shard_map/ppermute | solution.py:405
  64.0 2.7 %chi.2 = (f32[384,3072]{1,0:T(8,128)}, f32[384,3072]{1,0:T(8,128)}, bf16[768,160]{1,0:T(8,128)(2,1)S(1)}) custom-call(bf16[240,128]{1,0:T(8,128)(2,1)S(1)} %get-tuple-element.36.refs_0_, bf16[240,128]{1,0:T(8,128)(2,1)S(1)} %get-tuple-element.35.refs_1_, bf16[4,240,128]{2,1,0:T(8,128)(2,1)S(1)} %pad_maximum_fusion.refs_2_, ...), custom_call_target="tpu_custom_call" | custom-call | flops 377487360 | bytes 4718592 | tf_op jit(solution)/shard_map/chi/pallas_call | solution.py:369
  66.7 3.7 %collective-permute-done.10.refs_3_ = bf16[4,240,128]{2,1,0:T(8,128)(2,1)S(1)} collective-permute-done((bf16[4,240,128]{2,1,0:T(8,128)(2,1)S(1)}, bf16[4,240,128]{2,1,0:T(8,128)(2,1)S(1)}, u32[]{:S(2)}, u32[]{:S(2)}) %collective-permute-start.10) | collective-permute-done | bytes 245792 | tf_op jit(solution)/shard_map/ppermute | solution.py:405
  70.4 1.5 %collective-permute-done.14.refs_4_ = bf16[4,240,128]{2,1,0:T(8,128)(2,1)S(1)} collective-permute-done((bf16[4,240,128]{2,1,0:T(8,128)(2,1)S(1)}, bf16[4,240,128]{2,1,0:T(8,128)(2,1)S(1)}, u32[]{:S(2)}, u32[]{:S(2)}) %collective-permute-start.14) | collective-permute-done | bytes 245792 | tf_op jit(solution)/shard_map/ppermute | solution.py:405
  71.9 2.6 %chi.3 = (f32[384,3072]{1,0:T(8,128)}, f32[384,3072]{1,0:T(8,128)}) custom-call(bf16[768,160]{1,0:T(8,128)(2,1)S(1)} %get-tuple-element.16.refs_0_, f32[384,3072]{1,0:T(8,128)} %get-tuple-element.17.refs_1_, f32[384,3072]{1,0:T(8,128)} %get-tuple-element.18.refs_2_, ...), custom_call_target="tpu_custom_call", output_to_operand_aliasing={{0}: (1, {}), {1}: (2, {})} | custom-call | flops 377487360 | bytes 4718592 | tf_op jit(solution)/shard_map/chi/pallas_call | solution.py:369
  (31 shorter events, 0.2 us)
Async XLA Ops:
  2.2 1.1 %copy-start = (bf16[400,768]{1,0:T(8,128)(2,1)S(1)}, bf16[400,768]{1,0:T(8,128)(2,1)}, u32[]{:S(2)}) copy-start(bf16[400,768]{1,0:T(8,128)(2,1)} %constant.115.clone.source) | copy-start | bytes 1843204
  3.3 1.0 %copy-start.1 = (bf16[16,4,4096]{2,1,0:T(4,128)(2,1)S(1)}, bf16[16,4,4096]{2,1,0:T(4,128)(2,1)}, u32[]{:S(2)}) copy-start(bf16[16,4,4096]{2,1,0:T(4,128)(2,1)} %psi_v.1) | copy-start | bytes 1572868
  4.3 9.3 %copy-start.5 = (bf16[40,256]{1,0:T(8,128)(2,1)S(1)}, bf16[40,256]{1,0:T(8,128)(2,1)}, u32[]{:S(2)}) copy-start(bf16[40,256]{1,0:T(8,128)(2,1)} %constant.116.clone.pick) | copy-start | bytes 61444
  13.7 4.3 %copy-start.2 = (f32[8448,128]{1,0:T(8,128)}, f32[8448,128]{1,0:T(8,128)S(1)}, u32[]{:S(2)}) copy-start(f32[8448,128]{1,0:T(8,128)S(1)} %get-tuple-element.11) | copy-start | bytes 12976132
  13.7 4.8 %copy-start.8 = (s32[40]{0:T(128)S(1)}, s32[40]{0:T(128)}, u32[]{:S(2)}) copy-start(s32[40]{0:T(128)} %param.13) | copy-start | bytes 484
  13.7 4.8 %copy-start.9 = (f32[16]{0:T(128)S(1)}, f32[16]{0:T(128)}, u32[]{:S(2)}) copy-start(f32[16]{0:T(128)} %param.11) | copy-start | bytes 196
  13.7 4.9 %copy-start.6 = (s32[40]{0:T(128)S(1)}, s32[40]{0:T(128)}, u32[]{:S(2)}) copy-start(s32[40]{0:T(128)} %param.14) | copy-start | bytes 484
  13.7 4.9 %copy-start.7 = (f32[384]{0:T(512)S(1)}, f32[384]{0:T(512)}, u32[]{:S(2)}) copy-start(f32[384]{0:T(512)} %param.12) | copy-start | bytes 4612
  18.0 7.4 %collective-permute-start = (f32[4,256,128]{2,1,0:T(8,128)S(1)}, f32[4,256,128]{2,1,0:T(8,128)S(1)}, u32[]{:S(2)}, u32[]{:S(2)}) collective-permute-start(f32[4,256,128]{2,1,0:T(8,128)S(1)} %points.4.refs_0_), channel_id=1, source_target_pairs={{0,2},{1,3},{2,0},{3,1},{4,6},{5,7},{6,4},{7,5},{8,10},{9,11},{10,... | collective-permute-start | bytes 1572872 | tf_op jit(solution)/shard_map/ppermute | solution.py:405
  18.9 2.2 %copy-start.3 = (f32[8448,128]{1,0:T(8,128)S(1)}, f32[8448,128]{1,0:T(8,128)}, u32[]{:S(2)}) copy-start(f32[8448,128]{1,0:T(8,128)} %copy-done.2) | copy-start | bytes 12976132
  21.1 4.5 %copy-start.4 = (f32[8448,128]{1,0:T(8,128)S(1)}, f32[8448,128]{1,0:T(8,128)}, u32[]{:S(2)}) copy-start(f32[8448,128]{1,0:T(8,128)} %copy-done.2) | copy-start | bytes 12976132
  29.8 9.5 %collective-permute-start.2 = (f16[4,256,128]{2,1,0:T(8,128)(2,1)S(1)}, f16[4,256,128]{2,1,0:T(8,128)(2,1)S(1)}, u32[]{:S(2)}, u32[]{:S(2)}) collective-permute-start(f16[4,256,128]{2,1,0:T(8,128)(2,1)S(1)} %select_convert_fusion), channel_id=1, source_target_pairs={{0,4},{1,5},{2,6},{3,7},{4,0},{5,1},{6,2},{7,3},{8,12},{9,13},{10,... | collective-permute-start | bytes 786440 | tf_op jit(solution)/shard_map/ppermute | solution.py:405
  32.4 7.0 %collective-permute-start.1 = (f32[4,256,128]{2,1,0:T(8,128)S(1)}, f32[4,256,128]{2,1,0:T(8,128)S(1)}, u32[]{:S(2)}, u32[]{:S(2)}) collective-permute-start(f32[4,256,128]{2,1,0:T(8,128)S(1)} %points.6.refs_0_), channel_id=1, source_target_pairs={{0,2},{1,3},{2,0},{3,1},{4,6},{5,7},{6,4},{7,5},{8,10},{9,11},{10,... | collective-permute-start | bytes 1572872 | tf_op jit(solution)/shard_map/ppermute | solution.py:405
  39.7 4.6 %collective-permute-start.3 = (f16[256,128]{1,0:T(8,128)(2,1)S(1)}, f16[256,128]{1,0:T(8,128)(2,1)S(1)}, u32[]{:S(2)}, u32[]{:S(2)}) collective-permute-start(f16[256,128]{1,0:T(8,128)(2,1)S(1)} %get-tuple-element.28), channel_id=1, source_target_pairs={{0,8},{1,9},{2,10},{3,11},{4,12},{5,13},{6,14},{7,15},{8,0},{9,1},... | collective-permute-start | bytes 196616 | tf_op jit(solution)/shard_map/ppermute | solution.py:405
  41.7 6.8 %collective-permute-start.5 = (f16[256,128]{1,0:T(8,128)(2,1)S(1)}, f16[256,128]{1,0:T(8,128)(2,1)S(1)}, u32[]{:S(2)}, u32[]{:S(2)}) collective-permute-start(f16[256,128]{1,0:T(8,128)(2,1)S(1)} %get-tuple-element.29), channel_id=1, source_target_pairs={{0,24},{1,25},{2,26},{3,27},{4,28},{5,29},{6,30},{7,31},{8,16},{9,... | collective-permute-start | bytes 196616 | tf_op jit(solution)/shard_map/ppermute | solution.py:405
  44.2 6.4 %collective-permute-start.4 = (f16[256,128]{1,0:T(8,128)(2,1)S(1)}, f16[256,128]{1,0:T(8,128)(2,1)S(1)}, u32[]{:S(2)}, u32[]{:S(2)}) collective-permute-start(f16[256,128]{1,0:T(8,128)(2,1)S(1)} %get-tuple-element.30), channel_id=1, source_target_pairs={{0,16},{1,17},{2,18},{3,19},{4,20},{5,21},{6,22},{7,23},{8,24},{9,... | collective-permute-start | bytes 196616 | tf_op jit(solution)/shard_map/ppermute | solution.py:405
  50.7 9.7 %collective-permute-start.9 = (bf16[240,128]{1,0:T(8,128)(2,1)S(1)}, bf16[240,128]{1,0:T(8,128)(2,1)S(1)}, u32[]{:S(2)}, u32[]{:S(2)}) collective-permute-start(bf16[240,128]{1,0:T(8,128)(2,1)S(1)} %fusion.12), channel_id=1, source_target_pairs={{0,24},{1,26},{2,25},{3,27},{4,28},{5,30},{6,29},{7,31},{8,16},{9,... | collective-permute-start | bytes 184328 | tf_op jit(solution)/shard_map/ppermute | solution.py:405
  53.1 8.0 %collective-permute-start.8 = (bf16[240,128]{1,0:T(8,128)(2,1)S(1)}, bf16[240,128]{1,0:T(8,128)(2,1)S(1)}, u32[]{:S(2)}, u32[]{:S(2)}) collective-permute-start(bf16[240,128]{1,0:T(8,128)(2,1)S(1)} %fusion.12), channel_id=1, source_target_pairs={{0,16},{1,18},{2,17},{3,19},{4,20},{5,22},{6,21},{7,23},{8,24},{9,... | collective-permute-start | bytes 184328 | tf_op jit(solution)/shard_map/ppermute | solution.py:405
  53.1 8.0 %collective-permute-start.7 = (bf16[240,128]{1,0:T(8,128)(2,1)S(1)}, bf16[240,128]{1,0:T(8,128)(2,1)S(1)}, u32[]{:S(2)}, u32[]{:S(2)}) collective-permute-start(bf16[240,128]{1,0:T(8,128)(2,1)S(1)} %fusion.12), channel_id=1, source_target_pairs={{0,8},{1,10},{2,9},{3,11},{4,12},{5,14},{6,13},{7,15},{8,0},{9,2},... | collective-permute-start | bytes 184328 | tf_op jit(solution)/shard_map/ppermute | solution.py:405
  55.2 6.0 %collective-permute-start.6 = (bf16[240,128]{1,0:T(8,128)(2,1)S(1)}, bf16[240,128]{1,0:T(8,128)(2,1)S(1)}, u32[]{:S(2)}, u32[]{:S(2)}) collective-permute-start(bf16[240,128]{1,0:T(8,128)(2,1)S(1)} %fusion.12), channel_id=1, source_target_pairs={{0,0},{1,2},{2,1},{3,3},{4,4},{5,6},{6,5},{7,7},{8,8},{9,10},{10,9... | collective-permute-start | bytes 184328 | tf_op jit(solution)/shard_map/ppermute | solution.py:405
  55.8 8.1 %collective-permute-start.12 = (bf16[240,128]{1,0:T(8,128)(2,1)S(1)}, bf16[240,128]{1,0:T(8,128)(2,1)S(1)}, u32[]{:S(2)}, u32[]{:S(2)}) collective-permute-start(bf16[240,128]{1,0:T(8,128)(2,1)S(1)} %fusion.12), channel_id=1, source_target_pairs={{0,1},{1,0},{2,17},{3,16},{4,5},{5,4},{6,21},{7,20},{8,9},{9,8},{1... | collective-permute-start | bytes 184328 | tf_op jit(solution)/shard_map/ppermute | solution.py:405
  60.4 3.5 %collective-permute-start.11 = (bf16[240,128]{1,0:T(8,128)(2,1)S(1)}, bf16[240,128]{1,0:T(8,128)(2,1)S(1)}, u32[]{:S(2)}, u32[]{:S(2)}) collective-permute-start(bf16[240,128]{1,0:T(8,128)(2,1)S(1)} %fusion.12), channel_id=1, source_target_pairs={{0,0},{1,1},{2,16},{3,17},{4,4},{5,5},{6,20},{7,21},{8,8},{9,9},{1... | collective-permute-start | bytes 184328 | tf_op jit(solution)/shard_map/ppermute | solution.py:405
  61.2 2.8 %collective-permute-start.13 = (bf16[4,240,128]{2,1,0:T(8,128)(2,1)S(1)}, bf16[4,240,128]{2,1,0:T(8,128)(2,1)S(1)}, u32[]{:S(2)}, u32[]{:S(2)}) collective-permute-start(bf16[4,240,128]{2,1,0:T(8,128)(2,1)S(1)} %pad_maximum_fusion.refs_2_), channel_id=1, source_target_pairs={{0,2},{1,3},{2,0},{3,1},{4,6},{5,7},{6,4},{7,5},{8,10},{9,11},{10,... | collective-permute-start | bytes 737288 | tf_op jit(solution)/shard_map/ppermute | solution.py:405
  62.5 8.0 %collective-permute-start.10 = (bf16[4,240,128]{2,1,0:T(8,128)(2,1)S(1)}, bf16[4,240,128]{2,1,0:T(8,128)(2,1)S(1)}, u32[]{:S(2)}, u32[]{:S(2)}) collective-permute-start(bf16[4,240,128]{2,1,0:T(8,128)(2,1)S(1)} %pad_maximum_fusion.refs_2_), channel_id=1, source_target_pairs={{0,4},{1,5},{2,6},{3,7},{4,0},{5,1},{6,2},{7,3},{8,12},{9,13},{10,... | collective-permute-start | bytes 737288 | tf_op jit(solution)/shard_map/ppermute | solution.py:405
  70.4 1.5 %collective-permute-start.14 = (bf16[4,240,128]{2,1,0:T(8,128)(2,1)S(1)}, bf16[4,240,128]{2,1,0:T(8,128)(2,1)S(1)}, u32[]{:S(2)}, u32[]{:S(2)}) collective-permute-start(bf16[4,240,128]{2,1,0:T(8,128)(2,1)S(1)} %collective-permute-done.10.refs_3_), channel_id=1, source_target_pairs={{0,2},{1,3},{2,0},{3,1},{4,6},{5,7},{6,4},{7,5},{8,10},{9,11},{10,... | collective-permute-start | bytes 737288 | tf_op jit(solution)/shard_map/ppermute | solution.py:405

commit v2 on v1

--- a/solution.py
+++ b/solution.py
@@ -16,36 +16,14 @@
 F32 = jnp.float32
 
 
-def split_table(table):
-    high = table.astype(np.float32).astype(jnp.bfloat16)
-    low = (table - high.astype(np.float64)).astype(np.float32).astype(jnp.bfloat16)
-    return high, low
-
-
-def dft_tables(length, pair_count):
-    half = length // 2 + 1
-    group = 2 * LANES // length
-    index = np.arange(length)
-    angle = 2.0 * np.pi * (np.outer(index, index) % length) / length
-    cosine, sine = np.cos(angle), np.sin(angle)
-    z_table = np.zeros((half + half % 2, 2, group, group, length))
-    for y in range(group):
-        z_table[:half, 0, y, y, :] = cosine[:half]
-        z_table[:half, 1, y, y, :] = -sine[:half]
-    z_table = z_table.reshape(-1, group * length)
-    y_table = np.zeros((2, length, length // group, 2, group))
-    folded = lambda t: t.reshape(length, length // group, group)
-    y_table[0, :, :, 0, :] = folded(cosine)
-    y_table[0, :, :, 1, :] = folded(sine)
-    y_table[1, :, :, 0, :] = folded(-sine)
-    y_table[1, :, :, 1, :] = folded(cosine)
-    y_table = y_table.reshape(2 * length, 2 * length)
-    deep = [np.concatenate([high, high, low], 1) for high, low in map(split_table, (y_table, z_table))]
-    tables = np.zeros((deep[0].shape[0] + deep[1].shape[0], deep[1].shape[1]), jnp.bfloat16)
-    tables[: deep[0].shape[0], : deep[0].shape[1]] = deep[0]
-    tables[deep[0].shape[0] :] = deep[1]
-    pick = (np.arange(2 * LANES)[None, :] % SLOT == np.arange(pair_count)[:, None]).astype(jnp.bfloat16)
-    return tables, pick
+def cosine(turn, length):
+    from_half = jnp.abs(turn - length // 2)
+    folded = jnp.minimum(from_half, length // 2 - from_half)
+    square = (folded.astype(F32) * (2.0 * math.pi / length)) ** 2
+    value = jnp.full(square.shape, 1.0 / math.factorial(12), F32)
+    for order in range(10, -1, -2):
+        value = value * square + (-1.0) ** (order // 2) / math.factorial(order)
+    return jnp.where(from_half > length // 4, value, -value)
 
 
 def split(values):
@@ -58,62 +36,90 @@
     return lax.dot_general(left, right, (((1,), (1,)), ((), ())), preferred_element_type=F32)
 
 
-def transform_kernel(length, pair_count, info, psi_v, psi_c, source, plane, coef, *scratch):
-    val, con, tables, density, rows_z, sems = scratch
+def fill_tables(length, planes, z_table, y_table, coef):
+    quarter = length // 4
+    group = 2 * LANES // length
+
+    def put(table, values):
+        high, low = split(values)
+        for k, part in enumerate((high, high, low)):
+            table[:, k * values.shape[1] : (k + 1) * values.shape[1]] = part
+
+    shape = (z_table.shape[0], group * length)
+    row, column = (lax.broadcasted_iota(jnp.int32, shape, axis) for axis in range(2))
+    c, to_imag, y = row // (2 * group), row // group % 2, row % group
+    value = cosine((c * (column % length) + quarter * to_imag) % length, length)
+    put(z_table, jnp.where(column // length == y, value, 0.0))
+    shape = (2 * length, 2 * length)
+    row, column = (lax.broadcasted_iota(jnp.int32, shape, axis) for axis in range(2))
+    y, from_imag = column // (2 * group) * group + column % group, column // group % 2
+    turn = row % length * y + quarter * (row // length - from_imag) + length
+    put(y_table, cosine(turn % length, length))
+    shape = (length, 4 * LANES)
+    a, lane = (lax.broadcasted_iota(jnp.int32, shape, axis) for axis in range(2))
+    x = lax.axis_index("fft") * planes + lane % (2 * LANES) // SLOT
+    turn = a * x - quarter * (lane // (2 * LANES)) + length
+    high, low = split(cosine(turn % length, length))
+    coef[:length] = high
+    coef[length:] = low
+
+
+def transform_kernel(length, pair_count, info, g_index, psi_v, psi_c, plane, coef, spot, phase, *scratch):
+    val, con, z_table, y_table, chunk_0, chunk_1, rows_z, sems = scratch
     half = length // 2 + 1
     planes = psi_v.shape[1]
-    chunks = density.shape[0]
-    copies = [
-        pltpu.make_async_copy(a, b, sems.at[pair_count + i]) for i, (a, b) in enumerate([(psi_v, val), (source, tables)])
-    ]
-    copies[0].start()
+    steps = psi_v.shape[2] // (2 * LANES)
 
     def pair_copy(p):
         return pltpu.make_async_copy(psi_c.at[info[pair_count + p]], con.at[p], sems.at[p])
 
     for p in range(pair_count):
         pair_copy(p).start()
-    copies[1].start()
-    shape = (length, 4 * LANES)
-    a = lax.broadcasted_iota(jnp.int32, shape, 0)
-    lane = lax.broadcasted_iota(jnp.int32, shape, 1)
-    x = lax.axis_index("fft") * planes + lane % (2 * LANES) // SLOT
-    turn = a * x - length // 4 * (lane // (2 * LANES)) + length
-    high, low = split(jnp.cos((turn % length).astype(F32) * (2.0 * math.pi / length)))
-    coef[:length] = high
-    coef[length:] = low
-    copies[0].wait()
+    fill_tables(length, planes, z_table, y_table, coef)
+    points = g_index[...]
+    a, b, c = points // (length * length), points // length % length, points % length
+    flip = c > length // 2
+    mirrored = lambda k: jnp.where(flip, (length - k) % length, k)
+    spot[...] = mirrored(c) * length + mirrored(b)
+    phase[...] = mirrored(a) + jnp.where(flip, length, 0)
+    val[...] = psi_v[...].astype(F32)
     for p in range(pair_count):
         pair_copy(p).wait()
-        pair_density = con[p].astype(F32) * val[info[p]].astype(F32)
-        for k in range(chunks):
-            density[k, p * planes : (p + 1) * planes, :] = pair_density[:, k * LANES : (k + 1) * LANES]
-    copies[1].wait()
-
-    y_rows = 2 * length
-    z_rows = half * 8
-
-    def z_step(step, _):
+
+    def density(step, chunk):
+        lanes = pl.ds(pl.multiple_of(step * (2 * LANES), 2 * LANES), 2 * LANES)
+        for p in range(pair_count):
+            values = con[p, :, lanes].astype(F32) * val[info[p], :, lanes]
+            for k in range(2):
+                chunk[k, p * planes : (p + 1) * planes, :] = values[:, k * LANES : (k + 1) * LANES]
+
+    def z_step(step, chunk):
         parts = []
         for k in range(2):
             blocks = []
             for x in range(planes):
-                blocks.append(density[2 * step + k, pl.ds(x, pair_count, stride=planes), :])
+                blocks.append(chunk[k, pl.ds(x, pair_count, stride=planes), :])
                 blocks.append(jnp.zeros((SLOT - pair_count, LANES), F32))
             blocks += [jnp.zeros((SLOT, LANES), F32)] * (4 - planes)
             parts.append(jnp.concatenate(blocks, 0))
         high, low = split(jnp.concatenate(parts, 1))
-        result = dot_nt(tables[y_rows:, :], jnp.concatenate([high, low, high], 1))[:z_rows]
+        result = dot_nt(z_table[...], jnp.concatenate([high, low, high], 1))[: half * 8]
         rows_z[:, pl.ds(pl.multiple_of(step * 8, 8), 8), :] = result.reshape(half, 8, 2 * LANES)
+
+    density(0, chunk_0)
+
+    def two_steps(i, _):
+        density(2 * i + 1, chunk_1)
+        z_step(2 * i, chunk_0)
+        density(jnp.minimum(2 * i + 2, steps - 1), chunk_0)
+        z_step(2 * i + 1, chunk_1)
         return 0
 
-    lax.fori_loop(0, chunks // 2, z_step, 0, unroll=2)
+    lax.fori_loop(0, steps // 2, two_steps, 0)
 
     def y_step(c, _):
         high, low = split(rows_z[c])
-        result = jnp.dot(
-            tables[:y_rows, : 3 * y_rows], jnp.concatenate([high, low, high], 0), preferred_element_type=F32
-        )
+        result = jnp.dot(y_table[...], jnp.concatenate([high, low, high], 0), preferred_element_type=F32)
         for part in range(2):
             for xh in range(2):
                 block = result[part * length : (part + 1) * length, xh * LANES : (xh + 1) * LANES]
@@ -123,62 +129,73 @@
     lax.fori_loop(0, half, y_step, 0, unroll=3)
 
 
-def transform(psi_v, psi_c, info, pair_count, tables):
+def transform(psi_v, psi_c, info, pair_count, g_index):
     planes, plane_size = psi_v.shape[1], psi_v.shape[2]
     length = math.isqrt(plane_size)
     half = length // 2 + 1
-    chunks = plane_size // LANES
-    hbm = pl.BlockSpec(memory_space=pl.ANY)
+    vmem = pl.BlockSpec(memory_space=pltpu.VMEM)
+    index = jax.ShapeDtypeStruct(g_index.shape, jnp.int32)
     return pl.pallas_call(
         functools.partial(transform_kernel, length, pair_count),
         out_shape=[
             jax.ShapeDtypeStruct((half * length * 4, LANES), F32),
             jax.ShapeDtypeStruct((2 * length, 4 * LANES), BF16),
+            index,
+            index,
         ],
-        in_specs=[pl.BlockSpec(memory_space=pltpu.SMEM)] + [hbm] * 3,
-        out_specs=[pl.BlockSpec(memory_space=pltpu.VMEM)] * 2,
+        in_specs=[pl.BlockSpec(memory_space=pltpu.SMEM), vmem, vmem, pl.BlockSpec(memory_space=pl.ANY)],
+        out_specs=[vmem] * 4,
         scratch_shapes=[
-            pltpu.VMEM(psi_v.shape, BF16),
+            pltpu.VMEM(psi_v.shape, F32),
             pltpu.VMEM((pair_count, planes, plane_size), BF16),
-            pltpu.VMEM(tables.shape, BF16),
-            pltpu.VMEM((chunks, pair_count * planes, LANES), F32),
+            pltpu.VMEM(((half + half % 2) * 8, 6 * LANES), BF16),
+            pltpu.VMEM((2 * length, 6 * length), BF16),
+            pltpu.VMEM((2, pair_count * planes, LANES), F32),
+            pltpu.VMEM((2, pair_count * planes, LANES), F32),
             pltpu.VMEM((half, 2 * length, 2 * LANES), F32),
-            pltpu.SemaphoreType.DMA((pair_count + 2,)),
+            pltpu.SemaphoreType.DMA((pair_count,)),
         ],
-        compiler_params=pltpu.CompilerParams(vmem_limit_bytes=46 * 2**20),
+        compiler_params=pltpu.CompilerParams(vmem_limit_bytes=40 * 2**20),
         name="transform",
-    )(info, psi_v, psi_c, tables)
+    )(info, g_index, psi_v, psi_c)
 
 
 def landing(chip, chips):
     return chip * 2 % chips + chip // (chips // 2)
 
 
-def points_kernel(length, pair_count, planes, width, order, info, phase, plane, coef, pick, *refs):
-    out, tiles_0, tiles_1, peak = refs[-4:]
+def points_kernel(length, pair_count, width, orders, spot, phase, plane, coef, pick, *refs):
+    *refs, tiles_0, tiles_1, peak, local, sems = refs
+    outs = refs[-max(len(orders), 1) :]
     me = lax.axis_index("fft")
-    blocks, rows = out.shape[0], out.shape[1]
-    chunked = order is not None
-    peak[...] = jnp.zeros_like(peak)
+    blocks, rows = outs[0].shape[0], outs[0].shape[1]
+    last = blocks * len(outs) - 1
+    chunked = len(orders) > 0
     which = lax.broadcasted_iota(jnp.int32, (2 * length, width), 0) % length
 
     def index_of(block):
         if not chunked:
             return block
-        far, across = order
+        group, block = block // blocks, block % blocks
+        far, across = (
+            sum(jnp.where(group == k, order[axis], 0) for k, order in enumerate(orders)) for axis in range(2)
+        )
         half = lax.rem(lax.rem(me, 2) + far, 2)
         chips = phase.shape[0] // 2
         return half * chips + landing(jnp.bitwise_xor(me // 2, 2 * block + across), chips)
 
+    def fetch(block):
+        return pltpu.make_async_copy(spot.at[index_of(block)], local.at[block], sems.at[block])
+
     def gather(block, tiles):
-        first = 2 * pair_count + index_of(block) * width
         for start in range(0, width, UNROLL):
-            loaded = [plane[info[first + start + u]] for u in range(UNROLL)]
+            loaded = [plane[local[block, 0, start + u]] for u in range(UNROLL)]
             for u in range(UNROLL):
                 tiles[(start + u) * 4 : (start + u + 1) * 4, :] = loaded[u]
 
-    def combine(block, tiles):
-        turns = phase[index_of(block)]
+    def combine(group, block, tiles):
+        out = outs[group]
+        turns = phase[index_of(group * blocks + block)]
         one_hot = jnp.where(which == turns % length, 1.0, 0.0).astype(BF16)
         factors = lax.dot_general(
             one_hot, coef[...], (((0,), (0,)), ((), ())), preferred_element_type=F32
@@ -206,68 +223,67 @@
                 out[block, start : start + pair_count, :] = tile
                 peak[...] = jnp.maximum(peak[...], jnp.abs(tile))
 
+    for block in range(last + 1):
+        fetch(block).start()
+    peak[...] = jnp.zeros_like(peak)
+    fetch(0).wait()
     gather(0, tiles_0)
-
-    def two_blocks(step, _):
-        block = 2 * step
-        gather(block + 1, tiles_1)
-        combine(block, tiles_0)
-        gather(jnp.minimum(block + 2, blocks - 1), tiles_0)
-        combine(block + 1, tiles_1)
-        return 0
-
-    lax.fori_loop(0, blocks // 2, two_blocks, 0)
+    for block in range(1, last + 1):
+        fetch(block).wait()
+    for group in range(len(outs)):
+
+        def two_blocks(step, _):
+            block = group * blocks + 2 * step
+            gather(block + 1, tiles_1)
+            combine(group, 2 * step, tiles_0)
+            gather(jnp.minimum(block + 2, last), tiles_0)
+            combine(group, 2 * step + 1, tiles_1)
+            return 0
+
+        lax.fori_loop(0, blocks // 2, two_blocks, 0)
     if chunked:
         used = width // LANES * 2 * pair_count
         top = jnp.full((rows - used, LANES), jnp.max(peak[...]))
-        for block in range(blocks):
-            out[block, used:, :] = top
-
-
-def points(plane, coef, pick, info, phase, length, pair_count, planes, out_shape, order, after):
+        for out in outs:
+            for block in range(blocks):
+                out[block, used:, :] = top
+
+
+def points(spot, phase, plane, coef, pick, pair_count, out_shape, orders, after):
     after = () if after is None else (after,)
-    width = phase.shape[2]
+    count = max(len(orders), 1)
+    length, width = coef.shape[0] // 2, phase.shape[2]
     vmem = pl.BlockSpec(memory_space=pltpu.VMEM)
+    hbm = pl.BlockSpec(memory_space=pl.ANY)
     return pl.pallas_call(
-        functools.partial(points_kernel, length, pair_count, planes, width, order),
-        out_shape=jax.ShapeDtypeStruct(out_shape, F32),
-        in_specs=[pl.BlockSpec(memory_space=pltpu.SMEM)]
-        + [vmem] * 4
-        + [pl.BlockSpec(memory_space=pl.ANY)] * len(after),
-        out_specs=vmem,
+        functools.partial(points_kernel, length, pair_count, width, orders),
+        out_shape=[jax.ShapeDtypeStruct(out_shape, F32)] * count,
+        in_specs=[hbm] + [vmem] * 4 + [hbm] * len(after),
+        out_specs=[vmem] * count,
         scratch_shapes=[
             pltpu.VMEM((width * 4, LANES), F32),
             pltpu.VMEM((width * 4, LANES), F32),
             pltpu.VMEM((pair_count, LANES), F32),
+            pltpu.SMEM((count * out_shape[0], 1, width), jnp.int32),
+            pltpu.SemaphoreType.DMA((count * out_shape[0],)),
         ],
         compiler_params=pltpu.CompilerParams(vmem_limit_bytes=12 * 2**20),
-        cost_estimate=pl.CostEstimate(flops=10**9 * out_shape[0], bytes_accessed=2**20, transcendentals=0),
+        cost_estimate=pl.CostEstimate(flops=10**8 * out_shape[0], bytes_accessed=2**20, transcendentals=0),
         name="points",
-    )(info, phase, plane, coef, pick, *after)
+    )(spot, phase, plane, coef, pick, *after)
 
 
 def sphere_parts(psi_v, psi_c, pair_v, pair_c, g_index, devices, paired):
-    planes, plane_size = psi_v.shape[1], psi_v.shape[2]
-    length = math.isqrt(plane_size)
     pair_count = pair_v.shape[0]
     width = g_index.shape[0] // devices
-    a, b, c = g_index // plane_size, g_index // length % length, g_index % length
-    flip = c > length // 2
-    mirrored = lambda k: jnp.where(flip, (length - k) % length, k)
-    spot = mirrored(c) * length + mirrored(b)
-    phase = (mirrored(a) + jnp.where(flip, length, 0)).reshape(devices, 1, width)
-    info = jnp.concatenate([pair_v, pair_c, spot])
-    tables, pick = dft_tables(length, pair_count)
-    plane, coef = transform(psi_v, psi_c, info, pair_count, tables)
-    rest = (plane.reshape(-1, 4, LANES), coef, pick, info, phase, length, pair_count, planes)
+    info = jnp.concatenate([pair_v, pair_c])
+    plane, coef, spot, phase = transform(psi_v, psi_c, info, pair_count, g_index.reshape(devices, 1, width))
+    pick = (np.arange(2 * LANES)[None, :] % SLOT == np.arange(pair_count)[:, None]).astype(jnp.bfloat16)
+    rest = (spot, phase, plane.reshape(-1, 4, LANES), coef, pick, pair_count)
     if not paired:
-        return points(*rest, (devices, 2 * pair_count, width), None, None)
-    size = (width // LANES * 2 * pair_count + 16, LANES)
-    quarter = devices // 4
-    return [
-        functools.partial(points, *rest, (quarter, *size), order)
-        for order in ((1, 1), (0, 1), (1, 0), (0, 0))
-    ]
+        return points(*rest, (devices, 2 * pair_count, width), (), None)[0]
+    shape = (devices // 4, width // LANES * 2 * pair_count + 16, LANES)
+    return [functools.partial(points, *rest, shape, orders) for orders in (((1, 1),), ((0, 1),), ((1, 0), (0, 0)))]
 
 
 def chi_kernel(groups, pair_count, first, rows, cols, real, imag, left):
@@ -428,22 +444,24 @@
     chunks = width // LANES
     used = chunks * 2 * pair_count
     fft, grp = lax.axis_index("fft"), lax.axis_index("grp")
+    swap = lambda values: permute(values, lambda chip, core, y: (chip, 1 - core, y))
+    swap_x = lambda values: permute(values, lambda chip, core, y: (chip ^ 1, core, y))
+
+    calls = sphere_parts(psi_v, psi_c, pair_v, pair_c, g_index, devices, True)
+    (far,) = calls[0](None)
+    arrived = swap(far)
+    (across,) = calls[1](far)
+    across = across + arrived
+    coded, across = lax.optimization_barrier((encode(across, used), across))
+    arrived_x = swap_x(coded)
+    far, kept = calls[2](across)
+    arrived_x, far = lax.optimization_barrier((arrived_x, far))
+    kept = kept + swap(far) + decode(arrived_x, used)
+    (pair_v, pair_c), kept = lax.optimization_barrier(((pair_v, pair_c), kept))
     factor = pair_factor(energy_v, energy_c, pair_v, pair_c, length)
     factor = jnp.tile(factor, 2 * chunks)[:, None]
-    swap = lambda values: permute(values, lambda chip, core, y: (chip, 1 - core, y))
-    swap_x = lambda values: permute(values, lambda chip, core, y: (chip ^ 1, core, y))
-
-    calls = sphere_parts(psi_v, psi_c, pair_v, pair_c, g_index, devices, True)
-    far_x = calls[0](None)
-    arrived = swap(far_x)
-    across = calls[1](far_x) + arrived
-    coded, across = lax.optimization_barrier((encode(across, used), across))
-    arrived_x = swap_x(coded)
-    far = calls[2](across)
-    arrived = swap(far)
-    kept = calls[3](far) + arrived + decode(arrived_x, used)
     total = kept[0]
-    for s in range(1, quarter):
+    for s in reversed(range(1, quarter)):
         move = lambda chip, core, y, s=s: (chip ^ (2 * s), core, y)
         total = total + decode(permute(encode(kept[s], used), move), used)
     own = (total[:used] * factor).astype(BF16)

time: 75.1 us -> 67.3 us (0.90)
  local copies, waits for them, and re-layouts: 5.22 us -> 1.9 us
  Pallas kernels: 31.5 us -> 28.5 us
  waiting for transfers between devices: 13.9 us -> 12.8 us
    pallas_call x4 -> x3, Pallas kernels: 16.9 us -> 14.1 us  [points(): pl.pallas_call(functools.partial(points_kernel, length, pair_count, width...]
    unnamed x20 -> x14, local copies, waits for them, and re-layouts: 4.37 us -> 1.81 us
    ppermute x15, waiting for transfers between devices: 13.9 us -> 12.8 us  [permute(): return lax.ppermute(values, ('fft', 'grp'), perm)]
    add x3 -> x2, other arithmetic: 1.1 us -> 0.28 us  [the longest x1 0.23 us: two_groups(): kept = kept + swap(far) + decode(arrived_x, used)]
    concatenate x1 -> x0, local copies, waits for them, and re-layouts: 0.76 us -> none  [sphere_parts(): info = jnp.concatenate([pair_v, pair_c, spot])]
  transfers between devices with their start and end apart: 15 -> 15, of which waited for: 5 -> 7; matrix products, arithmetic and copies ran while one was open for 1% -> 1% of each run, Pallas kernels for 15% -> 20%
where the time goes in v2:
time: 67.3 us; the launch traced here: 66.9 us
  Pallas kernels  28.5 us (42%)
  starting transfers between devices  21 us (31%)
  waiting for transfers between devices  12.8 us (19%)
  local copies, waits for them, and re-layouts  1.9 us (3%)
  other arithmetic  1.81 us (3%)
  between operations  0.88 us (1%)
    ppermute x15, starting transfers between devices, permute(): return lax.ppermute(values, ('fft', 'grp'), perm)  21 us
    pallas_call x3, Pallas kernels, points(): pl.pallas_call(functools.partial(points_kernel, length, pair_count, width...  14.1 us
    ppermute x15, waiting for transfers between devices, permute(): return lax.ppermute(values, ('fft', 'grp'), perm)  12.8 us
    pallas_call x1, Pallas kernels, transform(): pl.pallas_call(functools.partial(transform_kernel, length, pair_count), o...  9 us
    pallas_call x2, Pallas kernels, chi_direct(): pl.pallas_call(functools.partial(chi_direct_kernel, pair_count, width, sk...  5.33 us
    unnamed x14, local copies, waits for them, and re-layouts  1.81 us
  transfers between devices with their start and end apart: 15, of which 7 were waited for; matrix products, arithmetic and copies ran while one was open for 1% of the time, Pallas kernels for 20%

profile of v2, /device:TPU:0, one launch (start us, length us, event | category | flops | bytes accessed | tf_op | source)
XLA Modules:
  0.0 66.9 jit_solution(6927791978056443405)
XLA Ops:
  0.6 0.7 %pad_add_fusion.info = s32[80]{0:T(128)S(1)} fusion(s32[40]{0:T(128)} %param.13, s32[40]{0:T(128)} %param.12), kind=kLoop, calls=%fused_computation.44 | loop fusion | flops 80 | bytes 640 | tf_op jit(solution)/shard_map/concatenate | solution.py:279
  1.4 1.0 %copy-done = bf16[16,4,4096]{2,1,0:T(4,128)(2,1)S(1)} copy-done((bf16[16,4,4096]{2,1,0:T(4,128)(2,1)S(1)}, bf16[16,4,4096]{2,1,0:T(4,128)(2,1)}, u32[]{:S(2)}) %copy-start) | copy-done | bytes 524312
  2.4 0.7 %copy-done.2 = s32[6144]{0:T(1024)S(1)} copy-done((s32[6144]{0:T(1024)S(1)}, s32[6144]{0:T(1024)}, u32[]{:S(2)}) %copy-start.2) | copy-done | bytes 24600
  3.2 9.0 %transform.1 = (f32[8448,128]{1,0:T(8,128)S(1)}, bf16[128,512]{1,0:T(8,128)(2,1)S(1)}, s32[16,1,384]{2,1,0:T(1,128)S(1)}, s32[16,1,384]{2,1,0:T(1,128)S(1)}) custom-call(s32[80]{0:T(128)S(1)} %pad_add_fusion.info, s32[16,1,384]{2,1,0:T(1,128)S(1)} %bitcast.48, bf16[16,4,4096]{2,1,0:T(4,128)(2,1)S(1)} %copy-done, bf16[384,4,4096]{2,1,0:T(4,128)(2,1)} %psi_c.1), custom_call_target="tpu_custom_call" | custom-call | tf_op jit(solution)/shard_map/transform/pallas_call | solution.py:138
  12.2 3.8 %points.3.refs_0_ = f32[4,256,128]{2,1,0:T(8,128)S(1)} custom-call(s32[16,1,384]{2,1,0:T(1,128)S(1)} %get-tuple-element.20.spot, s32[16,1,384]{2,1,0:T(1,128)S(1)} %get-tuple-element.21.phase, f32[2112,4,128]{2,1,0:T(4,128)S(1)} %bitcast.45, bf16[128,512]{1,0:T(8,128)(2,1)S(1)} %get-tuple-element.23.coef, bf16[40,256]{1,0:T(8,128)(2,1)S(1)} %copy-done.1), custom_call_target="tpu_custom_call" | custom-call | flops 400000000 | bytes 1048576 | tf_op jit(solution)/shard_map/points/pallas_call | solution.py:258
  16.0 0.5 collective-permute-start
  16.5 3.8 %points.4 = f32[4,256,128]{2,1,0:T(8,128)S(1)} custom-call(s32[16,1,384]{2,1,0:T(1,128)S(1)} %get-tuple-element.20.spot, s32[16,1,384]{2,1,0:T(1,128)S(1)} %get-tuple-element.21.phase, f32[2112,4,128]{2,1,0:T(4,128)S(1)} %bitcast.46, bf16[128,512]{1,0:T(8,128)(2,1)S(1)} %get-tuple-element.23.coef, bf16[40,256]{1,0:T(8,128)(2,1)S(1)} %copy-done.1, ...), custom_call_target="tpu_custom_call" | custom-call | flops 400000000 | bytes 1048576 | tf_op jit(solution)/shard_map/points/pallas_call | solution.py:258
  20.3 0.0 copy-start.3
  20.3 0.0 copy-start.4
  20.3 0.0 copy-start.5
  20.3 0.0 copy-start.6
  20.4 0.1 add.50.refs_0_
  20.4 0.1 select_convert_fusion
  20.6 2.6 %collective-permute-start.1 = (f16[4,256,128]{2,1,0:T(8,128)(2,1)S(1)}, f16[4,256,128]{2,1,0:T(8,128)(2,1)S(1)}, u32[]{:S(2)}, u32[]{:S(2)}) collective-permute-start(f16[4,256,128]{2,1,0:T(8,128)(2,1)S(1)} %select_convert_fusion), channel_id=1, source_target_pairs={{0,4},{1,5},{2,6},{3,7},{4,0},{5,1},{6,2},{7,3},{8,12},{9,13},{10,... | collective-permute-start | bytes 786440 | tf_op jit(solution)/shard_map/ppermute | solution.py:421
  23.2 6.5 %points.5 = (f32[4,256,128]{2,1,0:T(8,128)S(1)}, f32[4,256,128]{2,1,0:T(8,128)S(1)}) custom-call(s32[16,1,384]{2,1,0:T(1,128)S(1)} %get-tuple-element.20.spot, s32[16,1,384]{2,1,0:T(1,128)S(1)} %get-tuple-element.21.phase, f32[2112,4,128]{2,1,0:T(4,128)S(1)} %bitcast.47, bf16[128,512]{1,0:T(8,128)(2,1)S(1)} %get-tuple-element.23.coef, ...), custom_call_target="tpu_custom_call" | custom-call | flops 400000000 | bytes 1048576 | tf_op jit(solution)/shard_map/points/pallas_call | solution.py:258
  29.7 0.4 collective-permute-done.1
  30.1 1.9 %collective-permute-done.2 = f32[4,256,128]{2,1,0:T(8,128)S(1)} collective-permute-done((f32[4,256,128]{2,1,0:T(8,128)S(1)}, f32[4,256,128]{2,1,0:T(8,128)S(1)}, u32[]{:S(2)}, u32[]{:S(2)}) %collective-permute-start.2) | collective-permute-done | bytes 524320 | tf_op jit(solution)/shard_map/ppermute | solution.py:421
  32.0 0.2 multiply_add_fusion
  32.3 0.1 fusion.5
  32.4 3.9 %collective-permute-start.3 = (f16[256,128]{1,0:T(8,128)(2,1)S(1)}, f16[256,128]{1,0:T(8,128)(2,1)S(1)}, u32[]{:S(2)}, u32[]{:S(2)}) collective-permute-start(f16[256,128]{1,0:T(8,128)(2,1)S(1)} %get-tuple-element.46), channel_id=1, source_target_pairs={{0,24},{1,25},{2,26},{3,27},{4,28},{5,29},{6,30},{7,31},{8,16},{9,... | collective-permute-start | bytes 196616 | tf_op jit(solution)/shard_map/ppermute | solution.py:421
  36.3 0.2 select_reduce_fusion
  36.5 0.1 select_reduce_fusion.1
  36.7 0.1 mul.119
  36.7 0.0 collective-permute-start.5
  36.8 0.6 collective-permute-start.4
  37.3 1.9 %collective-permute-done.3 = f16[256,128]{1,0:T(8,128)(2,1)S(1)} collective-permute-done((f16[256,128]{1,0:T(8,128)(2,1)S(1)}, f16[256,128]{1,0:T(8,128)(2,1)S(1)}, u32[]{:S(2)}, u32[]{:S(2)}) %collective-permute-start.3) | collective-permute-done | bytes 65568 | tf_op jit(solution)/shard_map/ppermute | solution.py:421
  39.2 2.4 %collective-permute-done.5 = f16[256,128]{1,0:T(8,128)(2,1)S(1)} collective-permute-done((f16[256,128]{1,0:T(8,128)(2,1)S(1)}, f16[256,128]{1,0:T(8,128)(2,1)S(1)}, u32[]{:S(2)}, u32[]{:S(2)}) %collective-permute-start.5) | collective-permute-done | bytes 65568 | tf_op jit(solution)/shard_map/ppermute | solution.py:421
  41.6 1.1 %collective-permute-done.4 = f16[256,128]{1,0:T(8,128)(2,1)S(1)} collective-permute-done((f16[256,128]{1,0:T(8,128)(2,1)S(1)}, f16[256,128]{1,0:T(8,128)(2,1)S(1)}, u32[]{:S(2)}, u32[]{:S(2)}) %collective-permute-start.4) | collective-permute-done | bytes 65568 | tf_op jit(solution)/shard_map/ppermute | solution.py:421
  42.7 0.1 fusion.9
  42.8 2.5 %collective-permute-start.9 = (bf16[240,128]{1,0:T(8,128)(2,1)S(1)}, bf16[240,128]{1,0:T(8,128)(2,1)S(1)}, u32[]{:S(2)}, u32[]{:S(2)}) collective-permute-start(bf16[240,128]{1,0:T(8,128)(2,1)S(1)} %fusion.9), channel_id=1, source_target_pairs={{0,24},{1,26},{2,25},{3,27},{4,28},{5,30},{6,29},{7,31},{8,16},{9,... | collective-permute-start | bytes 184328 | tf_op jit(solution)/shard_map/ppermute | solution.py:421
  45.3 0.3 collective-permute-start.8
  45.6 1.7 %collective-permute-start.7 = (bf16[240,128]{1,0:T(8,128)(2,1)S(1)}, bf16[240,128]{1,0:T(8,128)(2,1)S(1)}, u32[]{:S(2)}, u32[]{:S(2)}) collective-permute-start(bf16[240,128]{1,0:T(8,128)(2,1)S(1)} %fusion.9), channel_id=1, source_target_pairs={{0,8},{1,10},{2,9},{3,11},{4,12},{5,14},{6,13},{7,15},{8,0},{9,2},... | collective-permute-start | bytes 184328 | tf_op jit(solution)/shard_map/ppermute | solution.py:421
  47.3 0.7 collective-permute-start.6
  48.0 4.6 %collective-permute-start.12 = (bf16[240,128]{1,0:T(8,128)(2,1)S(1)}, bf16[240,128]{1,0:T(8,128)(2,1)S(1)}, u32[]{:S(2)}, u32[]{:S(2)}) collective-permute-start(bf16[240,128]{1,0:T(8,128)(2,1)S(1)} %fusion.9), channel_id=1, source_target_pairs={{0,1},{1,0},{2,17},{3,16},{4,5},{5,4},{6,21},{7,20},{8,9},{9,8},{1... | collective-permute-start | bytes 184328 | tf_op jit(solution)/shard_map/ppermute | solution.py:421
  52.6 0.0 collective-permute-done.9
  52.6 0.7 collective-permute-start.11
  53.3 0.0 collective-permute-done.8
  53.3 0.0 collective-permute-done.7
  53.3 1.5 %collective-permute-start.13 = (bf16[4,240,128]{2,1,0:T(8,128)(2,1)S(1)}, bf16[4,240,128]{2,1,0:T(8,128)(2,1)S(1)}, u32[]{:S(2)}, u32[]{:S(2)}) collective-permute-start(bf16[4,240,128]{2,1,0:T(8,128)(2,1)S(1)} %pad_maximum_fusion.refs_2_), channel_id=1, source_target_pairs={{0,2},{1,3},{2,0},{3,1},{4,6},{5,7},{6,4},{7,5},{8,10},{9,11},{10,... | collective-permute-start | bytes 737288 | tf_op jit(solution)/shard_map/ppermute | solution.py:421
  54.8 1.5 %collective-permute-start.10 = (bf16[4,240,128]{2,1,0:T(8,128)(2,1)S(1)}, bf16[4,240,128]{2,1,0:T(8,128)(2,1)S(1)}, u32[]{:S(2)}, u32[]{:S(2)}) collective-permute-start(bf16[4,240,128]{2,1,0:T(8,128)(2,1)S(1)} %pad_maximum_fusion.refs_2_), channel_id=1, source_target_pairs={{0,4},{1,5},{2,6},{3,7},{4,0},{5,1},{6,2},{7,3},{8,12},{9,13},{10,... | collective-permute-start | bytes 737288 | tf_op jit(solution)/shard_map/ppermute | solution.py:421
  56.3 0.0 collective-permute-done.12
  56.3 0.0 collective-permute-done.11
  56.3 0.0 collective-permute-done.13.refs_3_
  56.3 2.7 %chi.2 = (f32[384,3072]{1,0:T(8,128)}, f32[384,3072]{1,0:T(8,128)}, bf16[768,160]{1,0:T(8,128)(2,1)S(1)}) custom-call(bf16[240,128]{1,0:T(8,128)(2,1)S(1)} %get-tuple-element.54.refs_0_, bf16[240,128]{1,0:T(8,128)(2,1)S(1)} %get-tuple-element.53.refs_1_, bf16[4,240,128]{2,1,0:T(8,128)(2,1)S(1)} %pad_maximum_fusion.refs_2_, ...), custom_call_target="tpu_custom_call" | custom-call | flops 377487360 | bytes 4718592 | tf_op jit(solution)/shard_map/chi/pallas_call | solution.py:385
  59.1 3.7 %collective-permute-done.10.refs_3_ = bf16[4,240,128]{2,1,0:T(8,128)(2,1)S(1)} collective-permute-done((bf16[4,240,128]{2,1,0:T(8,128)(2,1)S(1)}, bf16[4,240,128]{2,1,0:T(8,128)(2,1)S(1)}, u32[]{:S(2)}, u32[]{:S(2)}) %collective-permute-start.10) | collective-permute-done | bytes 245792 | tf_op jit(solution)/shard_map/ppermute | solution.py:421
  62.7 0.0 collective-permute-start.14
  62.8 1.5 %collective-permute-done.14.refs_4_ = bf16[4,240,128]{2,1,0:T(8,128)(2,1)S(1)} collective-permute-done((bf16[4,240,128]{2,1,0:T(8,128)(2,1)S(1)}, bf16[4,240,128]{2,1,0:T(8,128)(2,1)S(1)}, u32[]{:S(2)}, u32[]{:S(2)}) %collective-permute-start.14) | collective-permute-done | bytes 245792 | tf_op jit(solution)/shard_map/ppermute | solution.py:421
  64.3 2.6 %chi.3 = (f32[384,3072]{1,0:T(8,128)}, f32[384,3072]{1,0:T(8,128)}) custom-call(bf16[768,160]{1,0:T(8,128)(2,1)S(1)} %get-tuple-element.34.refs_0_, f32[384,3072]{1,0:T(8,128)} %get-tuple-element.35.refs_1_, f32[384,3072]{1,0:T(8,128)} %get-tuple-element.36.refs_2_, ...), custom_call_target="tpu_custom_call", output_to_operand_aliasing={{0}: (1, {}), {1}: (2, {})} | custom-call | flops 377487360 | bytes 4718592 | tf_op jit(solution)/shard_map/chi/pallas_call | solution.py:385
  (23 shorter events, 0.2 us)
Async XLA Ops:
  1.4 1.0 %copy-start = (bf16[16,4,4096]{2,1,0:T(4,128)(2,1)S(1)}, bf16[16,4,4096]{2,1,0:T(4,128)(2,1)}, u32[]{:S(2)}) copy-start(bf16[16,4,4096]{2,1,0:T(4,128)(2,1)} %psi_v.1) | copy-start | bytes 1572868
  2.4 0.7 %copy-start.2 = (s32[6144]{0:T(1024)S(1)}, s32[6144]{0:T(1024)}, u32[]{:S(2)}) copy-start(s32[6144]{0:T(1024)} %param.14) | copy-start | bytes 73732
  3.2 9.0 %copy-start.1 = (bf16[40,256]{1,0:T(8,128)(2,1)S(1)}, bf16[40,256]{1,0:T(8,128)(2,1)}, u32[]{:S(2)}) copy-start(bf16[40,256]{1,0:T(8,128)(2,1)} %constant.52.clone.pick) | copy-start | bytes 61444
  16.0 4.4 %collective-permute-start = (f32[4,256,128]{2,1,0:T(8,128)S(1)}, f32[4,256,128]{2,1,0:T(8,128)S(1)}, u32[]{:S(2)}, u32[]{:S(2)}) collective-permute-start(f32[4,256,128]{2,1,0:T(8,128)S(1)} %points.3.refs_0_), channel_id=1, source_target_pairs={{0,2},{1,3},{2,0},{3,1},{4,6},{5,7},{6,4},{7,5},{8,10},{9,11},{10,... | collective-permute-start | bytes 1572872 | tf_op jit(solution)/shard_map/ppermute | solution.py:421
  20.3 16.0 %copy-start.3 = (f32[384]{0:T(512)S(1)}, f32[384]{0:T(512)}, u32[]{:S(2)}) copy-start(f32[384]{0:T(512)} %param.11) | copy-start | bytes 4612
  20.3 16.0 %copy-start.4 = (s32[40]{0:T(128)S(1)}, s32[40]{0:T(128)}, u32[]{:S(2)}) copy-start(s32[40]{0:T(128)} %param.13) | copy-start | bytes 484
  20.3 16.2 %copy-start.5 = (s32[40]{0:T(128)S(1)}, s32[40]{0:T(128)}, u32[]{:S(2)}) copy-start(s32[40]{0:T(128)} %param.12) | copy-start | bytes 484
  20.3 16.2 %copy-start.6 = (f32[16]{0:T(128)S(1)}, f32[16]{0:T(128)}, u32[]{:S(2)}) copy-start(f32[16]{0:T(128)} %param.10) | copy-start | bytes 196
  20.6 9.5 %collective-permute-start.1 = (f16[4,256,128]{2,1,0:T(8,128)(2,1)S(1)}, f16[4,256,128]{2,1,0:T(8,128)(2,1)S(1)}, u32[]{:S(2)}, u32[]{:S(2)}) collective-permute-start(f16[4,256,128]{2,1,0:T(8,128)(2,1)S(1)} %select_convert_fusion), channel_id=1, source_target_pairs={{0,4},{1,5},{2,6},{3,7},{4,0},{5,1},{6,2},{7,3},{8,12},{9,13},{10,... | collective-permute-start | bytes 786440 | tf_op jit(solution)/shard_map/ppermute | solution.py:421
  30.1 1.9 %collective-permute-start.2 = (f32[4,256,128]{2,1,0:T(8,128)S(1)}, f32[4,256,128]{2,1,0:T(8,128)S(1)}, u32[]{:S(2)}, u32[]{:S(2)}) collective-permute-start(f32[4,256,128]{2,1,0:T(8,128)S(1)} %get-tuple-element.28), channel_id=1, source_target_pairs={{0,2},{1,3},{2,0},{3,1},{4,6},{5,7},{6,4},{7,5},{8,10},{9,11},{10,... | collective-permute-start | bytes 1572872 | tf_op jit(solution)/shard_map/ppermute | solution.py:421
  32.4 6.8 %collective-permute-start.3 = (f16[256,128]{1,0:T(8,128)(2,1)S(1)}, f16[256,128]{1,0:T(8,128)(2,1)S(1)}, u32[]{:S(2)}, u32[]{:S(2)}) collective-permute-start(f16[256,128]{1,0:T(8,128)(2,1)S(1)} %get-tuple-element.46), channel_id=1, source_target_pairs={{0,24},{1,25},{2,26},{3,27},{4,28},{5,29},{6,30},{7,31},{8,16},{9,... | collective-permute-start | bytes 196616 | tf_op jit(solution)/shard_map/ppermute | solution.py:421
  36.7 4.9 %collective-permute-start.5 = (f16[256,128]{1,0:T(8,128)(2,1)S(1)}, f16[256,128]{1,0:T(8,128)(2,1)S(1)}, u32[]{:S(2)}, u32[]{:S(2)}) collective-permute-start(f16[256,128]{1,0:T(8,128)(2,1)S(1)} %get-tuple-element.47), channel_id=1, source_target_pairs={{0,8},{1,9},{2,10},{3,11},{4,12},{5,13},{6,14},{7,15},{8,0},{9,1},... | collective-permute-start | bytes 196616 | tf_op jit(solution)/shard_map/ppermute | solution.py:421
  36.8 5.9 %collective-permute-start.4 = (f16[256,128]{1,0:T(8,128)(2,1)S(1)}, f16[256,128]{1,0:T(8,128)(2,1)S(1)}, u32[]{:S(2)}, u32[]{:S(2)}) collective-permute-start(f16[256,128]{1,0:T(8,128)(2,1)S(1)} %get-tuple-element.48), channel_id=1, source_target_pairs={{0,16},{1,17},{2,18},{3,19},{4,20},{5,21},{6,22},{7,23},{8,24},{9,... | collective-permute-start | bytes 196616 | tf_op jit(solution)/shard_map/ppermute | solution.py:421
  42.8 9.7 %collective-permute-start.9 = (bf16[240,128]{1,0:T(8,128)(2,1)S(1)}, bf16[240,128]{1,0:T(8,128)(2,1)S(1)}, u32[]{:S(2)}, u32[]{:S(2)}) collective-permute-start(bf16[240,128]{1,0:T(8,128)(2,1)S(1)} %fusion.9), channel_id=1, source_target_pairs={{0,24},{1,26},{2,25},{3,27},{4,28},{5,30},{6,29},{7,31},{8,16},{9,... | collective-permute-start | bytes 184328 | tf_op jit(solution)/shard_map/ppermute | solution.py:421
  45.3 7.9 %collective-permute-start.8 = (bf16[240,128]{1,0:T(8,128)(2,1)S(1)}, bf16[240,128]{1,0:T(8,128)(2,1)S(1)}, u32[]{:S(2)}, u32[]{:S(2)}) collective-permute-start(bf16[240,128]{1,0:T(8,128)(2,1)S(1)} %fusion.9), channel_id=1, source_target_pairs={{0,16},{1,18},{2,17},{3,19},{4,20},{5,22},{6,21},{7,23},{8,24},{9,... | collective-permute-start | bytes 184328 | tf_op jit(solution)/shard_map/ppermute | solution.py:421
  45.6 7.6 %collective-permute-start.7 = (bf16[240,128]{1,0:T(8,128)(2,1)S(1)}, bf16[240,128]{1,0:T(8,128)(2,1)S(1)}, u32[]{:S(2)}, u32[]{:S(2)}) collective-permute-start(bf16[240,128]{1,0:T(8,128)(2,1)S(1)} %fusion.9), channel_id=1, source_target_pairs={{0,8},{1,10},{2,9},{3,11},{4,12},{5,14},{6,13},{7,15},{8,0},{9,2},... | collective-permute-start | bytes 184328 | tf_op jit(solution)/shard_map/ppermute | solution.py:421
  47.3 6.0 %collective-permute-start.6 = (bf16[240,128]{1,0:T(8,128)(2,1)S(1)}, bf16[240,128]{1,0:T(8,128)(2,1)S(1)}, u32[]{:S(2)}, u32[]{:S(2)}) collective-permute-start(bf16[240,128]{1,0:T(8,128)(2,1)S(1)} %fusion.9), channel_id=1, source_target_pairs={{0,0},{1,2},{2,1},{3,3},{4,4},{5,6},{6,5},{7,7},{8,8},{9,10},{10,9... | collective-permute-start | bytes 184328 | tf_op jit(solution)/shard_map/ppermute | solution.py:421
  48.0 8.3 %collective-permute-start.12 = (bf16[240,128]{1,0:T(8,128)(2,1)S(1)}, bf16[240,128]{1,0:T(8,128)(2,1)S(1)}, u32[]{:S(2)}, u32[]{:S(2)}) collective-permute-start(bf16[240,128]{1,0:T(8,128)(2,1)S(1)} %fusion.9), channel_id=1, source_target_pairs={{0,1},{1,0},{2,17},{3,16},{4,5},{5,4},{6,21},{7,20},{8,9},{9,8},{1... | collective-permute-start | bytes 184328 | tf_op jit(solution)/shard_map/ppermute | solution.py:421
  52.6 3.7 %collective-permute-start.11 = (bf16[240,128]{1,0:T(8,128)(2,1)S(1)}, bf16[240,128]{1,0:T(8,128)(2,1)S(1)}, u32[]{:S(2)}, u32[]{:S(2)}) collective-permute-start(bf16[240,128]{1,0:T(8,128)(2,1)S(1)} %fusion.9), channel_id=1, source_target_pairs={{0,0},{1,1},{2,16},{3,17},{4,4},{5,5},{6,20},{7,21},{8,8},{9,9},{1... | collective-permute-start | bytes 184328 | tf_op jit(solution)/shard_map/ppermute | solution.py:421
  53.3 3.0 %collective-permute-start.13 = (bf16[4,240,128]{2,1,0:T(8,128)(2,1)S(1)}, bf16[4,240,128]{2,1,0:T(8,128)(2,1)S(1)}, u32[]{:S(2)}, u32[]{:S(2)}) collective-permute-start(bf16[4,240,128]{2,1,0:T(8,128)(2,1)S(1)} %pad_maximum_fusion.refs_2_), channel_id=1, source_target_pairs={{0,2},{1,3},{2,0},{3,1},{4,6},{5,7},{6,4},{7,5},{8,10},{9,11},{10,... | collective-permute-start | bytes 737288 | tf_op jit(solution)/shard_map/ppermute | solution.py:421
  54.8 8.0 %collective-permute-start.10 = (bf16[4,240,128]{2,1,0:T(8,128)(2,1)S(1)}, bf16[4,240,128]{2,1,0:T(8,128)(2,1)S(1)}, u32[]{:S(2)}, u32[]{:S(2)}) collective-permute-start(bf16[4,240,128]{2,1,0:T(8,128)(2,1)S(1)} %pad_maximum_fusion.refs_2_), channel_id=1, source_target_pairs={{0,4},{1,5},{2,6},{3,7},{4,0},{5,1},{6,2},{7,3},{8,12},{9,13},{10,... | collective-permute-start | bytes 737288 | tf_op jit(solution)/shard_map/ppermute | solution.py:421
  62.7 1.5 %collective-permute-start.14 = (bf16[4,240,128]{2,1,0:T(8,128)(2,1)S(1)}, bf16[4,240,128]{2,1,0:T(8,128)(2,1)S(1)}, u32[]{:S(2)}, u32[]{:S(2)}) collective-permute-start(bf16[4,240,128]{2,1,0:T(8,128)(2,1)S(1)} %collective-permute-done.10.refs_3_), channel_id=1, source_target_pairs={{0,2},{1,3},{2,0},{3,1},{4,6},{5,7},{6,4},{7,5},{8,10},{9,11},{10,... | collective-permute-start | bytes 737288 | tf_op jit(solution)/shard_map/ppermute | solution.py:421

commit v3 on v2

--- a/solution.py
+++ b/solution.py
@@ -36,20 +36,25 @@
     return lax.dot_general(left, right, (((1,), (1,)), ((), ())), preferred_element_type=F32)
 
 
-def fill_tables(length, planes, z_table, y_table, coef):
+def put(table, values):
+    high, low = split(values)
+    for k, part in enumerate((high, high, low)):
+        table[:, k * values.shape[1] : (k + 1) * values.shape[1]] = part
+
+
+def fill_z_table(length, z_table):
     quarter = length // 4
     group = 2 * LANES // length
-
-    def put(table, values):
-        high, low = split(values)
-        for k, part in enumerate((high, high, low)):
-            table[:, k * values.shape[1] : (k + 1) * values.shape[1]] = part
-
     shape = (z_table.shape[0], group * length)
     row, column = (lax.broadcasted_iota(jnp.int32, shape, axis) for axis in range(2))
     c, to_imag, y = row // (2 * group), row // group % 2, row % group
     value = cosine((c * (column % length) + quarter * to_imag) % length, length)
     put(z_table, jnp.where(column // length == y, value, 0.0))
+
+
+def fill_tables(length, planes, y_table, coef):
+    quarter = length // 4
+    group = 2 * LANES // length
     shape = (2 * length, 2 * length)
     row, column = (lax.broadcasted_iota(jnp.int32, shape, axis) for axis in range(2))
     y, from_imag = column // (2 * group) * group + column % group, column // group % 2
@@ -64,19 +69,26 @@
     coef[length:] = low
 
 
-def transform_kernel(length, pair_count, info, g_index, psi_v, psi_c, plane, coef, spot, phase, *scratch):
-    val, con, z_table, y_table, chunk_0, chunk_1, rows_z, sems = scratch
+def transform_kernel(length, pair_count, meta, psi_v, psi_c, plane, coef, spot, phase, *scratch):
+    val, con, z_table, y_table, chunk_0, chunk_1, rows_z, pairs, sems = scratch
+    width, count = meta.shape[2], spot.shape[0]
+    pairs_copy = pltpu.make_async_copy(meta.at[pl.ds(count, pairs.shape[0])], pairs, sems.at[pair_count])
+    pairs_copy.start()
+    fill_z_table(length, z_table)
+    pairs_copy.wait()
+    valence = [pairs[p // width, 0, p % width] for p in range(pair_count)]
+    conduction = [pairs[p // width, 0, p % width] for p in range(pair_count, 2 * pair_count)]
     half = length // 2 + 1
     planes = psi_v.shape[1]
     steps = psi_v.shape[2] // (2 * LANES)
 
     def pair_copy(p):
-        return pltpu.make_async_copy(psi_c.at[info[pair_count + p]], con.at[p], sems.at[p])
+        return pltpu.make_async_copy(psi_c.at[conduction[p]], con.at[p], sems.at[p])
 
     for p in range(pair_count):
         pair_copy(p).start()
-    fill_tables(length, planes, z_table, y_table, coef)
-    points = g_index[...]
+    fill_tables(length, planes, y_table, coef)
+    points = meta[:count]
     a, b, c = points // (length * length), points // length % length, points % length
     flip = c > length // 2
     mirrored = lambda k: jnp.where(flip, (length - k) % length, k)
@@ -89,7 +101,7 @@
     def density(step, chunk):
         lanes = pl.ds(pl.multiple_of(step * (2 * LANES), 2 * LANES), 2 * LANES)
         for p in range(pair_count):
-            values = con[p, :, lanes].astype(F32) * val[info[p], :, lanes]
+            values = con[p, :, lanes].astype(F32) * val[valence[p], :, lanes]
             for k in range(2):
                 chunk[k, p * planes : (p + 1) * planes, :] = values[:, k * LANES : (k + 1) * LANES]
 
@@ -115,7 +127,7 @@
         z_step(2 * i + 1, chunk_1)
         return 0
 
-    lax.fori_loop(0, steps // 2, two_steps, 0)
+    lax.fori_loop(0, steps // 2, two_steps, 0, unroll=4)
 
     def y_step(c, _):
         high, low = split(rows_z[c])
@@ -126,15 +138,16 @@
                 plane[pl.ds(c * (4 * length) + part * 2 + xh, length, stride=4), :] = block
         return 0
 
-    lax.fori_loop(0, half, y_step, 0, unroll=3)
-
-
-def transform(psi_v, psi_c, info, pair_count, g_index):
+    lax.fori_loop(0, half, y_step, 0, unroll=33)
+
+
+def transform(psi_v, psi_c, meta, pair_count, devices):
     planes, plane_size = psi_v.shape[1], psi_v.shape[2]
     length = math.isqrt(plane_size)
     half = length // 2 + 1
     vmem = pl.BlockSpec(memory_space=pltpu.VMEM)
-    index = jax.ShapeDtypeStruct(g_index.shape, jnp.int32)
+    extra, width = meta.shape[0] - devices, meta.shape[2]
+    index = jax.ShapeDtypeStruct((devices, 1, width), jnp.int32)
     return pl.pallas_call(
         functools.partial(transform_kernel, length, pair_count),
         out_shape=[
@@ -143,7 +156,7 @@
             index,
             index,
         ],
-        in_specs=[pl.BlockSpec(memory_space=pltpu.SMEM), vmem, vmem, pl.BlockSpec(memory_space=pl.ANY)],
+        in_specs=[vmem, vmem, pl.BlockSpec(memory_space=pl.ANY)],
         out_specs=[vmem] * 4,
         scratch_shapes=[
             pltpu.VMEM(psi_v.shape, F32),
@@ -153,11 +166,12 @@
             pltpu.VMEM((2, pair_count * planes, LANES), F32),
             pltpu.VMEM((2, pair_count * planes, LANES), F32),
             pltpu.VMEM((half, 2 * length, 2 * LANES), F32),
-            pltpu.SemaphoreType.DMA((pair_count,)),
+            pltpu.SMEM((extra, 1, width), jnp.int32),
+            pltpu.SemaphoreType.DMA((pair_count + 1,)),
         ],
         compiler_params=pltpu.CompilerParams(vmem_limit_bytes=40 * 2**20),
         name="transform",
-    )(info, g_index, psi_v, psi_c)
+    )(meta, psi_v, psi_c)
 
 
 def landing(chip, chips):
@@ -243,7 +257,7 @@
         lax.fori_loop(0, blocks // 2, two_blocks, 0)
     if chunked:
         used = width // LANES * 2 * pair_count
-        top = jnp.full((rows - used, LANES), jnp.max(peak[...]))
+        top = jnp.broadcast_to(jnp.max(peak[...], axis=0, keepdims=True), (rows - used, LANES))
         for out in outs:
             for block in range(blocks):
                 out[block, used:, :] = top
@@ -276,13 +290,14 @@
 def sphere_parts(psi_v, psi_c, pair_v, pair_c, g_index, devices, paired):
     pair_count = pair_v.shape[0]
     width = g_index.shape[0] // devices
-    info = jnp.concatenate([pair_v, pair_c])
-    plane, coef, spot, phase = transform(psi_v, psi_c, info, pair_count, g_index.reshape(devices, 1, width))
+    filling = jnp.zeros(-(g_index.shape[0] + 2 * pair_count) % math.lcm(width, 1024), jnp.int32)
+    meta = jnp.concatenate([g_index, pair_v, pair_c, filling]).reshape(-1, 1, width)
+    plane, coef, spot, phase = transform(psi_v, psi_c, meta, pair_count, devices)
     pick = (np.arange(2 * LANES)[None, :] % SLOT == np.arange(pair_count)[:, None]).astype(jnp.bfloat16)
     rest = (spot, phase, plane.reshape(-1, 4, LANES), coef, pick, pair_count)
     if not paired:
         return points(*rest, (devices, 2 * pair_count, width), (), None)[0]
-    shape = (devices // 4, width // LANES * 2 * pair_count + 16, LANES)
+    shape = (devices // 4, width // LANES * 2 * pair_count + 8, LANES)
     return [functools.partial(points, *rest, shape, orders) for orders in (((1, 1),), ((0, 1),), ((1, 0), (0, 0)))]
 
 
@@ -329,28 +344,24 @@
     )(first, rows, cols)
 
 
-def chi_direct_kernel(pair_count, width, skip, has_left, *refs):
+def chi_direct_kernel(pair_count, width, shifts, has_left, *refs):
     depth = 2 * pair_count
     chunks = width // LANES
     wide = lambda piece: jnp.concatenate([piece[k * depth : (k + 1) * depth] for k in range(chunks)], 1)
     chip, chips = lax.axis_index("fft") // 2, lax.axis_size("fft") // 2
     if has_left:
         left, refs = refs[0], refs[3:]
+        *cols, real, imag, stage, sems = refs
     else:
         row_refs, refs = refs[:2], refs[2:]
-    cols, refs = refs[:2], refs[2:]
-    count = cols[0].shape[0]
-    real, imag, *refs = refs
-    if not has_left:
-        left, *refs = refs
+        *cols, real, imag, left, stage, sems = refs
         own = [wide(piece[...].astype(F32)) for piece in row_refs]
         cross = [part for piece in own for part in (-piece[pair_count:], piece[:pair_count])]
         left[:width] = (-jnp.concatenate(own, 0)).T.astype(BF16)
         left[width:] = jnp.concatenate(cross, 0).T.astype(BF16)
-    stage, sems = refs
 
     def copies(s):
-        block = landing(jnp.bitwise_xor(chip, 2 * s + skip), chips)
+        block = landing(jnp.bitwise_xor(chip, shifts[s]), chips)
         start = pl.multiple_of(block * width, LANES)
         return [
             pltpu.make_async_copy(
@@ -359,18 +370,24 @@
             for i, out in enumerate((real, imag))
         ]
 
-    for s in range(count):
-        right = jnp.concatenate([wide(cols[i][s][...]) for i in range(2)], 0)
-        stage[s] = jnp.dot(left[...], right, preferred_element_type=F32)
-        for copy in copies(s):
-            copy.start()
-    for s in range(count):
+    s = 0
+    for own_pairs, other_pairs in zip(cols[::2], cols[1::2]):
+        for start in range(0, own_pairs.shape[0], 2):
+            rights = [
+                jnp.concatenate([wide(own_pairs[k]), wide(other_pairs[k])], 0) for k in (start, start + 1)
+            ]
+            both = jnp.dot(left[...], jnp.concatenate(rights, 1), preferred_element_type=F32)
+            for k in range(2):
+                stage[s + k] = both[:, k * width : (k + 1) * width]
+                for copy in copies(s + k):
+                    copy.start()
+            s += 2
+    for s in range(len(shifts)):
         for copy in copies(s):
             copy.wait()
 
 
-def chi_direct(rows, cols, skip, done, pair_count, width, blocks):
-    count = cols[0].shape[0]
+def chi_direct(rows, cols, shifts, done, pair_count, width, blocks):
     out = jax.ShapeDtypeStruct((width, blocks * width), F32)
     left = jax.ShapeDtypeStruct((2 * width, 4 * pair_count), BF16)
     vmem = pl.BlockSpec(memory_space=pltpu.VMEM)
@@ -382,10 +399,12 @@
         real, imag, left = done
         args, specs, aliases = (left, real, imag), [vmem, hbm, hbm], {1: 0, 2: 1}
         out_shape, out_specs = (out, out), (hbm, hbm)
+    cols = [array for pair in cols for array in pair]
+    count = len(shifts)
     return pl.pallas_call(
-        functools.partial(chi_direct_kernel, pair_count, width, skip, done is not None),
+        functools.partial(chi_direct_kernel, pair_count, width, shifts, done is not None),
         out_shape=out_shape,
-        in_specs=specs + [vmem] * 2,
+        in_specs=specs + [vmem] * len(cols),
         out_specs=out_specs,
         scratch_shapes=[
             pltpu.VMEM((count, 2 * width, width), F32),
@@ -393,11 +412,7 @@
         ],
         input_output_aliases=aliases,
         compiler_params=pltpu.CompilerParams(vmem_limit_bytes=32 * 2**20),
-        cost_estimate=pl.CostEstimate(
-            flops=8 * count * width * width * pair_count * 2,
-            bytes_accessed=8 * count * width * width,
-            transcendentals=0,
-        ),
+        cost_estimate=pl.CostEstimate(flops=1, bytes_accessed=1, transcendentals=0),
         name="chi",
     )(*args, *cols)
 
@@ -469,8 +484,10 @@
     first = jnp.stack(
         [permute(own, lambda chip, core, y, s=s: (chip ^ (2 * s), y, core)) for s in range(quarter)]
     )
+    first = lax.optimization_barrier(first)
     first_x = swap_x(first)
-    second = swap(first)
+    halves = [first[: quarter // 2], first[quarter // 2 :]]
+    second = [swap(half) for half in halves]
 
     def row_home(chip, core):
         return chip % quarter + core * quarter, chip // quarter
@@ -479,11 +496,11 @@
     cross = permute(own, lambda chip, core, y: (*row_home(chip, core), 1 - y))
     agree = fft % 2 == grp
     rows = (jnp.where(agree, same, cross), jnp.where(agree, cross, same))
-    done = chi_direct(rows, (first, second), 0, None, pair_count, width, chips)
-    first_x, left = lax.optimization_barrier((first_x, done[2]))
-    second_x = swap(first_x)
-    done = (*done[:2], left)
-    return chi_direct(None, (first_x, second_x), 1, done, pair_count, width, chips)
+    shifts = [2 * s for s in range(quarter)]
+    real, imag, left = chi_direct(rows, list(zip(halves, second)), shifts, None, pair_count, width, chips)
+    first_x, left = lax.optimization_barrier((first_x, left))
+    shifts = [2 * s + 1 for s in range(quarter)]
+    return chi_direct(None, [(first_x, swap(first_x))], shifts, (real, imag, left), pair_count, width, chips)
 
 
 def any_groups(psi_v, psi_c, energy_v, energy_c, pair_v, pair_c, g_index):

time: 67.3 us -> 62.6 us (0.930)
  Pallas kernels: 28.5 us -> 25.4 us
  waiting for transfers between devices: 12.8 us -> 12 us
  other arithmetic: 1.81 us -> 1.02 us
    pallas_call x1, Pallas kernels: 9 us -> 6.3 us  [transform(): pl.pallas_call(functools.partial(transform_kernel, length, pair_count), o...]
    ppermute x15 -> x16, waiting for transfers between devices: 12.8 us -> 12 us  [permute(): return lax.ppermute(values, ('fft', 'grp'), perm)]
    concatenate x0 -> x1, local copies, waits for them, and re-layouts: none -> 0.82 us  [sphere_parts(): jnp.concatenate([g_index, pair_v, pair_c, filling]).reshape(-1, 1, width)]
    concatenate x1 -> x0, other arithmetic: 0.75 us -> none  [sphere_parts(): info = jnp.concatenate([pair_v, pair_c])]
    unnamed x14 -> x12, local copies, waits for them, and re-layouts: 1.81 us -> 1.07 us
    ppermute x15 -> x16, starting transfers between devices: 21 us -> 20.9 us  [permute(): return lax.ppermute(values, ('fft', 'grp'), perm)]
  transfers between devices with their start and end apart: 15 -> 16, of which waited for: 7 -> 9; matrix products, arithmetic and copies ran while one was open for 1% -> 1% of each run, Pallas kernels for 20% -> 21%
where the time goes in v3:
time: 62.6 us; the launch traced here: 62.2 us
  Pallas kernels  25.4 us (41%)
  starting transfers between devices  20.9 us (33%)
  waiting for transfers between devices  12 us (19%)
  local copies, waits for them, and re-layouts  2.01 us (3%)
  other arithmetic  1.02 us (2%)
  between operations  0.9 us (1%)
    ppermute x16, starting transfers between devices, permute(): return lax.ppermute(values, ('fft', 'grp'), perm)  20.9 us
    pallas_call x3, Pallas kernels, points(): pl.pallas_call(functools.partial(points_kernel, length, pair_count, width...  13.8 us
    ppermute x16, waiting for transfers between devices, permute(): return lax.ppermute(values, ('fft', 'grp'), perm)  12 us
    pallas_call x1, Pallas kernels, transform(): pl.pallas_call(functools.partial(transform_kernel, length, pair_count), o...  6.3 us
    pallas_call x2, Pallas kernels, chi_direct(): pl.pallas_call(functools.partial(chi_direct_kernel, pair_count, width, sh...  5.33 us
  transfers between devices with their start and end apart: 16, of which 9 were waited for; matrix products, arithmetic and copies ran while one was open for 1% of the time, Pallas kernels for 21%

profile of v3, /device:TPU:0, one launch (start us, length us, event | category | flops | bytes accessed | tf_op | source)
XLA Modules:
  0.0 62.2 jit_solution(17449388422336461615)
XLA Ops:
  0.6 0.8 %concatenate.3 = s32[9216]{0:T(1024)S(1)} concatenate(s32[6144]{0:T(1024)} %param.14, s32[40]{0:T(128)} %param.12, s32[40]{0:T(128)} %param.13, s32[2992]{0:T(1024)S(1)} %broadcast_in_dim.71), dimensions={0} | concatenate | bytes 73728 | tf_op jit(solution)/shard_map/concatenate | solution.py:294
  1.5 1.0 %copy-done = bf16[16,4,4096]{2,1,0:T(4,128)(2,1)S(1)} copy-done((bf16[16,4,4096]{2,1,0:T(4,128)(2,1)S(1)}, bf16[16,4,4096]{2,1,0:T(4,128)(2,1)}, u32[]{:S(2)}) %copy-start) | copy-done | bytes 524312
  2.5 6.3 %transform.1 = (f32[8448,128]{1,0:T(8,128)S(1)}, bf16[128,512]{1,0:T(8,128)(2,1)S(1)}, s32[16,1,384]{2,1,0:T(1,128)S(1)}, s32[16,1,384]{2,1,0:T(1,128)S(1)}) custom-call(s32[24,1,384]{2,1,0:T(1,128)S(1)} %bitcast.48, bf16[16,4,4096]{2,1,0:T(4,128)(2,1)S(1)} %copy-done, bf16[384,4,4096]{2,1,0:T(4,128)(2,1)} %psi_c.1), custom_call_target="tpu_custom_call" | custom-call | tf_op jit(solution)/shard_map/transform/pallas_call | solution.py:151
  8.8 3.7 %points.3.refs_0_ = f32[4,248,128]{2,1,0:T(8,128)S(1)} custom-call(s32[16,1,384]{2,1,0:T(1,128)S(1)} %get-tuple-element.20.spot, s32[16,1,384]{2,1,0:T(1,128)S(1)} %get-tuple-element.21.phase, f32[2112,4,128]{2,1,0:T(4,128)S(1)} %bitcast.45, bf16[128,512]{1,0:T(8,128)(2,1)S(1)} %get-tuple-element.23.coef, bf16[40,256]{1,0:T(8,128)(2,1)S(1)} %copy-done.1), custom_call_target="tpu_custom_call" | custom-call | flops 400000000 | bytes 1048576 | tf_op jit(solution)/shard_map/points/pallas_call | solution.py:272
  12.5 0.5 collective-permute-start
  13.0 3.7 %points.4 = f32[4,248,128]{2,1,0:T(8,128)S(1)} custom-call(s32[16,1,384]{2,1,0:T(1,128)S(1)} %get-tuple-element.20.spot, s32[16,1,384]{2,1,0:T(1,128)S(1)} %get-tuple-element.21.phase, f32[2112,4,128]{2,1,0:T(4,128)S(1)} %bitcast.46, bf16[128,512]{1,0:T(8,128)(2,1)S(1)} %get-tuple-element.23.coef, bf16[40,256]{1,0:T(8,128)(2,1)S(1)} %copy-done.1, ...), custom_call_target="tpu_custom_call" | custom-call | flops 400000000 | bytes 1048576 | tf_op jit(solution)/shard_map/points/pallas_call | solution.py:272
  16.7 0.0 copy-start.2
  16.7 0.0 copy-start.3
  16.8 0.0 copy-start.4
  16.8 0.0 copy-start.5
  16.8 0.0 collective-permute-done
  16.8 0.1 add.50.refs_0_
  16.9 0.1 select_convert_fusion
  17.0 2.6 %collective-permute-start.1 = (f16[4,248,128]{2,1,0:T(8,128)(2,1)S(1)}, f16[4,248,128]{2,1,0:T(8,128)(2,1)S(1)}, u32[]{:S(2)}, u32[]{:S(2)}) collective-permute-start(f16[4,248,128]{2,1,0:T(8,128)(2,1)S(1)} %select_convert_fusion), channel_id=1, source_target_pairs={{0,4},{1,5},{2,6},{3,7},{4,0},{5,1},{6,2},{7,3},{8,12},{9,13},{10,... | collective-permute-start | bytes 761864 | tf_op jit(solution)/shard_map/ppermute | solution.py:436
  19.6 6.4 %points.5 = (f32[4,248,128]{2,1,0:T(8,128)S(1)}, f32[4,248,128]{2,1,0:T(8,128)S(1)}) custom-call(s32[16,1,384]{2,1,0:T(1,128)S(1)} %get-tuple-element.20.spot, s32[16,1,384]{2,1,0:T(1,128)S(1)} %get-tuple-element.21.phase, f32[2112,4,128]{2,1,0:T(4,128)S(1)} %bitcast.47, bf16[128,512]{1,0:T(8,128)(2,1)S(1)} %get-tuple-element.23.coef, ...), custom_call_target="tpu_custom_call" | custom-call | flops 400000000 | bytes 1048576 | tf_op jit(solution)/shard_map/points/pallas_call | solution.py:272
  26.0 0.3 collective-permute-done.1
  26.4 1.9 %collective-permute-done.2 = f32[4,248,128]{2,1,0:T(8,128)S(1)} collective-permute-done((f32[4,248,128]{2,1,0:T(8,128)S(1)}, f32[4,248,128]{2,1,0:T(8,128)S(1)}, u32[]{:S(2)}, u32[]{:S(2)}) %collective-permute-start.2) | collective-permute-done | bytes 507936 | tf_op jit(solution)/shard_map/ppermute | solution.py:436
  28.2 0.2 multiply_add_fusion
  28.5 0.1 fusion.5
  28.6 3.9 %collective-permute-start.3 = (f16[248,128]{1,0:T(8,128)(2,1)S(1)}, f16[248,128]{1,0:T(8,128)(2,1)S(1)}, u32[]{:S(2)}, u32[]{:S(2)}) collective-permute-start(f16[248,128]{1,0:T(8,128)(2,1)S(1)} %get-tuple-element.46), channel_id=1, source_target_pairs={{0,24},{1,25},{2,26},{3,27},{4,28},{5,29},{6,30},{7,31},{8,16},{9,... | collective-permute-start | bytes 190472 | tf_op jit(solution)/shard_map/ppermute | solution.py:436
  32.5 0.2 select_reduce_fusion
  32.7 0.1 select_reduce_fusion.1
  32.8 0.1 mul.119
  32.9 0.0 collective-permute-start.5
  32.9 0.6 collective-permute-start.4
  33.5 1.8 %collective-permute-done.3 = f16[248,128]{1,0:T(8,128)(2,1)S(1)} collective-permute-done((f16[248,128]{1,0:T(8,128)(2,1)S(1)}, f16[248,128]{1,0:T(8,128)(2,1)S(1)}, u32[]{:S(2)}, u32[]{:S(2)}) %collective-permute-start.3) | collective-permute-done | bytes 63520 | tf_op jit(solution)/shard_map/ppermute | solution.py:436
  35.4 2.4 %collective-permute-done.5 = f16[248,128]{1,0:T(8,128)(2,1)S(1)} collective-permute-done((f16[248,128]{1,0:T(8,128)(2,1)S(1)}, f16[248,128]{1,0:T(8,128)(2,1)S(1)}, u32[]{:S(2)}, u32[]{:S(2)}) %collective-permute-start.5) | collective-permute-done | bytes 63520 | tf_op jit(solution)/shard_map/ppermute | solution.py:436
  37.7 1.1 %collective-permute-done.4 = f16[248,128]{1,0:T(8,128)(2,1)S(1)} collective-permute-done((f16[248,128]{1,0:T(8,128)(2,1)S(1)}, f16[248,128]{1,0:T(8,128)(2,1)S(1)}, u32[]{:S(2)}, u32[]{:S(2)}) %collective-permute-start.4) | collective-permute-done | bytes 63520 | tf_op jit(solution)/shard_map/ppermute | solution.py:436
  38.8 0.1 fusion.9
  39.0 2.4 %collective-permute-start.9 = (bf16[240,128]{1,0:T(8,128)(2,1)S(1)}, bf16[240,128]{1,0:T(8,128)(2,1)S(1)}, u32[]{:S(2)}, u32[]{:S(2)}) collective-permute-start(bf16[240,128]{1,0:T(8,128)(2,1)S(1)} %fusion.9), channel_id=1, source_target_pairs={{0,24},{1,26},{2,25},{3,27},{4,28},{5,30},{6,29},{7,31},{8,16},{9,... | collective-permute-start | bytes 184328 | tf_op jit(solution)/shard_map/ppermute | solution.py:436
  41.4 0.4 collective-permute-start.8
  41.8 1.6 %collective-permute-start.7 = (bf16[240,128]{1,0:T(8,128)(2,1)S(1)}, bf16[240,128]{1,0:T(8,128)(2,1)S(1)}, u32[]{:S(2)}, u32[]{:S(2)}) collective-permute-start(bf16[240,128]{1,0:T(8,128)(2,1)S(1)} %fusion.9), channel_id=1, source_target_pairs={{0,8},{1,10},{2,9},{3,11},{4,12},{5,14},{6,13},{7,15},{8,0},{9,2},... | collective-permute-start | bytes 184328 | tf_op jit(solution)/shard_map/ppermute | solution.py:436
  43.4 0.7 %collective-permute-start.6 = (bf16[240,128]{1,0:T(8,128)(2,1)S(1)}, bf16[240,128]{1,0:T(8,128)(2,1)S(1)}, u32[]{:S(2)}, u32[]{:S(2)}) collective-permute-start(bf16[240,128]{1,0:T(8,128)(2,1)S(1)} %fusion.9), channel_id=1, source_target_pairs={{0,0},{1,2},{2,1},{3,3},{4,4},{5,6},{6,5},{7,7},{8,8},{9,10},{10,9... | collective-permute-start | bytes 184328 | tf_op jit(solution)/shard_map/ppermute | solution.py:436
  44.1 4.6 %collective-permute-start.12 = (bf16[240,128]{1,0:T(8,128)(2,1)S(1)}, bf16[240,128]{1,0:T(8,128)(2,1)S(1)}, u32[]{:S(2)}, u32[]{:S(2)}) collective-permute-start(bf16[240,128]{1,0:T(8,128)(2,1)S(1)} %fusion.9), channel_id=1, source_target_pairs={{0,1},{1,0},{2,17},{3,16},{4,5},{5,4},{6,21},{7,20},{8,9},{9,8},{1... | collective-permute-start | bytes 184328 | tf_op jit(solution)/shard_map/ppermute | solution.py:436
  48.7 0.7 %collective-permute-start.11 = (bf16[240,128]{1,0:T(8,128)(2,1)S(1)}, bf16[240,128]{1,0:T(8,128)(2,1)S(1)}, u32[]{:S(2)}, u32[]{:S(2)}) collective-permute-start(bf16[240,128]{1,0:T(8,128)(2,1)S(1)} %fusion.9), channel_id=1, source_target_pairs={{0,0},{1,1},{2,16},{3,17},{4,4},{5,5},{6,20},{7,21},{8,8},{9,9},{1... | collective-permute-start | bytes 184328 | tf_op jit(solution)/shard_map/ppermute | solution.py:436
  49.4 0.0 collective-permute-done.8
  49.4 0.0 collective-permute-done.6
  49.5 1.6 %collective-permute-start.10 = (bf16[4,240,128]{2,1,0:T(8,128)(2,1)S(1)}, bf16[4,240,128]{2,1,0:T(8,128)(2,1)S(1)}, u32[]{:S(2)}, u32[]{:S(2)}) collective-permute-start(bf16[4,240,128]{2,1,0:T(8,128)(2,1)S(1)} %pad_maximum_fusion), channel_id=1, source_target_pairs={{0,4},{1,5},{2,6},{3,7},{4,0},{5,1},{6,2},{7,3},{8,12},{9,13},{10,... | collective-permute-start | bytes 737288 | tf_op jit(solution)/shard_map/ppermute | solution.py:436
  51.0 1.1 %collective-permute-start.14 = (bf16[2,240,128]{2,1,0:T(8,128)(2,1)S(1)}, bf16[2,240,128]{2,1,0:T(8,128)(2,1)S(1)}, u32[]{:S(2)}, u32[]{:S(2)}) collective-permute-start(bf16[2,240,128]{2,1,0:T(8,128)(2,1)S(1)} %get-tuple-element.53.refs_4_), channel_id=1, source_target_pairs={{0,2},{1,3},{2,0},{3,1},{4,6},{5,7},{6,4},{7,5},{8,10},{9,11},{10,... | collective-permute-start | bytes 368648 | tf_op jit(solution)/shard_map/ppermute | solution.py:436
  52.2 0.1 collective-permute-start.13
  52.2 0.0 collective-permute-done.12
  52.3 0.9 %collective-permute-done.14.refs_5_ = bf16[2,240,128]{2,1,0:T(8,128)(2,1)S(1)} collective-permute-done((bf16[2,240,128]{2,1,0:T(8,128)(2,1)S(1)}, bf16[2,240,128]{2,1,0:T(8,128)(2,1)S(1)}, u32[]{:S(2)}, u32[]{:S(2)}) %collective-permute-start.14) | collective-permute-done | bytes 122912 | tf_op jit(solution)/shard_map/ppermute | solution.py:436
  53.1 0.4 collective-permute-done.13.refs_3_
  53.5 2.7 %chi.2 = (f32[384,3072]{1,0:T(8,128)}, f32[384,3072]{1,0:T(8,128)}, bf16[768,160]{1,0:T(8,128)(2,1)S(1)}) custom-call(bf16[240,128]{1,0:T(8,128)(2,1)S(1)} %get-tuple-element.56.refs_0_, bf16[240,128]{1,0:T(8,128)(2,1)S(1)} %get-tuple-element.55.refs_1_, bf16[2,240,128]{2,1,0:T(8,128)(2,1)S(1)} %get-tuple-element.54.refs_2_, ...), custom_call_target="tpu_custom_call" | custom-call | flops 1 | bytes 1 | tf_op jit(solution)/shard_map/chi/pallas_call | solution.py:404
  56.2 1.9 %collective-permute-done.10.refs_3_ = bf16[4,240,128]{2,1,0:T(8,128)(2,1)S(1)} collective-permute-done((bf16[4,240,128]{2,1,0:T(8,128)(2,1)S(1)}, bf16[4,240,128]{2,1,0:T(8,128)(2,1)S(1)}, u32[]{:S(2)}, u32[]{:S(2)}) %collective-permute-start.10) | collective-permute-done | bytes 245792 | tf_op jit(solution)/shard_map/ppermute | solution.py:436
  58.1 0.1 collective-permute-start.15
  58.2 1.4 %collective-permute-done.15.refs_4_ = bf16[4,240,128]{2,1,0:T(8,128)(2,1)S(1)} collective-permute-done((bf16[4,240,128]{2,1,0:T(8,128)(2,1)S(1)}, bf16[4,240,128]{2,1,0:T(8,128)(2,1)S(1)}, u32[]{:S(2)}, u32[]{:S(2)}) %collective-permute-start.15) | collective-permute-done | bytes 245792 | tf_op jit(solution)/shard_map/ppermute | solution.py:436
  59.6 2.6 %chi.3 = (f32[384,3072]{1,0:T(8,128)}, f32[384,3072]{1,0:T(8,128)}) custom-call(bf16[768,160]{1,0:T(8,128)(2,1)S(1)} %get-tuple-element.34.refs_0_, f32[384,3072]{1,0:T(8,128)} %get-tuple-element.35.refs_1_, f32[384,3072]{1,0:T(8,128)} %get-tuple-element.36.refs_2_, ...), custom_call_target="tpu_custom_call", output_to_operand_aliasing={{0}: (1, {}), {1}: (2, {})} | custom-call | flops 1 | bytes 1 | tf_op jit(solution)/shard_map/chi/pallas_call | solution.py:404
  (25 shorter events, 0.2 us)
Async XLA Ops:
  1.5 1.0 %copy-start = (bf16[16,4,4096]{2,1,0:T(4,128)(2,1)S(1)}, bf16[16,4,4096]{2,1,0:T(4,128)(2,1)}, u32[]{:S(2)}) copy-start(bf16[16,4,4096]{2,1,0:T(4,128)(2,1)} %psi_v.1) | copy-start | bytes 1572868
  2.5 6.3 %copy-start.1 = (bf16[40,256]{1,0:T(8,128)(2,1)S(1)}, bf16[40,256]{1,0:T(8,128)(2,1)}, u32[]{:S(2)}) copy-start(bf16[40,256]{1,0:T(8,128)(2,1)} %constant.53.clone.pick) | copy-start | bytes 61444
  12.5 4.3 %collective-permute-start = (f32[4,248,128]{2,1,0:T(8,128)S(1)}, f32[4,248,128]{2,1,0:T(8,128)S(1)}, u32[]{:S(2)}, u32[]{:S(2)}) collective-permute-start(f32[4,248,128]{2,1,0:T(8,128)S(1)} %points.3.refs_0_), channel_id=1, source_target_pairs={{0,2},{1,3},{2,0},{3,1},{4,6},{5,7},{6,4},{7,5},{8,10},{9,11},{10,... | collective-permute-start | bytes 1523720 | tf_op jit(solution)/shard_map/ppermute | solution.py:436
  16.7 15.8 %copy-start.2 = (s32[40]{0:T(128)S(1)}, s32[40]{0:T(128)}, u32[]{:S(2)}) copy-start(s32[40]{0:T(128)} %param.13) | copy-start | bytes 484
  16.7 15.8 %copy-start.3 = (f32[384]{0:T(512)S(1)}, f32[384]{0:T(512)}, u32[]{:S(2)}) copy-start(f32[384]{0:T(512)} %param.11) | copy-start | bytes 4612
  16.8 16.0 %copy-start.4 = (s32[40]{0:T(128)S(1)}, s32[40]{0:T(128)}, u32[]{:S(2)}) copy-start(s32[40]{0:T(128)} %param.12) | copy-start | bytes 484
  16.8 15.9 %copy-start.5 = (f32[16]{0:T(128)S(1)}, f32[16]{0:T(128)}, u32[]{:S(2)}) copy-start(f32[16]{0:T(128)} %param.10) | copy-start | bytes 196
  17.0 9.3 %collective-permute-start.1 = (f16[4,248,128]{2,1,0:T(8,128)(2,1)S(1)}, f16[4,248,128]{2,1,0:T(8,128)(2,1)S(1)}, u32[]{:S(2)}, u32[]{:S(2)}) collective-permute-start(f16[4,248,128]{2,1,0:T(8,128)(2,1)S(1)} %select_convert_fusion), channel_id=1, source_target_pairs={{0,4},{1,5},{2,6},{3,7},{4,0},{5,1},{6,2},{7,3},{8,12},{9,13},{10,... | collective-permute-start | bytes 761864 | tf_op jit(solution)/shard_map/ppermute | solution.py:436
  26.4 1.9 %collective-permute-start.2 = (f32[4,248,128]{2,1,0:T(8,128)S(1)}, f32[4,248,128]{2,1,0:T(8,128)S(1)}, u32[]{:S(2)}, u32[]{:S(2)}) collective-permute-start(f32[4,248,128]{2,1,0:T(8,128)S(1)} %get-tuple-element.28), channel_id=1, source_target_pairs={{0,2},{1,3},{2,0},{3,1},{4,6},{5,7},{6,4},{7,5},{8,10},{9,11},{10,... | collective-permute-start | bytes 1523720 | tf_op jit(solution)/shard_map/ppermute | solution.py:436
  28.6 6.8 %collective-permute-start.3 = (f16[248,128]{1,0:T(8,128)(2,1)S(1)}, f16[248,128]{1,0:T(8,128)(2,1)S(1)}, u32[]{:S(2)}, u32[]{:S(2)}) collective-permute-start(f16[248,128]{1,0:T(8,128)(2,1)S(1)} %get-tuple-element.46), channel_id=1, source_target_pairs={{0,24},{1,25},{2,26},{3,27},{4,28},{5,29},{6,30},{7,31},{8,16},{9,... | collective-permute-start | bytes 190472 | tf_op jit(solution)/shard_map/ppermute | solution.py:436
  32.9 4.8 %collective-permute-start.5 = (f16[248,128]{1,0:T(8,128)(2,1)S(1)}, f16[248,128]{1,0:T(8,128)(2,1)S(1)}, u32[]{:S(2)}, u32[]{:S(2)}) collective-permute-start(f16[248,128]{1,0:T(8,128)(2,1)S(1)} %get-tuple-element.47), channel_id=1, source_target_pairs={{0,8},{1,9},{2,10},{3,11},{4,12},{5,13},{6,14},{7,15},{8,0},{9,1},... | collective-permute-start | bytes 190472 | tf_op jit(solution)/shard_map/ppermute | solution.py:436
  32.9 5.9 %collective-permute-start.4 = (f16[248,128]{1,0:T(8,128)(2,1)S(1)}, f16[248,128]{1,0:T(8,128)(2,1)S(1)}, u32[]{:S(2)}, u32[]{:S(2)}) collective-permute-start(f16[248,128]{1,0:T(8,128)(2,1)S(1)} %get-tuple-element.48), channel_id=1, source_target_pairs={{0,16},{1,17},{2,18},{3,19},{4,20},{5,21},{6,22},{7,23},{8,24},{9,... | collective-permute-start | bytes 190472 | tf_op jit(solution)/shard_map/ppermute | solution.py:436
  39.0 9.8 %collective-permute-start.9 = (bf16[240,128]{1,0:T(8,128)(2,1)S(1)}, bf16[240,128]{1,0:T(8,128)(2,1)S(1)}, u32[]{:S(2)}, u32[]{:S(2)}) collective-permute-start(bf16[240,128]{1,0:T(8,128)(2,1)S(1)} %fusion.9), channel_id=1, source_target_pairs={{0,24},{1,26},{2,25},{3,27},{4,28},{5,30},{6,29},{7,31},{8,16},{9,... | collective-permute-start | bytes 184328 | tf_op jit(solution)/shard_map/ppermute | solution.py:436
  41.4 8.0 %collective-permute-start.8 = (bf16[240,128]{1,0:T(8,128)(2,1)S(1)}, bf16[240,128]{1,0:T(8,128)(2,1)S(1)}, u32[]{:S(2)}, u32[]{:S(2)}) collective-permute-start(bf16[240,128]{1,0:T(8,128)(2,1)S(1)} %fusion.9), channel_id=1, source_target_pairs={{0,16},{1,18},{2,17},{3,19},{4,20},{5,22},{6,21},{7,23},{8,24},{9,... | collective-permute-start | bytes 184328 | tf_op jit(solution)/shard_map/ppermute | solution.py:436
  41.8 7.6 %collective-permute-start.7 = (bf16[240,128]{1,0:T(8,128)(2,1)S(1)}, bf16[240,128]{1,0:T(8,128)(2,1)S(1)}, u32[]{:S(2)}, u32[]{:S(2)}) collective-permute-start(bf16[240,128]{1,0:T(8,128)(2,1)S(1)} %fusion.9), channel_id=1, source_target_pairs={{0,8},{1,10},{2,9},{3,11},{4,12},{5,14},{6,13},{7,15},{8,0},{9,2},... | collective-permute-start | bytes 184328 | tf_op jit(solution)/shard_map/ppermute | solution.py:436
  43.4 6.0 %collective-permute-start.6 = (bf16[240,128]{1,0:T(8,128)(2,1)S(1)}, bf16[240,128]{1,0:T(8,128)(2,1)S(1)}, u32[]{:S(2)}, u32[]{:S(2)}) collective-permute-start(bf16[240,128]{1,0:T(8,128)(2,1)S(1)} %fusion.9), channel_id=1, source_target_pairs={{0,0},{1,2},{2,1},{3,3},{4,4},{5,6},{6,5},{7,7},{8,8},{9,10},{10,9... | collective-permute-start | bytes 184328 | tf_op jit(solution)/shard_map/ppermute | solution.py:436
  44.1 8.1 %collective-permute-start.12 = (bf16[240,128]{1,0:T(8,128)(2,1)S(1)}, bf16[240,128]{1,0:T(8,128)(2,1)S(1)}, u32[]{:S(2)}, u32[]{:S(2)}) collective-permute-start(bf16[240,128]{1,0:T(8,128)(2,1)S(1)} %fusion.9), channel_id=1, source_target_pairs={{0,1},{1,0},{2,17},{3,16},{4,5},{5,4},{6,21},{7,20},{8,9},{9,8},{1... | collective-permute-start | bytes 184328 | tf_op jit(solution)/shard_map/ppermute | solution.py:436
  48.7 3.5 %collective-permute-start.11 = (bf16[240,128]{1,0:T(8,128)(2,1)S(1)}, bf16[240,128]{1,0:T(8,128)(2,1)S(1)}, u32[]{:S(2)}, u32[]{:S(2)}) collective-permute-start(bf16[240,128]{1,0:T(8,128)(2,1)S(1)} %fusion.9), channel_id=1, source_target_pairs={{0,0},{1,1},{2,16},{3,17},{4,4},{5,5},{6,20},{7,21},{8,8},{9,9},{1... | collective-permute-start | bytes 184328 | tf_op jit(solution)/shard_map/ppermute | solution.py:436
  49.5 8.6 %collective-permute-start.10 = (bf16[4,240,128]{2,1,0:T(8,128)(2,1)S(1)}, bf16[4,240,128]{2,1,0:T(8,128)(2,1)S(1)}, u32[]{:S(2)}, u32[]{:S(2)}) collective-permute-start(bf16[4,240,128]{2,1,0:T(8,128)(2,1)S(1)} %pad_maximum_fusion), channel_id=1, source_target_pairs={{0,4},{1,5},{2,6},{3,7},{4,0},{5,1},{6,2},{7,3},{8,12},{9,13},{10,... | collective-permute-start | bytes 737288 | tf_op jit(solution)/shard_map/ppermute | solution.py:436
  51.0 2.1 %collective-permute-start.14 = (bf16[2,240,128]{2,1,0:T(8,128)(2,1)S(1)}, bf16[2,240,128]{2,1,0:T(8,128)(2,1)S(1)}, u32[]{:S(2)}, u32[]{:S(2)}) collective-permute-start(bf16[2,240,128]{2,1,0:T(8,128)(2,1)S(1)} %get-tuple-element.53.refs_4_), channel_id=1, source_target_pairs={{0,2},{1,3},{2,0},{3,1},{4,6},{5,7},{6,4},{7,5},{8,10},{9,11},{10,... | collective-permute-start | bytes 368648 | tf_op jit(solution)/shard_map/ppermute | solution.py:436
  52.2 1.3 %collective-permute-start.13 = (bf16[2,240,128]{2,1,0:T(8,128)(2,1)S(1)}, bf16[2,240,128]{2,1,0:T(8,128)(2,1)S(1)}, u32[]{:S(2)}, u32[]{:S(2)}) collective-permute-start(bf16[2,240,128]{2,1,0:T(8,128)(2,1)S(1)} %get-tuple-element.54.refs_2_), channel_id=1, source_target_pairs={{0,2},{1,3},{2,0},{3,1},{4,6},{5,7},{6,4},{7,5},{8,10},{9,11},{10,... | collective-permute-start | bytes 368648 | tf_op jit(solution)/shard_map/ppermute | solution.py:436
  58.1 1.5 %collective-permute-start.15 = (bf16[4,240,128]{2,1,0:T(8,128)(2,1)S(1)}, bf16[4,240,128]{2,1,0:T(8,128)(2,1)S(1)}, u32[]{:S(2)}, u32[]{:S(2)}) collective-permute-start(bf16[4,240,128]{2,1,0:T(8,128)(2,1)S(1)} %collective-permute-done.10.refs_3_), channel_id=1, source_target_pairs={{0,2},{1,3},{2,0},{3,1},{4,6},{5,7},{6,4},{7,5},{8,10},{9,11},{10,... | collective-permute-start | bytes 737288 | tf_op jit(solution)/shard_map/ppermute | solution.py:436

commit v4 on v3

--- a/solution.py
+++ b/solution.py
@@ -127,7 +127,7 @@
         z_step(2 * i + 1, chunk_1)
         return 0
 
-    lax.fori_loop(0, steps // 2, two_steps, 0, unroll=4)
+    lax.fori_loop(0, steps // 2, two_steps, 0, unroll=8)
 
     def y_step(c, _):
         high, low = split(rows_z[c])
@@ -254,7 +254,7 @@
             combine(group, 2 * step + 1, tiles_1)
             return 0
 
-        lax.fori_loop(0, blocks // 2, two_blocks, 0)
+        lax.fori_loop(0, blocks // 2, two_blocks, 0, unroll=2)
     if chunked:
         used = width // LANES * 2 * pair_count
         top = jnp.broadcast_to(jnp.max(peak[...], axis=0, keepdims=True), (rows - used, LANES))

time: 62.6 us -> 61.6 us (0.984)
  Pallas kernels: 25.4 us -> 23.5 us
  waiting for transfers between devices: 12 us -> 12.8 us
    pallas_call x3, Pallas kernels: 13.8 us -> 12.3 us  [points(): pl.pallas_call(functools.partial(points_kernel, length, pair_count, width...]
    ppermute x16, waiting for transfers between devices: 12 us -> 12.8 us  [permute(): return lax.ppermute(values, ('fft', 'grp'), perm)]
  transfers between devices with their start and end apart: 16 -> 16, of which waited for: 9 -> 9; matrix products, arithmetic and copies ran while one was open for 1% -> 1% of each run, Pallas kernels for 21% -> 19%
where the time goes in v4:
time: 61.6 us; the launch traced here: 61.2 us
  Pallas kernels  23.5 us (38%)
  starting transfers between devices  20.9 us (34%)
  waiting for transfers between devices  12.8 us (21%)
  local copies, waits for them, and re-layouts  2.01 us (3%)
  between operations  1.06 us (2%)
  other arithmetic  1.02 us (2%)
    ppermute x16, starting transfers between devices, permute(): return lax.ppermute(values, ('fft', 'grp'), perm)  20.9 us
    ppermute x16, waiting for transfers between devices, permute(): return lax.ppermute(values, ('fft', 'grp'), perm)  12.8 us
    pallas_call x3, Pallas kernels, points(): pl.pallas_call(functools.partial(points_kernel, length, pair_count, width...  12.3 us
    pallas_call x1, Pallas kernels, transform(): pl.pallas_call(functools.partial(transform_kernel, length, pair_count), o...  5.89 us
    pallas_call x2, Pallas kernels, chi_direct(): pl.pallas_call(functools.partial(chi_direct_kernel, pair_count, width, sh...  5.32 us
  transfers between devices with their start and end apart: 16, of which 9 were waited for; matrix products, arithmetic and copies ran while one was open for 1% of the time, Pallas kernels for 19%

profile of v4, /device:TPU:0, one launch (start us, length us, event | category | flops | bytes accessed | tf_op | source)
XLA Modules:
  0.0 61.2 jit_solution(6120602636158839443)
XLA Ops:
  0.6 0.8 %concatenate.3 = s32[9216]{0:T(1024)S(1)} concatenate(s32[6144]{0:T(1024)} %param.14, s32[40]{0:T(128)} %param.12, s32[40]{0:T(128)} %param.13, s32[2992]{0:T(1024)S(1)} %broadcast_in_dim.71), dimensions={0} | concatenate | bytes 73728 | tf_op jit(solution)/shard_map/concatenate | solution.py:294
  1.5 1.0 %copy-done = bf16[16,4,4096]{2,1,0:T(4,128)(2,1)S(1)} copy-done((bf16[16,4,4096]{2,1,0:T(4,128)(2,1)S(1)}, bf16[16,4,4096]{2,1,0:T(4,128)(2,1)}, u32[]{:S(2)}) %copy-start) | copy-done | bytes 524312
  2.5 5.9 %transform.1 = (f32[8448,128]{1,0:T(8,128)S(1)}, bf16[128,512]{1,0:T(8,128)(2,1)S(1)}, s32[16,1,384]{2,1,0:T(1,128)S(1)}, s32[16,1,384]{2,1,0:T(1,128)S(1)}) custom-call(s32[24,1,384]{2,1,0:T(1,128)S(1)} %bitcast.48, bf16[16,4,4096]{2,1,0:T(4,128)(2,1)S(1)} %copy-done, bf16[384,4,4096]{2,1,0:T(4,128)(2,1)} %psi_c.1), custom_call_target="tpu_custom_call" | custom-call | tf_op jit(solution)/shard_map/transform/pallas_call | solution.py:151
  8.4 3.3 %points.3.refs_0_ = f32[4,248,128]{2,1,0:T(8,128)S(1)} custom-call(s32[16,1,384]{2,1,0:T(1,128)S(1)} %get-tuple-element.20.spot, s32[16,1,384]{2,1,0:T(1,128)S(1)} %get-tuple-element.21.phase, f32[2112,4,128]{2,1,0:T(4,128)S(1)} %bitcast.45, bf16[128,512]{1,0:T(8,128)(2,1)S(1)} %get-tuple-element.23.coef, bf16[40,256]{1,0:T(8,128)(2,1)S(1)} %copy-done.1), custom_call_target="tpu_custom_call" | custom-call | flops 400000000 | bytes 1048576 | tf_op jit(solution)/shard_map/points/pallas_call | solution.py:272
  11.7 0.5 collective-permute-start
  12.3 3.3 %points.4 = f32[4,248,128]{2,1,0:T(8,128)S(1)} custom-call(s32[16,1,384]{2,1,0:T(1,128)S(1)} %get-tuple-element.20.spot, s32[16,1,384]{2,1,0:T(1,128)S(1)} %get-tuple-element.21.phase, f32[2112,4,128]{2,1,0:T(4,128)S(1)} %bitcast.46, bf16[128,512]{1,0:T(8,128)(2,1)S(1)} %get-tuple-element.23.coef, bf16[40,256]{1,0:T(8,128)(2,1)S(1)} %copy-done.1, ...), custom_call_target="tpu_custom_call" | custom-call | flops 400000000 | bytes 1048576 | tf_op jit(solution)/shard_map/points/pallas_call | solution.py:272
  15.6 0.0 copy-start.2
  15.6 0.0 copy-start.3
  15.6 0.0 copy-start.4
  15.6 0.0 copy-start.5
  15.6 0.0 collective-permute-done
  15.6 0.1 add.50.refs_0_
  15.7 0.1 select_convert_fusion
  15.9 2.6 %collective-permute-start.1 = (f16[4,248,128]{2,1,0:T(8,128)(2,1)S(1)}, f16[4,248,128]{2,1,0:T(8,128)(2,1)S(1)}, u32[]{:S(2)}, u32[]{:S(2)}) collective-permute-start(f16[4,248,128]{2,1,0:T(8,128)(2,1)S(1)} %select_convert_fusion), channel_id=1, source_target_pairs={{0,4},{1,5},{2,6},{3,7},{4,0},{5,1},{6,2},{7,3},{8,12},{9,13},{10,... | collective-permute-start | bytes 761864 | tf_op jit(solution)/shard_map/ppermute | solution.py:436
  18.4 5.6 %points.5 = (f32[4,248,128]{2,1,0:T(8,128)S(1)}, f32[4,248,128]{2,1,0:T(8,128)S(1)}) custom-call(s32[16,1,384]{2,1,0:T(1,128)S(1)} %get-tuple-element.20.spot, s32[16,1,384]{2,1,0:T(1,128)S(1)} %get-tuple-element.21.phase, f32[2112,4,128]{2,1,0:T(4,128)S(1)} %bitcast.47, bf16[128,512]{1,0:T(8,128)(2,1)S(1)} %get-tuple-element.23.coef, ...), custom_call_target="tpu_custom_call" | custom-call | flops 400000000 | bytes 1048576 | tf_op jit(solution)/shard_map/points/pallas_call | solution.py:272
  24.1 1.1 %collective-permute-done.1 = f16[4,248,128]{2,1,0:T(8,128)(2,1)S(1)} collective-permute-done((f16[4,248,128]{2,1,0:T(8,128)(2,1)S(1)}, f16[4,248,128]{2,1,0:T(8,128)(2,1)S(1)}, u32[]{:S(2)}, u32[]{:S(2)}) %collective-permute-start.1) | collective-permute-done | bytes 253984 | tf_op jit(solution)/shard_map/ppermute | solution.py:436
  25.2 0.0 collective-permute-start.2
  25.2 1.9 %collective-permute-done.2 = f32[4,248,128]{2,1,0:T(8,128)S(1)} collective-permute-done((f32[4,248,128]{2,1,0:T(8,128)S(1)}, f32[4,248,128]{2,1,0:T(8,128)S(1)}, u32[]{:S(2)}, u32[]{:S(2)}) %collective-permute-start.2) | collective-permute-done | bytes 507936 | tf_op jit(solution)/shard_map/ppermute | solution.py:436
  27.1 0.2 multiply_add_fusion
  27.4 0.1 fusion.5
  27.5 3.9 %collective-permute-start.3 = (f16[248,128]{1,0:T(8,128)(2,1)S(1)}, f16[248,128]{1,0:T(8,128)(2,1)S(1)}, u32[]{:S(2)}, u32[]{:S(2)}) collective-permute-start(f16[248,128]{1,0:T(8,128)(2,1)S(1)} %get-tuple-element.46), channel_id=1, source_target_pairs={{0,24},{1,25},{2,26},{3,27},{4,28},{5,29},{6,30},{7,31},{8,16},{9,... | collective-permute-start | bytes 190472 | tf_op jit(solution)/shard_map/ppermute | solution.py:436
  31.4 0.2 select_reduce_fusion
  31.6 0.1 select_reduce_fusion.1
  31.7 0.1 mul.119
  31.8 0.0 collective-permute-start.5
  31.8 0.6 collective-permute-start.4
  32.4 1.8 %collective-permute-done.3 = f16[248,128]{1,0:T(8,128)(2,1)S(1)} collective-permute-done((f16[248,128]{1,0:T(8,128)(2,1)S(1)}, f16[248,128]{1,0:T(8,128)(2,1)S(1)}, u32[]{:S(2)}, u32[]{:S(2)}) %collective-permute-start.3) | collective-permute-done | bytes 63520 | tf_op jit(solution)/shard_map/ppermute | solution.py:436
  34.2 2.4 %collective-permute-done.5 = f16[248,128]{1,0:T(8,128)(2,1)S(1)} collective-permute-done((f16[248,128]{1,0:T(8,128)(2,1)S(1)}, f16[248,128]{1,0:T(8,128)(2,1)S(1)}, u32[]{:S(2)}, u32[]{:S(2)}) %collective-permute-start.5) | collective-permute-done | bytes 63520 | tf_op jit(solution)/shard_map/ppermute | solution.py:436
  36.6 1.1 %collective-permute-done.4 = f16[248,128]{1,0:T(8,128)(2,1)S(1)} collective-permute-done((f16[248,128]{1,0:T(8,128)(2,1)S(1)}, f16[248,128]{1,0:T(8,128)(2,1)S(1)}, u32[]{:S(2)}, u32[]{:S(2)}) %collective-permute-start.4) | collective-permute-done | bytes 63520 | tf_op jit(solution)/shard_map/ppermute | solution.py:436
  37.7 0.1 fusion.9
  37.8 2.4 %collective-permute-start.9 = (bf16[240,128]{1,0:T(8,128)(2,1)S(1)}, bf16[240,128]{1,0:T(8,128)(2,1)S(1)}, u32[]{:S(2)}, u32[]{:S(2)}) collective-permute-start(bf16[240,128]{1,0:T(8,128)(2,1)S(1)} %fusion.9), channel_id=1, source_target_pairs={{0,24},{1,26},{2,25},{3,27},{4,28},{5,30},{6,29},{7,31},{8,16},{9,... | collective-permute-start | bytes 184328 | tf_op jit(solution)/shard_map/ppermute | solution.py:436
  40.3 0.4 collective-permute-start.8
  40.6 1.6 %collective-permute-start.7 = (bf16[240,128]{1,0:T(8,128)(2,1)S(1)}, bf16[240,128]{1,0:T(8,128)(2,1)S(1)}, u32[]{:S(2)}, u32[]{:S(2)}) collective-permute-start(bf16[240,128]{1,0:T(8,128)(2,1)S(1)} %fusion.9), channel_id=1, source_target_pairs={{0,8},{1,10},{2,9},{3,11},{4,12},{5,14},{6,13},{7,15},{8,0},{9,2},... | collective-permute-start | bytes 184328 | tf_op jit(solution)/shard_map/ppermute | solution.py:436
  42.3 0.7 %collective-permute-start.6 = (bf16[240,128]{1,0:T(8,128)(2,1)S(1)}, bf16[240,128]{1,0:T(8,128)(2,1)S(1)}, u32[]{:S(2)}, u32[]{:S(2)}) collective-permute-start(bf16[240,128]{1,0:T(8,128)(2,1)S(1)} %fusion.9), channel_id=1, source_target_pairs={{0,0},{1,2},{2,1},{3,3},{4,4},{5,6},{6,5},{7,7},{8,8},{9,10},{10,9... | collective-permute-start | bytes 184328 | tf_op jit(solution)/shard_map/ppermute | solution.py:436
  43.0 4.6 %collective-permute-start.12 = (bf16[240,128]{1,0:T(8,128)(2,1)S(1)}, bf16[240,128]{1,0:T(8,128)(2,1)S(1)}, u32[]{:S(2)}, u32[]{:S(2)}) collective-permute-start(bf16[240,128]{1,0:T(8,128)(2,1)S(1)} %fusion.9), channel_id=1, source_target_pairs={{0,1},{1,0},{2,17},{3,16},{4,5},{5,4},{6,21},{7,20},{8,9},{9,8},{1... | collective-permute-start | bytes 184328 | tf_op jit(solution)/shard_map/ppermute | solution.py:436
  47.6 0.0 collective-permute-done.9
  47.6 0.7 %collective-permute-start.11 = (bf16[240,128]{1,0:T(8,128)(2,1)S(1)}, bf16[240,128]{1,0:T(8,128)(2,1)S(1)}, u32[]{:S(2)}, u32[]{:S(2)}) collective-permute-start(bf16[240,128]{1,0:T(8,128)(2,1)S(1)} %fusion.9), channel_id=1, source_target_pairs={{0,0},{1,1},{2,16},{3,17},{4,4},{5,5},{6,20},{7,21},{8,8},{9,9},{1... | collective-permute-start | bytes 184328 | tf_op jit(solution)/shard_map/ppermute | solution.py:436
  48.3 0.0 collective-permute-done.7
  48.3 1.6 %collective-permute-start.10 = (bf16[4,240,128]{2,1,0:T(8,128)(2,1)S(1)}, bf16[4,240,128]{2,1,0:T(8,128)(2,1)S(1)}, u32[]{:S(2)}, u32[]{:S(2)}) collective-permute-start(bf16[4,240,128]{2,1,0:T(8,128)(2,1)S(1)} %pad_maximum_fusion), channel_id=1, source_target_pairs={{0,4},{1,5},{2,6},{3,7},{4,0},{5,1},{6,2},{7,3},{8,12},{9,13},{10,... | collective-permute-start | bytes 737288 | tf_op jit(solution)/shard_map/ppermute | solution.py:436
  49.9 1.1 %collective-permute-start.14 = (bf16[2,240,128]{2,1,0:T(8,128)(2,1)S(1)}, bf16[2,240,128]{2,1,0:T(8,128)(2,1)S(1)}, u32[]{:S(2)}, u32[]{:S(2)}) collective-permute-start(bf16[2,240,128]{2,1,0:T(8,128)(2,1)S(1)} %get-tuple-element.53.refs_4_), channel_id=1, source_target_pairs={{0,2},{1,3},{2,0},{3,1},{4,6},{5,7},{6,4},{7,5},{8,10},{9,11},{10,... | collective-permute-start | bytes 368648 | tf_op jit(solution)/shard_map/ppermute | solution.py:436
  51.0 0.1 collective-permute-start.13
  51.1 0.9 %collective-permute-done.14.refs_5_ = bf16[2,240,128]{2,1,0:T(8,128)(2,1)S(1)} collective-permute-done((bf16[2,240,128]{2,1,0:T(8,128)(2,1)S(1)}, bf16[2,240,128]{2,1,0:T(8,128)(2,1)S(1)}, u32[]{:S(2)}, u32[]{:S(2)}) %collective-permute-start.14) | collective-permute-done | bytes 122912 | tf_op jit(solution)/shard_map/ppermute | solution.py:436
  52.0 0.4 collective-permute-done.13.refs_3_
  52.4 2.7 %chi.2 = (f32[384,3072]{1,0:T(8,128)}, f32[384,3072]{1,0:T(8,128)}, bf16[768,160]{1,0:T(8,128)(2,1)S(1)}) custom-call(bf16[240,128]{1,0:T(8,128)(2,1)S(1)} %get-tuple-element.56.refs_0_, bf16[240,128]{1,0:T(8,128)(2,1)S(1)} %get-tuple-element.55.refs_1_, bf16[2,240,128]{2,1,0:T(8,128)(2,1)S(1)} %get-tuple-element.54.refs_2_, ...), custom_call_target="tpu_custom_call" | custom-call | flops 1 | bytes 1 | tf_op jit(solution)/shard_map/chi/pallas_call | solution.py:404
  55.1 1.9 %collective-permute-done.10.refs_3_ = bf16[4,240,128]{2,1,0:T(8,128)(2,1)S(1)} collective-permute-done((bf16[4,240,128]{2,1,0:T(8,128)(2,1)S(1)}, bf16[4,240,128]{2,1,0:T(8,128)(2,1)S(1)}, u32[]{:S(2)}, u32[]{:S(2)}) %collective-permute-start.10) | collective-permute-done | bytes 245792 | tf_op jit(solution)/shard_map/ppermute | solution.py:436
  56.9 0.1 collective-permute-start.15
  57.1 1.4 %collective-permute-done.15.refs_4_ = bf16[4,240,128]{2,1,0:T(8,128)(2,1)S(1)} collective-permute-done((bf16[4,240,128]{2,1,0:T(8,128)(2,1)S(1)}, bf16[4,240,128]{2,1,0:T(8,128)(2,1)S(1)}, u32[]{:S(2)}, u32[]{:S(2)}) %collective-permute-start.15) | collective-permute-done | bytes 245792 | tf_op jit(solution)/shard_map/ppermute | solution.py:436
  58.5 2.6 %chi.3 = (f32[384,3072]{1,0:T(8,128)}, f32[384,3072]{1,0:T(8,128)}) custom-call(bf16[768,160]{1,0:T(8,128)(2,1)S(1)} %get-tuple-element.34.refs_0_, f32[384,3072]{1,0:T(8,128)} %get-tuple-element.35.refs_1_, f32[384,3072]{1,0:T(8,128)} %get-tuple-element.36.refs_2_, ...), custom_call_target="tpu_custom_call", output_to_operand_aliasing={{0}: (1, {}), {1}: (2, {})} | custom-call | flops 1 | bytes 1 | tf_op jit(solution)/shard_map/chi/pallas_call | solution.py:404
  (25 shorter events, 0.2 us)
Async XLA Ops:
  1.5 1.0 %copy-start = (bf16[16,4,4096]{2,1,0:T(4,128)(2,1)S(1)}, bf16[16,4,4096]{2,1,0:T(4,128)(2,1)}, u32[]{:S(2)}) copy-start(bf16[16,4,4096]{2,1,0:T(4,128)(2,1)} %psi_v.1) | copy-start | bytes 1572868
  2.5 5.9 %copy-start.1 = (bf16[40,256]{1,0:T(8,128)(2,1)S(1)}, bf16[40,256]{1,0:T(8,128)(2,1)}, u32[]{:S(2)}) copy-start(bf16[40,256]{1,0:T(8,128)(2,1)} %constant.53.clone.pick) | copy-start | bytes 61444
  11.7 3.9 %collective-permute-start = (f32[4,248,128]{2,1,0:T(8,128)S(1)}, f32[4,248,128]{2,1,0:T(8,128)S(1)}, u32[]{:S(2)}, u32[]{:S(2)}) collective-permute-start(f32[4,248,128]{2,1,0:T(8,128)S(1)} %points.3.refs_0_), channel_id=1, source_target_pairs={{0,2},{1,3},{2,0},{3,1},{4,6},{5,7},{6,4},{7,5},{8,10},{9,11},{10,... | collective-permute-start | bytes 1523720 | tf_op jit(solution)/shard_map/ppermute | solution.py:436
  15.6 15.8 %copy-start.2 = (s32[40]{0:T(128)S(1)}, s32[40]{0:T(128)}, u32[]{:S(2)}) copy-start(s32[40]{0:T(128)} %param.13) | copy-start | bytes 484
  15.6 15.8 %copy-start.3 = (f32[384]{0:T(512)S(1)}, f32[384]{0:T(512)}, u32[]{:S(2)}) copy-start(f32[384]{0:T(512)} %param.11) | copy-start | bytes 4612
  15.6 16.0 %copy-start.4 = (s32[40]{0:T(128)S(1)}, s32[40]{0:T(128)}, u32[]{:S(2)}) copy-start(s32[40]{0:T(128)} %param.12) | copy-start | bytes 484
  15.6 16.0 %copy-start.5 = (f32[16]{0:T(128)S(1)}, f32[16]{0:T(128)}, u32[]{:S(2)}) copy-start(f32[16]{0:T(128)} %param.10) | copy-start | bytes 196
  15.9 9.4 %collective-permute-start.1 = (f16[4,248,128]{2,1,0:T(8,128)(2,1)S(1)}, f16[4,248,128]{2,1,0:T(8,128)(2,1)S(1)}, u32[]{:S(2)}, u32[]{:S(2)}) collective-permute-start(f16[4,248,128]{2,1,0:T(8,128)(2,1)S(1)} %select_convert_fusion), channel_id=1, source_target_pairs={{0,4},{1,5},{2,6},{3,7},{4,0},{5,1},{6,2},{7,3},{8,12},{9,13},{10,... | collective-permute-start | bytes 761864 | tf_op jit(solution)/shard_map/ppermute | solution.py:436
  25.2 1.9 %collective-permute-start.2 = (f32[4,248,128]{2,1,0:T(8,128)S(1)}, f32[4,248,128]{2,1,0:T(8,128)S(1)}, u32[]{:S(2)}, u32[]{:S(2)}) collective-permute-start(f32[4,248,128]{2,1,0:T(8,128)S(1)} %get-tuple-element.28), channel_id=1, source_target_pairs={{0,2},{1,3},{2,0},{3,1},{4,6},{5,7},{6,4},{7,5},{8,10},{9,11},{10,... | collective-permute-start | bytes 1523720 | tf_op jit(solution)/shard_map/ppermute | solution.py:436
  27.5 6.7 %collective-permute-start.3 = (f16[248,128]{1,0:T(8,128)(2,1)S(1)}, f16[248,128]{1,0:T(8,128)(2,1)S(1)}, u32[]{:S(2)}, u32[]{:S(2)}) collective-permute-start(f16[248,128]{1,0:T(8,128)(2,1)S(1)} %get-tuple-element.46), channel_id=1, source_target_pairs={{0,24},{1,25},{2,26},{3,27},{4,28},{5,29},{6,30},{7,31},{8,16},{9,... | collective-permute-start | bytes 190472 | tf_op jit(solution)/shard_map/ppermute | solution.py:436
  31.8 4.8 %collective-permute-start.5 = (f16[248,128]{1,0:T(8,128)(2,1)S(1)}, f16[248,128]{1,0:T(8,128)(2,1)S(1)}, u32[]{:S(2)}, u32[]{:S(2)}) collective-permute-start(f16[248,128]{1,0:T(8,128)(2,1)S(1)} %get-tuple-element.47), channel_id=1, source_target_pairs={{0,8},{1,9},{2,10},{3,11},{4,12},{5,13},{6,14},{7,15},{8,0},{9,1},... | collective-permute-start | bytes 190472 | tf_op jit(solution)/shard_map/ppermute | solution.py:436
  31.8 5.9 %collective-permute-start.4 = (f16[248,128]{1,0:T(8,128)(2,1)S(1)}, f16[248,128]{1,0:T(8,128)(2,1)S(1)}, u32[]{:S(2)}, u32[]{:S(2)}) collective-permute-start(f16[248,128]{1,0:T(8,128)(2,1)S(1)} %get-tuple-element.48), channel_id=1, source_target_pairs={{0,16},{1,17},{2,18},{3,19},{4,20},{5,21},{6,22},{7,23},{8,24},{9,... | collective-permute-start | bytes 190472 | tf_op jit(solution)/shard_map/ppermute | solution.py:436
  37.8 9.7 %collective-permute-start.9 = (bf16[240,128]{1,0:T(8,128)(2,1)S(1)}, bf16[240,128]{1,0:T(8,128)(2,1)S(1)}, u32[]{:S(2)}, u32[]{:S(2)}) collective-permute-start(bf16[240,128]{1,0:T(8,128)(2,1)S(1)} %fusion.9), channel_id=1, source_target_pairs={{0,24},{1,26},{2,25},{3,27},{4,28},{5,30},{6,29},{7,31},{8,16},{9,... | collective-permute-start | bytes 184328 | tf_op jit(solution)/shard_map/ppermute | solution.py:436
  40.3 8.0 %collective-permute-start.8 = (bf16[240,128]{1,0:T(8,128)(2,1)S(1)}, bf16[240,128]{1,0:T(8,128)(2,1)S(1)}, u32[]{:S(2)}, u32[]{:S(2)}) collective-permute-start(bf16[240,128]{1,0:T(8,128)(2,1)S(1)} %fusion.9), channel_id=1, source_target_pairs={{0,16},{1,18},{2,17},{3,19},{4,20},{5,22},{6,21},{7,23},{8,24},{9,... | collective-permute-start | bytes 184328 | tf_op jit(solution)/shard_map/ppermute | solution.py:436
  40.6 7.6 %collective-permute-start.7 = (bf16[240,128]{1,0:T(8,128)(2,1)S(1)}, bf16[240,128]{1,0:T(8,128)(2,1)S(1)}, u32[]{:S(2)}, u32[]{:S(2)}) collective-permute-start(bf16[240,128]{1,0:T(8,128)(2,1)S(1)} %fusion.9), channel_id=1, source_target_pairs={{0,8},{1,10},{2,9},{3,11},{4,12},{5,14},{6,13},{7,15},{8,0},{9,2},... | collective-permute-start | bytes 184328 | tf_op jit(solution)/shard_map/ppermute | solution.py:436
  42.3 6.0 %collective-permute-start.6 = (bf16[240,128]{1,0:T(8,128)(2,1)S(1)}, bf16[240,128]{1,0:T(8,128)(2,1)S(1)}, u32[]{:S(2)}, u32[]{:S(2)}) collective-permute-start(bf16[240,128]{1,0:T(8,128)(2,1)S(1)} %fusion.9), channel_id=1, source_target_pairs={{0,0},{1,2},{2,1},{3,3},{4,4},{5,6},{6,5},{7,7},{8,8},{9,10},{10,9... | collective-permute-start | bytes 184328 | tf_op jit(solution)/shard_map/ppermute | solution.py:436
  43.0 8.1 %collective-permute-start.12 = (bf16[240,128]{1,0:T(8,128)(2,1)S(1)}, bf16[240,128]{1,0:T(8,128)(2,1)S(1)}, u32[]{:S(2)}, u32[]{:S(2)}) collective-permute-start(bf16[240,128]{1,0:T(8,128)(2,1)S(1)} %fusion.9), channel_id=1, source_target_pairs={{0,1},{1,0},{2,17},{3,16},{4,5},{5,4},{6,21},{7,20},{8,9},{9,8},{1... | collective-permute-start | bytes 184328 | tf_op jit(solution)/shard_map/ppermute | solution.py:436
  47.6 3.5 %collective-permute-start.11 = (bf16[240,128]{1,0:T(8,128)(2,1)S(1)}, bf16[240,128]{1,0:T(8,128)(2,1)S(1)}, u32[]{:S(2)}, u32[]{:S(2)}) collective-permute-start(bf16[240,128]{1,0:T(8,128)(2,1)S(1)} %fusion.9), channel_id=1, source_target_pairs={{0,0},{1,1},{2,16},{3,17},{4,4},{5,5},{6,20},{7,21},{8,8},{9,9},{1... | collective-permute-start | bytes 184328 | tf_op jit(solution)/shard_map/ppermute | solution.py:436
  48.3 8.6 %collective-permute-start.10 = (bf16[4,240,128]{2,1,0:T(8,128)(2,1)S(1)}, bf16[4,240,128]{2,1,0:T(8,128)(2,1)S(1)}, u32[]{:S(2)}, u32[]{:S(2)}) collective-permute-start(bf16[4,240,128]{2,1,0:T(8,128)(2,1)S(1)} %pad_maximum_fusion), channel_id=1, source_target_pairs={{0,4},{1,5},{2,6},{3,7},{4,0},{5,1},{6,2},{7,3},{8,12},{9,13},{10,... | collective-permute-start | bytes 737288 | tf_op jit(solution)/shard_map/ppermute | solution.py:436
  49.9 2.1 %collective-permute-start.14 = (bf16[2,240,128]{2,1,0:T(8,128)(2,1)S(1)}, bf16[2,240,128]{2,1,0:T(8,128)(2,1)S(1)}, u32[]{:S(2)}, u32[]{:S(2)}) collective-permute-start(bf16[2,240,128]{2,1,0:T(8,128)(2,1)S(1)} %get-tuple-element.53.refs_4_), channel_id=1, source_target_pairs={{0,2},{1,3},{2,0},{3,1},{4,6},{5,7},{6,4},{7,5},{8,10},{9,11},{10,... | collective-permute-start | bytes 368648 | tf_op jit(solution)/shard_map/ppermute | solution.py:436
  51.0 1.3 %collective-permute-start.13 = (bf16[2,240,128]{2,1,0:T(8,128)(2,1)S(1)}, bf16[2,240,128]{2,1,0:T(8,128)(2,1)S(1)}, u32[]{:S(2)}, u32[]{:S(2)}) collective-permute-start(bf16[2,240,128]{2,1,0:T(8,128)(2,1)S(1)} %get-tuple-element.54.refs_2_), channel_id=1, source_target_pairs={{0,2},{1,3},{2,0},{3,1},{4,6},{5,7},{6,4},{7,5},{8,10},{9,11},{10,... | collective-permute-start | bytes 368648 | tf_op jit(solution)/shard_map/ppermute | solution.py:436
  56.9 1.5 %collective-permute-start.15 = (bf16[4,240,128]{2,1,0:T(8,128)(2,1)S(1)}, bf16[4,240,128]{2,1,0:T(8,128)(2,1)S(1)}, u32[]{:S(2)}, u32[]{:S(2)}) collective-permute-start(bf16[4,240,128]{2,1,0:T(8,128)(2,1)S(1)} %collective-permute-done.10.refs_3_), channel_id=1, source_target_pairs={{0,2},{1,3},{2,0},{3,1},{4,6},{5,7},{6,4},{7,5},{8,10},{9,11},{10,... | collective-permute-start | bytes 737288 | tf_op jit(solution)/shard_map/ppermute | solution.py:436

commit v5 on v4

--- a/solution.py
+++ b/solution.py
@@ -240,21 +240,27 @@
     for block in range(last + 1):
         fetch(block).start()
     peak[...] = jnp.zeros_like(peak)
-    fetch(0).wait()
-    gather(0, tiles_0)
-    for block in range(1, last + 1):
-        fetch(block).wait()
-    for group in range(len(outs)):
+    tiles = (tiles_0, tiles_1)
+    if chunked:
+        for block in range(last + 2):
+            if block <= last:
+                fetch(block).wait()
+                gather(block, tiles[block % 2])
+            if block > 0:
+                combine((block - 1) // blocks, (block - 1) % blocks, tiles[(block - 1) % 2])
+    else:
+        for block in range(last + 1):
+            fetch(block).wait()
+        gather(0, tiles_0)
 
         def two_blocks(step, _):
-            block = group * blocks + 2 * step
-            gather(block + 1, tiles_1)
-            combine(group, 2 * step, tiles_0)
-            gather(jnp.minimum(block + 2, last), tiles_0)
-            combine(group, 2 * step + 1, tiles_1)
+            gather(2 * step + 1, tiles_1)
+            combine(0, 2 * step, tiles_0)
+            gather(jnp.minimum(2 * step + 2, last), tiles_0)
+            combine(0, 2 * step + 1, tiles_1)
             return 0
 
-        lax.fori_loop(0, blocks // 2, two_blocks, 0, unroll=2)
+        lax.fori_loop(0, blocks // 2, two_blocks, 0)
     if chunked:
         used = width // LANES * 2 * pair_count
         top = jnp.broadcast_to(jnp.max(peak[...], axis=0, keepdims=True), (rows - used, LANES))

time: 61.6 us -> 61 us (level)
  Pallas kernels: 23.5 us -> 22.6 us
    pallas_call x3, Pallas kernels: 12.3 us -> 11.4 us  [points(): pl.pallas_call(functools.partial(points_kernel, length, pair_count, width...]
  transfers between devices with their start and end apart: 16 -> 16, of which waited for: 9 -> 9; matrix products, arithmetic and copies ran while one was open for 1% -> 1% of each run, Pallas kernels for 19% -> 18%
where the time goes in v5:
time: 61 us; the launch traced here: 60.7 us
  Pallas kernels  22.6 us (37%)
  starting transfers between devices  20.9 us (34%)
  waiting for transfers between devices  13.1 us (21%)
  local copies, waits for them, and re-layouts  2.01 us (3%)
  between operations  1.06 us (2%)
  other arithmetic  1.02 us (2%)
    ppermute x16, starting transfers between devices, permute(): return lax.ppermute(values, ('fft', 'grp'), perm)  20.9 us
    ppermute x16, waiting for transfers between devices, permute(): return lax.ppermute(values, ('fft', 'grp'), perm)  13.1 us
    pallas_call x3, Pallas kernels, points(): pl.pallas_call(functools.partial(points_kernel, length, pair_count, width...  11.4 us
    pallas_call x1, Pallas kernels, transform(): pl.pallas_call(functools.partial(transform_kernel, length, pair_count), o...  5.89 us
    pallas_call x2, Pallas kernels, chi_direct(): pl.pallas_call(functools.partial(chi_direct_kernel, pair_count, width, sh...  5.33 us
  transfers between devices with their start and end apart: 16, of which 9 were waited for; matrix products, arithmetic and copies ran while one was open for 1% of the time, Pallas kernels for 18%

profile of v5, /device:TPU:0, one launch (start us, length us, event | category | flops | bytes accessed | tf_op | source)
XLA Modules:
  0.0 60.7 jit_solution(1333804402927466270)
XLA Ops:
  0.6 0.8 %concatenate.3 = s32[9216]{0:T(1024)S(1)} concatenate(s32[6144]{0:T(1024)} %param.14, s32[40]{0:T(128)} %param.12, s32[40]{0:T(128)} %param.13, s32[2992]{0:T(1024)S(1)} %broadcast_in_dim.71), dimensions={0} | concatenate | bytes 73728 | tf_op jit(solution)/shard_map/concatenate | solution.py:300
  1.5 1.0 %copy-done = bf16[16,4,4096]{2,1,0:T(4,128)(2,1)S(1)} copy-done((bf16[16,4,4096]{2,1,0:T(4,128)(2,1)S(1)}, bf16[16,4,4096]{2,1,0:T(4,128)(2,1)}, u32[]{:S(2)}) %copy-start) | copy-done | bytes 524312
  2.5 5.9 %transform.1 = (f32[8448,128]{1,0:T(8,128)S(1)}, bf16[128,512]{1,0:T(8,128)(2,1)S(1)}, s32[16,1,384]{2,1,0:T(1,128)S(1)}, s32[16,1,384]{2,1,0:T(1,128)S(1)}) custom-call(s32[24,1,384]{2,1,0:T(1,128)S(1)} %bitcast.48, bf16[16,4,4096]{2,1,0:T(4,128)(2,1)S(1)} %copy-done, bf16[384,4,4096]{2,1,0:T(4,128)(2,1)} %psi_c.1), custom_call_target="tpu_custom_call" | custom-call | tf_op jit(solution)/shard_map/transform/pallas_call | solution.py:151
  8.4 3.0 %points.3.refs_0_ = f32[4,248,128]{2,1,0:T(8,128)S(1)} custom-call(s32[16,1,384]{2,1,0:T(1,128)S(1)} %get-tuple-element.20.spot, s32[16,1,384]{2,1,0:T(1,128)S(1)} %get-tuple-element.21.phase, f32[2112,4,128]{2,1,0:T(4,128)S(1)} %bitcast.45, bf16[128,512]{1,0:T(8,128)(2,1)S(1)} %get-tuple-element.23.coef, bf16[40,256]{1,0:T(8,128)(2,1)S(1)} %copy-done.1), custom_call_target="tpu_custom_call" | custom-call | flops 400000000 | bytes 1048576 | tf_op jit(solution)/shard_map/points/pallas_call | solution.py:278
  11.4 0.5 collective-permute-start
  12.0 3.0 %points.4 = f32[4,248,128]{2,1,0:T(8,128)S(1)} custom-call(s32[16,1,384]{2,1,0:T(1,128)S(1)} %get-tuple-element.20.spot, s32[16,1,384]{2,1,0:T(1,128)S(1)} %get-tuple-element.21.phase, f32[2112,4,128]{2,1,0:T(4,128)S(1)} %bitcast.46, bf16[128,512]{1,0:T(8,128)(2,1)S(1)} %get-tuple-element.23.coef, bf16[40,256]{1,0:T(8,128)(2,1)S(1)} %copy-done.1, ...), custom_call_target="tpu_custom_call" | custom-call | flops 400000000 | bytes 1048576 | tf_op jit(solution)/shard_map/points/pallas_call | solution.py:278
  15.0 0.0 copy-start.2
  15.0 0.0 copy-start.3
  15.0 0.0 copy-start.4
  15.0 0.0 copy-start.5
  15.1 0.0 collective-permute-done
  15.1 0.1 add.50.refs_0_
  15.2 0.1 select_convert_fusion
  15.3 2.6 %collective-permute-start.1 = (f16[4,248,128]{2,1,0:T(8,128)(2,1)S(1)}, f16[4,248,128]{2,1,0:T(8,128)(2,1)S(1)}, u32[]{:S(2)}, u32[]{:S(2)}) collective-permute-start(f16[4,248,128]{2,1,0:T(8,128)(2,1)S(1)} %select_convert_fusion), channel_id=1, source_target_pairs={{0,4},{1,5},{2,6},{3,7},{4,0},{5,1},{6,2},{7,3},{8,12},{9,13},{10,... | collective-permute-start | bytes 761864 | tf_op jit(solution)/shard_map/ppermute | solution.py:442
  17.9 5.4 %points.5 = (f32[4,248,128]{2,1,0:T(8,128)S(1)}, f32[4,248,128]{2,1,0:T(8,128)S(1)}) custom-call(s32[16,1,384]{2,1,0:T(1,128)S(1)} %get-tuple-element.20.spot, s32[16,1,384]{2,1,0:T(1,128)S(1)} %get-tuple-element.21.phase, f32[2112,4,128]{2,1,0:T(4,128)S(1)} %bitcast.47, bf16[128,512]{1,0:T(8,128)(2,1)S(1)} %get-tuple-element.23.coef, ...), custom_call_target="tpu_custom_call" | custom-call | flops 400000000 | bytes 1048576 | tf_op jit(solution)/shard_map/points/pallas_call | solution.py:278
  23.3 1.4 %collective-permute-done.1 = f16[4,248,128]{2,1,0:T(8,128)(2,1)S(1)} collective-permute-done((f16[4,248,128]{2,1,0:T(8,128)(2,1)S(1)}, f16[4,248,128]{2,1,0:T(8,128)(2,1)S(1)}, u32[]{:S(2)}, u32[]{:S(2)}) %collective-permute-start.1) | collective-permute-done | bytes 253984 | tf_op jit(solution)/shard_map/ppermute | solution.py:442
  24.7 1.9 %collective-permute-done.2 = f32[4,248,128]{2,1,0:T(8,128)S(1)} collective-permute-done((f32[4,248,128]{2,1,0:T(8,128)S(1)}, f32[4,248,128]{2,1,0:T(8,128)S(1)}, u32[]{:S(2)}, u32[]{:S(2)}) %collective-permute-start.2) | collective-permute-done | bytes 507936 | tf_op jit(solution)/shard_map/ppermute | solution.py:442
  26.5 0.2 multiply_add_fusion
  26.8 0.1 fusion.5
  26.9 3.9 %collective-permute-start.3 = (f16[248,128]{1,0:T(8,128)(2,1)S(1)}, f16[248,128]{1,0:T(8,128)(2,1)S(1)}, u32[]{:S(2)}, u32[]{:S(2)}) collective-permute-start(f16[248,128]{1,0:T(8,128)(2,1)S(1)} %get-tuple-element.46), channel_id=1, source_target_pairs={{0,24},{1,25},{2,26},{3,27},{4,28},{5,29},{6,30},{7,31},{8,16},{9,... | collective-permute-start | bytes 190472 | tf_op jit(solution)/shard_map/ppermute | solution.py:442
  30.8 0.2 select_reduce_fusion
  31.0 0.1 select_reduce_fusion.1
  31.1 0.1 mul.119
  31.2 0.0 collective-permute-start.5
  31.2 0.6 collective-permute-start.4
  31.8 1.8 %collective-permute-done.3 = f16[248,128]{1,0:T(8,128)(2,1)S(1)} collective-permute-done((f16[248,128]{1,0:T(8,128)(2,1)S(1)}, f16[248,128]{1,0:T(8,128)(2,1)S(1)}, u32[]{:S(2)}, u32[]{:S(2)}) %collective-permute-start.3) | collective-permute-done | bytes 63520 | tf_op jit(solution)/shard_map/ppermute | solution.py:442
  33.7 2.4 %collective-permute-done.5 = f16[248,128]{1,0:T(8,128)(2,1)S(1)} collective-permute-done((f16[248,128]{1,0:T(8,128)(2,1)S(1)}, f16[248,128]{1,0:T(8,128)(2,1)S(1)}, u32[]{:S(2)}, u32[]{:S(2)}) %collective-permute-start.5) | collective-permute-done | bytes 63520 | tf_op jit(solution)/shard_map/ppermute | solution.py:442
  36.0 1.1 %collective-permute-done.4 = f16[248,128]{1,0:T(8,128)(2,1)S(1)} collective-permute-done((f16[248,128]{1,0:T(8,128)(2,1)S(1)}, f16[248,128]{1,0:T(8,128)(2,1)S(1)}, u32[]{:S(2)}, u32[]{:S(2)}) %collective-permute-start.4) | collective-permute-done | bytes 63520 | tf_op jit(solution)/shard_map/ppermute | solution.py:442
  37.1 0.1 fusion.9
  37.3 2.4 %collective-permute-start.9 = (bf16[240,128]{1,0:T(8,128)(2,1)S(1)}, bf16[240,128]{1,0:T(8,128)(2,1)S(1)}, u32[]{:S(2)}, u32[]{:S(2)}) collective-permute-start(bf16[240,128]{1,0:T(8,128)(2,1)S(1)} %fusion.9), channel_id=1, source_target_pairs={{0,24},{1,26},{2,25},{3,27},{4,28},{5,30},{6,29},{7,31},{8,16},{9,... | collective-permute-start | bytes 184328 | tf_op jit(solution)/shard_map/ppermute | solution.py:442
  39.7 0.4 collective-permute-start.8
  40.1 1.6 %collective-permute-start.7 = (bf16[240,128]{1,0:T(8,128)(2,1)S(1)}, bf16[240,128]{1,0:T(8,128)(2,1)S(1)}, u32[]{:S(2)}, u32[]{:S(2)}) collective-permute-start(bf16[240,128]{1,0:T(8,128)(2,1)S(1)} %fusion.9), channel_id=1, source_target_pairs={{0,8},{1,10},{2,9},{3,11},{4,12},{5,14},{6,13},{7,15},{8,0},{9,2},... | collective-permute-start | bytes 184328 | tf_op jit(solution)/shard_map/ppermute | solution.py:442
  41.7 0.7 %collective-permute-start.6 = (bf16[240,128]{1,0:T(8,128)(2,1)S(1)}, bf16[240,128]{1,0:T(8,128)(2,1)S(1)}, u32[]{:S(2)}, u32[]{:S(2)}) collective-permute-start(bf16[240,128]{1,0:T(8,128)(2,1)S(1)} %fusion.9), channel_id=1, source_target_pairs={{0,0},{1,2},{2,1},{3,3},{4,4},{5,6},{6,5},{7,7},{8,8},{9,10},{10,9... | collective-permute-start | bytes 184328 | tf_op jit(solution)/shard_map/ppermute | solution.py:442
  42.4 4.6 %collective-permute-start.12 = (bf16[240,128]{1,0:T(8,128)(2,1)S(1)}, bf16[240,128]{1,0:T(8,128)(2,1)S(1)}, u32[]{:S(2)}, u32[]{:S(2)}) collective-permute-start(bf16[240,128]{1,0:T(8,128)(2,1)S(1)} %fusion.9), channel_id=1, source_target_pairs={{0,1},{1,0},{2,17},{3,16},{4,5},{5,4},{6,21},{7,20},{8,9},{9,8},{1... | collective-permute-start | bytes 184328 | tf_op jit(solution)/shard_map/ppermute | solution.py:442
  47.0 0.0 collective-permute-done.9
  47.0 0.7 %collective-permute-start.11 = (bf16[240,128]{1,0:T(8,128)(2,1)S(1)}, bf16[240,128]{1,0:T(8,128)(2,1)S(1)}, u32[]{:S(2)}, u32[]{:S(2)}) collective-permute-start(bf16[240,128]{1,0:T(8,128)(2,1)S(1)} %fusion.9), channel_id=1, source_target_pairs={{0,0},{1,1},{2,16},{3,17},{4,4},{5,5},{6,20},{7,21},{8,8},{9,9},{1... | collective-permute-start | bytes 184328 | tf_op jit(solution)/shard_map/ppermute | solution.py:442
  47.7 0.0 collective-permute-done.8
  47.8 1.6 %collective-permute-start.10 = (bf16[4,240,128]{2,1,0:T(8,128)(2,1)S(1)}, bf16[4,240,128]{2,1,0:T(8,128)(2,1)S(1)}, u32[]{:S(2)}, u32[]{:S(2)}) collective-permute-start(bf16[4,240,128]{2,1,0:T(8,128)(2,1)S(1)} %pad_maximum_fusion), channel_id=1, source_target_pairs={{0,4},{1,5},{2,6},{3,7},{4,0},{5,1},{6,2},{7,3},{8,12},{9,13},{10,... | collective-permute-start | bytes 737288 | tf_op jit(solution)/shard_map/ppermute | solution.py:442
  49.4 1.1 %collective-permute-start.14 = (bf16[2,240,128]{2,1,0:T(8,128)(2,1)S(1)}, bf16[2,240,128]{2,1,0:T(8,128)(2,1)S(1)}, u32[]{:S(2)}, u32[]{:S(2)}) collective-permute-start(bf16[2,240,128]{2,1,0:T(8,128)(2,1)S(1)} %get-tuple-element.53.refs_4_), channel_id=1, source_target_pairs={{0,2},{1,3},{2,0},{3,1},{4,6},{5,7},{6,4},{7,5},{8,10},{9,11},{10,... | collective-permute-start | bytes 368648 | tf_op jit(solution)/shard_map/ppermute | solution.py:442
  50.5 0.1 collective-permute-start.13
  50.5 0.0 collective-permute-done.12
  50.6 0.9 %collective-permute-done.14.refs_5_ = bf16[2,240,128]{2,1,0:T(8,128)(2,1)S(1)} collective-permute-done((bf16[2,240,128]{2,1,0:T(8,128)(2,1)S(1)}, bf16[2,240,128]{2,1,0:T(8,128)(2,1)S(1)}, u32[]{:S(2)}, u32[]{:S(2)}) %collective-permute-start.14) | collective-permute-done | bytes 122912 | tf_op jit(solution)/shard_map/ppermute | solution.py:442
  51.4 0.4 collective-permute-done.13.refs_3_
  51.8 2.7 %chi.2 = (f32[384,3072]{1,0:T(8,128)}, f32[384,3072]{1,0:T(8,128)}, bf16[768,160]{1,0:T(8,128)(2,1)S(1)}) custom-call(bf16[240,128]{1,0:T(8,128)(2,1)S(1)} %get-tuple-element.56.refs_0_, bf16[240,128]{1,0:T(8,128)(2,1)S(1)} %get-tuple-element.55.refs_1_, bf16[2,240,128]{2,1,0:T(8,128)(2,1)S(1)} %get-tuple-element.54.refs_2_, ...), custom_call_target="tpu_custom_call" | custom-call | flops 1 | bytes 1 | tf_op jit(solution)/shard_map/chi/pallas_call | solution.py:410
  54.5 1.9 %collective-permute-done.10.refs_3_ = bf16[4,240,128]{2,1,0:T(8,128)(2,1)S(1)} collective-permute-done((bf16[4,240,128]{2,1,0:T(8,128)(2,1)S(1)}, bf16[4,240,128]{2,1,0:T(8,128)(2,1)S(1)}, u32[]{:S(2)}, u32[]{:S(2)}) %collective-permute-start.10) | collective-permute-done | bytes 245792 | tf_op jit(solution)/shard_map/ppermute | solution.py:442
  56.4 0.1 collective-permute-start.15
  56.5 1.4 %collective-permute-done.15.refs_4_ = bf16[4,240,128]{2,1,0:T(8,128)(2,1)S(1)} collective-permute-done((bf16[4,240,128]{2,1,0:T(8,128)(2,1)S(1)}, bf16[4,240,128]{2,1,0:T(8,128)(2,1)S(1)}, u32[]{:S(2)}, u32[]{:S(2)}) %collective-permute-start.15) | collective-permute-done | bytes 245792 | tf_op jit(solution)/shard_map/ppermute | solution.py:442
  57.9 2.6 %chi.3 = (f32[384,3072]{1,0:T(8,128)}, f32[384,3072]{1,0:T(8,128)}) custom-call(bf16[768,160]{1,0:T(8,128)(2,1)S(1)} %get-tuple-element.34.refs_0_, f32[384,3072]{1,0:T(8,128)} %get-tuple-element.35.refs_1_, f32[384,3072]{1,0:T(8,128)} %get-tuple-element.36.refs_2_, ...), custom_call_target="tpu_custom_call", output_to_operand_aliasing={{0}: (1, {}), {1}: (2, {})} | custom-call | flops 1 | bytes 1 | tf_op jit(solution)/shard_map/chi/pallas_call | solution.py:410
  (25 shorter events, 0.2 us)
Async XLA Ops:
  1.5 1.0 %copy-start = (bf16[16,4,4096]{2,1,0:T(4,128)(2,1)S(1)}, bf16[16,4,4096]{2,1,0:T(4,128)(2,1)}, u32[]{:S(2)}) copy-start(bf16[16,4,4096]{2,1,0:T(4,128)(2,1)} %psi_v.1) | copy-start | bytes 1572868
  2.5 5.9 %copy-start.1 = (bf16[40,256]{1,0:T(8,128)(2,1)S(1)}, bf16[40,256]{1,0:T(8,128)(2,1)}, u32[]{:S(2)}) copy-start(bf16[40,256]{1,0:T(8,128)(2,1)} %constant.53.clone.pick) | copy-start | bytes 61444
  11.4 3.6 %collective-permute-start = (f32[4,248,128]{2,1,0:T(8,128)S(1)}, f32[4,248,128]{2,1,0:T(8,128)S(1)}, u32[]{:S(2)}, u32[]{:S(2)}) collective-permute-start(f32[4,248,128]{2,1,0:T(8,128)S(1)} %points.3.refs_0_), channel_id=1, source_target_pairs={{0,2},{1,3},{2,0},{3,1},{4,6},{5,7},{6,4},{7,5},{8,10},{9,11},{10,... | collective-permute-start | bytes 1523720 | tf_op jit(solution)/shard_map/ppermute | solution.py:442
  15.0 15.8 %copy-start.2 = (s32[40]{0:T(128)S(1)}, s32[40]{0:T(128)}, u32[]{:S(2)}) copy-start(s32[40]{0:T(128)} %param.13) | copy-start | bytes 484
  15.0 15.8 %copy-start.3 = (f32[384]{0:T(512)S(1)}, f32[384]{0:T(512)}, u32[]{:S(2)}) copy-start(f32[384]{0:T(512)} %param.11) | copy-start | bytes 4612
  15.0 16.0 %copy-start.4 = (s32[40]{0:T(128)S(1)}, s32[40]{0:T(128)}, u32[]{:S(2)}) copy-start(s32[40]{0:T(128)} %param.12) | copy-start | bytes 484
  15.0 16.0 %copy-start.5 = (f32[16]{0:T(128)S(1)}, f32[16]{0:T(128)}, u32[]{:S(2)}) copy-start(f32[16]{0:T(128)} %param.10) | copy-start | bytes 196
  15.3 9.4 %collective-permute-start.1 = (f16[4,248,128]{2,1,0:T(8,128)(2,1)S(1)}, f16[4,248,128]{2,1,0:T(8,128)(2,1)S(1)}, u32[]{:S(2)}, u32[]{:S(2)}) collective-permute-start(f16[4,248,128]{2,1,0:T(8,128)(2,1)S(1)} %select_convert_fusion), channel_id=1, source_target_pairs={{0,4},{1,5},{2,6},{3,7},{4,0},{5,1},{6,2},{7,3},{8,12},{9,13},{10,... | collective-permute-start | bytes 761864 | tf_op jit(solution)/shard_map/ppermute | solution.py:442
  24.7 1.9 %collective-permute-start.2 = (f32[4,248,128]{2,1,0:T(8,128)S(1)}, f32[4,248,128]{2,1,0:T(8,128)S(1)}, u32[]{:S(2)}, u32[]{:S(2)}) collective-permute-start(f32[4,248,128]{2,1,0:T(8,128)S(1)} %get-tuple-element.28), channel_id=1, source_target_pairs={{0,2},{1,3},{2,0},{3,1},{4,6},{5,7},{6,4},{7,5},{8,10},{9,11},{10,... | collective-permute-start | bytes 1523720 | tf_op jit(solution)/shard_map/ppermute | solution.py:442
  26.9 6.7 %collective-permute-start.3 = (f16[248,128]{1,0:T(8,128)(2,1)S(1)}, f16[248,128]{1,0:T(8,128)(2,1)S(1)}, u32[]{:S(2)}, u32[]{:S(2)}) collective-permute-start(f16[248,128]{1,0:T(8,128)(2,1)S(1)} %get-tuple-element.46), channel_id=1, source_target_pairs={{0,24},{1,25},{2,26},{3,27},{4,28},{5,29},{6,30},{7,31},{8,16},{9,... | collective-permute-start | bytes 190472 | tf_op jit(solution)/shard_map/ppermute | solution.py:442
  31.2 4.8 %collective-permute-start.5 = (f16[248,128]{1,0:T(8,128)(2,1)S(1)}, f16[248,128]{1,0:T(8,128)(2,1)S(1)}, u32[]{:S(2)}, u32[]{:S(2)}) collective-permute-start(f16[248,128]{1,0:T(8,128)(2,1)S(1)} %get-tuple-element.47), channel_id=1, source_target_pairs={{0,8},{1,9},{2,10},{3,11},{4,12},{5,13},{6,14},{7,15},{8,0},{9,1},... | collective-permute-start | bytes 190472 | tf_op jit(solution)/shard_map/ppermute | solution.py:442
  31.2 5.9 %collective-permute-start.4 = (f16[248,128]{1,0:T(8,128)(2,1)S(1)}, f16[248,128]{1,0:T(8,128)(2,1)S(1)}, u32[]{:S(2)}, u32[]{:S(2)}) collective-permute-start(f16[248,128]{1,0:T(8,128)(2,1)S(1)} %get-tuple-element.48), channel_id=1, source_target_pairs={{0,16},{1,17},{2,18},{3,19},{4,20},{5,21},{6,22},{7,23},{8,24},{9,... | collective-permute-start | bytes 190472 | tf_op jit(solution)/shard_map/ppermute | solution.py:442
  37.3 9.8 %collective-permute-start.9 = (bf16[240,128]{1,0:T(8,128)(2,1)S(1)}, bf16[240,128]{1,0:T(8,128)(2,1)S(1)}, u32[]{:S(2)}, u32[]{:S(2)}) collective-permute-start(bf16[240,128]{1,0:T(8,128)(2,1)S(1)} %fusion.9), channel_id=1, source_target_pairs={{0,24},{1,26},{2,25},{3,27},{4,28},{5,30},{6,29},{7,31},{8,16},{9,... | collective-permute-start | bytes 184328 | tf_op jit(solution)/shard_map/ppermute | solution.py:442
  39.7 8.0 %collective-permute-start.8 = (bf16[240,128]{1,0:T(8,128)(2,1)S(1)}, bf16[240,128]{1,0:T(8,128)(2,1)S(1)}, u32[]{:S(2)}, u32[]{:S(2)}) collective-permute-start(bf16[240,128]{1,0:T(8,128)(2,1)S(1)} %fusion.9), channel_id=1, source_target_pairs={{0,16},{1,18},{2,17},{3,19},{4,20},{5,22},{6,21},{7,23},{8,24},{9,... | collective-permute-start | bytes 184328 | tf_op jit(solution)/shard_map/ppermute | solution.py:442
  40.1 7.6 %collective-permute-start.7 = (bf16[240,128]{1,0:T(8,128)(2,1)S(1)}, bf16[240,128]{1,0:T(8,128)(2,1)S(1)}, u32[]{:S(2)}, u32[]{:S(2)}) collective-permute-start(bf16[240,128]{1,0:T(8,128)(2,1)S(1)} %fusion.9), channel_id=1, source_target_pairs={{0,8},{1,10},{2,9},{3,11},{4,12},{5,14},{6,13},{7,15},{8,0},{9,2},... | collective-permute-start | bytes 184328 | tf_op jit(solution)/shard_map/ppermute | solution.py:442
  41.7 6.0 %collective-permute-start.6 = (bf16[240,128]{1,0:T(8,128)(2,1)S(1)}, bf16[240,128]{1,0:T(8,128)(2,1)S(1)}, u32[]{:S(2)}, u32[]{:S(2)}) collective-permute-start(bf16[240,128]{1,0:T(8,128)(2,1)S(1)} %fusion.9), channel_id=1, source_target_pairs={{0,0},{1,2},{2,1},{3,3},{4,4},{5,6},{6,5},{7,7},{8,8},{9,10},{10,9... | collective-permute-start | bytes 184328 | tf_op jit(solution)/shard_map/ppermute | solution.py:442
  42.4 8.2 %collective-permute-start.12 = (bf16[240,128]{1,0:T(8,128)(2,1)S(1)}, bf16[240,128]{1,0:T(8,128)(2,1)S(1)}, u32[]{:S(2)}, u32[]{:S(2)}) collective-permute-start(bf16[240,128]{1,0:T(8,128)(2,1)S(1)} %fusion.9), channel_id=1, source_target_pairs={{0,1},{1,0},{2,17},{3,16},{4,5},{5,4},{6,21},{7,20},{8,9},{9,8},{1... | collective-permute-start | bytes 184328 | tf_op jit(solution)/shard_map/ppermute | solution.py:442
  47.0 3.5 %collective-permute-start.11 = (bf16[240,128]{1,0:T(8,128)(2,1)S(1)}, bf16[240,128]{1,0:T(8,128)(2,1)S(1)}, u32[]{:S(2)}, u32[]{:S(2)}) collective-permute-start(bf16[240,128]{1,0:T(8,128)(2,1)S(1)} %fusion.9), channel_id=1, source_target_pairs={{0,0},{1,1},{2,16},{3,17},{4,4},{5,5},{6,20},{7,21},{8,8},{9,9},{1... | collective-permute-start | bytes 184328 | tf_op jit(solution)/shard_map/ppermute | solution.py:442
  47.8 8.6 %collective-permute-start.10 = (bf16[4,240,128]{2,1,0:T(8,128)(2,1)S(1)}, bf16[4,240,128]{2,1,0:T(8,128)(2,1)S(1)}, u32[]{:S(2)}, u32[]{:S(2)}) collective-permute-start(bf16[4,240,128]{2,1,0:T(8,128)(2,1)S(1)} %pad_maximum_fusion), channel_id=1, source_target_pairs={{0,4},{1,5},{2,6},{3,7},{4,0},{5,1},{6,2},{7,3},{8,12},{9,13},{10,... | collective-permute-start | bytes 737288 | tf_op jit(solution)/shard_map/ppermute | solution.py:442
  49.4 2.1 %collective-permute-start.14 = (bf16[2,240,128]{2,1,0:T(8,128)(2,1)S(1)}, bf16[2,240,128]{2,1,0:T(8,128)(2,1)S(1)}, u32[]{:S(2)}, u32[]{:S(2)}) collective-permute-start(bf16[2,240,128]{2,1,0:T(8,128)(2,1)S(1)} %get-tuple-element.53.refs_4_), channel_id=1, source_target_pairs={{0,2},{1,3},{2,0},{3,1},{4,6},{5,7},{6,4},{7,5},{8,10},{9,11},{10,... | collective-permute-start | bytes 368648 | tf_op jit(solution)/shard_map/ppermute | solution.py:442
  50.5 1.3 %collective-permute-start.13 = (bf16[2,240,128]{2,1,0:T(8,128)(2,1)S(1)}, bf16[2,240,128]{2,1,0:T(8,128)(2,1)S(1)}, u32[]{:S(2)}, u32[]{:S(2)}) collective-permute-start(bf16[2,240,128]{2,1,0:T(8,128)(2,1)S(1)} %get-tuple-element.54.refs_2_), channel_id=1, source_target_pairs={{0,2},{1,3},{2,0},{3,1},{4,6},{5,7},{6,4},{7,5},{8,10},{9,11},{10,... | collective-permute-start | bytes 368648 | tf_op jit(solution)/shard_map/ppermute | solution.py:442
  56.4 1.5 %collective-permute-start.15 = (bf16[4,240,128]{2,1,0:T(8,128)(2,1)S(1)}, bf16[4,240,128]{2,1,0:T(8,128)(2,1)S(1)}, u32[]{:S(2)}, u32[]{:S(2)}) collective-permute-start(bf16[4,240,128]{2,1,0:T(8,128)(2,1)S(1)} %collective-permute-done.10.refs_3_), channel_id=1, source_target_pairs={{0,2},{1,3},{2,0},{3,1},{4,6},{5,7},{6,4},{7,5},{8,10},{9,11},{10,... | collective-permute-start | bytes 737288 | tf_op jit(solution)/shard_map/ppermute | solution.py:442
